TPU v7x, 256 devices: a whole 4x4x8 slice. The times are simulated.
256 devices in a mesh: spec: 32 (over x_lo, z, core), bucket: 8 (over y, x_hi).
Axes of the slice: x: 4 (x_hi: 2, x_lo: 2; x = x_hi * 2 + x_lo), y: 4, z: 8, core: 2. Of those that a mesh axis runs over, the one named last changes fastest.
Arguments:
- spectra: bfloat16 [2048, 65536], P('bucket', 'spec'), may hold values from 0 to 20
- theory: bfloat16 [512, 65536], P('bucket', 'spec'), may hold values from 0 to 16
- cand: int32 [2048, 128], P('bucket'), may hold values from 0 to 511
- half: int32 [128], P('spec'), may hold values from 25 to 75
Outputs:
- cand_scores: float32 [2048, 128], P('bucket')
- peptide_score: float32 [512], P(('spec', 'bucket'))
All inputs are finite; a program needn't handle non-finite values.
Results may differ from a plain program's by a relative error of at most 0.0041.
Values may be sent and summed in bfloat16 or wider, within the bound.
No kernel may reach another device: no remote copies, remote signals or barrier semaphores. Data moves between devices by JAX's collectives and lax.ppermute only.
A program may use at most 64 MiB of HBM per device.

v0:
```python
import jax
import jax.numpy as jnp
from jax import lax
from jax.sharding import PartitionSpec as P

HALF = 75
REGION = 512


def extended_2(block, sides, width):
    for axis, dim in sides:
        count = lax.axis_size(axis)
        forward = [(i, i + 1) for i in range(count - 1)]
        backward = [(target, source) for source, target in forward]
        low = lax.ppermute(
            lax.slice_in_dim(block, block.shape[dim] - width, None, axis=dim), axis, forward
        )
        high = lax.ppermute(lax.slice_in_dim(block, 0, width, axis=dim), axis, backward)
        block = jnp.concatenate([low, block, high], axis=dim)
    return block


def broadcast(value, axis, source):
    kept = jnp.where(lax.axis_index(axis) == source, value, 0).astype(value.dtype)
    return lax.psum(kept, axis)


def make_band(widths):
    block_iota = lax.broadcasted_iota(jnp.int32, (3, 128, 128), 0)
    input_iota = lax.broadcasted_iota(jnp.int32, (3, 128, 128), 1)
    output_iota = lax.broadcasted_iota(jnp.int32, (3, 128, 128), 2)
    offset = 128 * (block_iota - 1) + input_iota - output_iota
    return jnp.abs(offset)[None] <= widths[:, None, None, None]


def zscores(score_tile, cand_ids):
    average = jnp.mean(score_tile, axis=1, keepdims=True)
    spread = jnp.mean(jnp.square(score_tile - average), axis=1, keepdims=True)
    picked = jnp.take_along_axis(score_tile, cand_ids, axis=1)
    return (picked - average) * lax.rsqrt(spread + 1e-06)


def against(processed, received):
    return lax.dot_general(
        processed, received, (((1,), (1,)), ((), ())), preferred_element_type=jnp.float32
    )


def on_device(spectra, theory, cand, half):
    row_count, bin_count = spectra.shape
    spec_count = lax.axis_size("spec")
    bucket_count = lax.axis_size("bucket")
    per_bucket = theory.shape[0]
    peptides_all = per_bucket * bucket_count
    position = lax.axis_index("spec")
    extended = extended_2(spectra, (("spec", 1),), HALF)
    bin_widths = jnp.repeat(half, REGION)
    tile_count = bin_count // 128
    padded = jnp.pad(extended, ((0, 0), (128 - HALF, 128 - HALF)))
    tile_view = padded.reshape(row_count, tile_count + 2, 128)
    band_weights = make_band(jnp.repeat(half, REGION // 128)).astype(jnp.bfloat16)
    window_sums = jnp.zeros((row_count, tile_count, 128), jnp.float32)
    for k in range(3):
        window_sums = window_sums + jnp.einsum(
            "rtc,tcd->rtd",
            tile_view[:, k : k + tile_count],
            band_weights[:, k],
            preferred_element_type=jnp.float32,
        )
    window_sums = window_sums.reshape(row_count, bin_count)
    divisor = (2 * bin_widths + 1).astype(jnp.float32)
    processed = (spectra.astype(jnp.float32) - window_sums / divisor).astype(jnp.bfloat16)
    zero_tile = jnp.zeros((row_count, peptides_all), jnp.float32)

    def rooted_step(step_index, running):
        received = broadcast(theory, "bucket", step_index)
        return lax.dynamic_update_slice(
            running, against(processed, received), (jnp.int32(0), step_index * per_bucket)
        )

    score_tile = lax.fori_loop(0, bucket_count, rooted_step, zero_tile)
    summed = lax.psum(score_tile, "spec")
    cand_scores = zscores(summed, cand)
    col_share = cand.shape[1] // spec_count
    local_ids = lax.dynamic_slice_in_dim(cand, position * col_share, col_share, 1)
    local_scores = lax.dynamic_slice_in_dim(cand_scores, position * col_share, col_share, 1)
    partial_value = jax.ops.segment_sum(
        jax.nn.softplus(local_scores).reshape(-1), local_ids.reshape(-1), num_segments=peptides_all
    )
    mean_load = cand.shape[1] * row_count / per_bucket
    peptide_score = (
        lax.psum_scatter(partial_value, ("spec", "bucket"), scatter_dimension=0, tiled=True)
        / mean_load
    )
    return (cand_scores, peptide_score)


def solution(mesh):
    return jax.shard_map(
        on_device,
        mesh=mesh,
        in_specs=(P("bucket", "spec"), P("bucket", "spec"), P("bucket", None), P("spec")),
        out_specs=(P("bucket", None), P(("spec", "bucket"))),
        check_vma=False,
    )
```

profile of v0, /device:TPU:8, one launch (start us, length us, event | category | flops | bytes accessed | tf_op | source)
XLA Modules:
  0.0 1347.0 jit_solution(1085945206522732928)
XLA Ops:
  8.0 1.5 copy.14
  9.6 1.7 collective-permute-start
  11.3 1.3 collective-permute-start.1
  13.0 0.5 broadcast_compare_fusion
  13.6 0.1 reshape.69
  13.8 2.4 collective-permute-done.1
  16.1 1.4 concatenate.3
  17.6 0.3 pad.4
  17.9 0.4 fusion.2
  18.3 0.4 fusion.4
  18.7 1.8 add_add_fusion
  20.6 1.9 copy.20
  22.5 1.6 subtract_convert_fusion
  24.2 743.9 %while.15 = (s32[]{:T(128)}, f32[256,512]{0,1:T(8,128)S(1)}, bf16[64,2048]{1,0:T(8,128)(2,1)S(1)}, bf16[256,2048]{1,0:T(8,128)(2,1)S(1)}, s32[]{:T(128)}, /*index=5*/s32[]{:T(128)}, s32[]{:T(128)}, s32[]{:T(128)}, u32[]{:T(128)}) while((s32[]{:T(128)}, f32[256,512]{0,1:T(8,128)S(1)}, bf16[64,2048]{1,0:T(8,128)(2,1)S(1)}, ...), condition=%wide.region_2.3_spmd, body=%wide.region_0.2_spmd.sunk | while | flops 67371016 | bytes 3473621 | solution.py:81
  24.3 0.7 broadcast_select_fusion.2
  25.0 96.0 %all-reduce.7.cloned.1.call-done = bf16[64,2048]{1,0:T(8,128)(2,1)} async-done(((bf16[64,2048]{1,0:T(8,128)(2,1)}), bf16[64,2048]{1,0:T(8,128)(2,1)}) %all-reduce.7.cloned.1.call-update) | async-done | bytes 262160 | tf_op jit(solution)/shard_map/while/body/eval_jaxpr/psum | solution.py:25
  121.1 1.4 fusion.19
  122.5 0.7 broadcast_select_fusion.2
  123.3 90.1 %all-reduce.7.cloned.1.call-done = bf16[64,2048]{1,0:T(8,128)(2,1)} async-done(((bf16[64,2048]{1,0:T(8,128)(2,1)}), bf16[64,2048]{1,0:T(8,128)(2,1)}) %all-reduce.7.cloned.1.call-update) | async-done | bytes 262160 | tf_op jit(solution)/shard_map/while/body/eval_jaxpr/psum | solution.py:25
  213.4 1.4 fusion.19
  214.9 0.7 broadcast_select_fusion.2
  215.6 90.1 %all-reduce.7.cloned.1.call-done = bf16[64,2048]{1,0:T(8,128)(2,1)} async-done(((bf16[64,2048]{1,0:T(8,128)(2,1)}), bf16[64,2048]{1,0:T(8,128)(2,1)}) %all-reduce.7.cloned.1.call-update) | async-done | bytes 262160 | tf_op jit(solution)/shard_map/while/body/eval_jaxpr/psum | solution.py:25
  305.8 1.4 fusion.19
  307.2 0.7 broadcast_select_fusion.2
  308.0 89.8 %all-reduce.7.cloned.1.call-done = bf16[64,2048]{1,0:T(8,128)(2,1)} async-done(((bf16[64,2048]{1,0:T(8,128)(2,1)}), bf16[64,2048]{1,0:T(8,128)(2,1)}) %all-reduce.7.cloned.1.call-update) | async-done | bytes 262160 | tf_op jit(solution)/shard_map/while/body/eval_jaxpr/psum | solution.py:25
  397.8 1.4 fusion.19
  399.3 0.7 broadcast_select_fusion.2
  400.0 89.8 %all-reduce.7.cloned.1.call-done = bf16[64,2048]{1,0:T(8,128)(2,1)} async-done(((bf16[64,2048]{1,0:T(8,128)(2,1)}), bf16[64,2048]{1,0:T(8,128)(2,1)}) %all-reduce.7.cloned.1.call-update) | async-done | bytes 262160 | tf_op jit(solution)/shard_map/while/body/eval_jaxpr/psum | solution.py:25
  489.9 1.4 fusion.19
  491.3 0.7 broadcast_select_fusion.2
  492.1 89.8 %all-reduce.7.cloned.1.call-done = bf16[64,2048]{1,0:T(8,128)(2,1)} async-done(((bf16[64,2048]{1,0:T(8,128)(2,1)}), bf16[64,2048]{1,0:T(8,128)(2,1)}) %all-reduce.7.cloned.1.call-update) | async-done | bytes 262160 | tf_op jit(solution)/shard_map/while/body/eval_jaxpr/psum | solution.py:25
  581.9 1.4 fusion.19
  583.4 0.7 broadcast_select_fusion.2
  584.1 90.1 %all-reduce.7.cloned.1.call-done = bf16[64,2048]{1,0:T(8,128)(2,1)} async-done(((bf16[64,2048]{1,0:T(8,128)(2,1)}), bf16[64,2048]{1,0:T(8,128)(2,1)}) %all-reduce.7.cloned.1.call-update) | async-done | bytes 262160 | tf_op jit(solution)/shard_map/while/body/eval_jaxpr/psum | solution.py:25
  674.3 1.4 fusion.19
  675.8 0.7 broadcast_select_fusion.2
  676.5 90.1 %all-reduce.7.cloned.1.call-done = bf16[64,2048]{1,0:T(8,128)(2,1)} async-done(((bf16[64,2048]{1,0:T(8,128)(2,1)}), bf16[64,2048]{1,0:T(8,128)(2,1)}) %all-reduce.7.cloned.1.call-update) | async-done | bytes 262160 | tf_op jit(solution)/shard_map/while/body/eval_jaxpr/psum | solution.py:25
  766.7 1.4 fusion.19
  768.1 0.7 copy-done.2
  768.9 222.9 %all-reduce.5.cloned.1.call-done = f32[256,512]{0,1:T(8,128)} async-done(((f32[256,512]{0,1:T(8,128)}), f32[256,512]{0,1:T(8,128)}) %all-reduce.5.cloned.1.call-update) | async-done | bytes 524304 | tf_op jit(solution)/shard_map/psum | solution.py:82
  991.9 1.2 reduce_sum.18
  993.1 1.1 multiply_reduce_fusion
  994.2 260.6 %gather_fusion = f32[32768]{0:T(1024)S(1)} fusion(f32[256,512]{0,1:T(8,128)S(1)} %copy-done, s32[32768]{0:T(1024)S(1)} %fusion.8), kind=kCustom, calls=%fused_computation | custom fusion | bytes 524288 | tf_op jit(solution)/shard_map/jit(take_along_axis)/gather | solution.py:39
  1254.8 0.1 fusion.7
  1255.0 0.2 compare_select_fusion
  1255.2 7.6 scatter_custom_fusion
  1262.8 76.1 %all-reduce.1 = f32[512]{0:T(512)S(1)} all-reduce(f32[512]{0:T(512)S(1)} %scatter_custom_fusion), channel_id=2, replica_groups=mesh['spec'=32,'bucket'=8] {'spec','bucket'}, use_global_device_ids=true, to_apply=%region_7.8.clone | all-reduce | flops 512 | bytes 4096
  1339.0 0.6 dynamic-slice_multiply_fusion
  (44 shorter events, 1.2 us)
Async XLA Ops:
  8.0 4.7 copy-start.5
  8.0 5.5 copy-start.3
  9.6 4.2 collective-permute-start
  11.3 4.8 collective-permute-start.1
  22.5 1.7 copy-start.1
  24.2 96.9 %all-reduce.7.cloned.1.call-start = ((), (), s32[]{:S(2)}) async-start(), calls=%async_computation.1 | async-start | bytes 524288 | tf_op jit(solution)/shard_map/while/body/eval_jaxpr/psum | solution.py:25
  122.5 91.0 %all-reduce.7.cloned.1.call-start = ((), (), s32[]{:S(2)}) async-start(), calls=%async_computation.1 | async-start | bytes 524288 | tf_op jit(solution)/shard_map/while/body/eval_jaxpr/psum | solution.py:25
  214.8 91.0 %all-reduce.7.cloned.1.call-start = ((), (), s32[]{:S(2)}) async-start(), calls=%async_computation.1 | async-start | bytes 524288 | tf_op jit(solution)/shard_map/while/body/eval_jaxpr/psum | solution.py:25
  307.2 90.6 %all-reduce.7.cloned.1.call-start = ((), (), s32[]{:S(2)}) async-start(), calls=%async_computation.1 | async-start | bytes 524288 | tf_op jit(solution)/shard_map/while/body/eval_jaxpr/psum | solution.py:25
  399.2 90.6 %all-reduce.7.cloned.1.call-start = ((), (), s32[]{:S(2)}) async-start(), calls=%async_computation.1 | async-start | bytes 524288 | tf_op jit(solution)/shard_map/while/body/eval_jaxpr/psum | solution.py:25
  491.3 90.6 %all-reduce.7.cloned.1.call-start = ((), (), s32[]{:S(2)}) async-start(), calls=%async_computation.1 | async-start | bytes 524288 | tf_op jit(solution)/shard_map/while/body/eval_jaxpr/psum | solution.py:25
  583.3 91.0 %all-reduce.7.cloned.1.call-start = ((), (), s32[]{:S(2)}) async-start(), calls=%async_computation.1 | async-start | bytes 524288 | tf_op jit(solution)/shard_map/while/body/eval_jaxpr/psum | solution.py:25
  675.7 91.0 %all-reduce.7.cloned.1.call-start = ((), (), s32[]{:S(2)}) async-start(), calls=%async_computation.1 | async-start | bytes 524288 | tf_op jit(solution)/shard_map/while/body/eval_jaxpr/psum | solution.py:25
  768.1 0.8 copy-start.2
  768.1 223.8 %all-reduce.5.cloned.1.call-start = ((), (), s32[]{:S(2)}) async-start(), calls=%async_computation | async-start | bytes 1048576 | tf_op jit(solution)/shard_map/psum | solution.py:82
  991.9 2.4 copy-start
  1254.9 84.6 %copy-start.4 = (f32[256,128]{1,0:T(8,128)}, f32[256,128]{1,0:T(8,128)S(1)}, u32[]{:S(2)}) copy-start(f32[256,128]{1,0:T(8,128)S(1)} %fusion.7) | copy-start | bytes 393220
Sparse Core Ops, SparseCore 0:
  27.8 93.1 all-reduce.6
  126.1 87.2 all-reduce.6
  218.5 87.2 all-reduce.6
  310.5 87.2 all-reduce.6
  402.6 87.2 all-reduce.6
  494.6 87.2 all-reduce.6
  587.0 87.2 all-reduce.6
  679.3 87.2 all-reduce.6
Sparse Core Ops, SparseCore 1:
  771.1 220.7 all-reduce.4
where the time goes:
time: 1350 us
  waiting for transfers between devices  952 us (71%)
  local copies, waits for them, and re-layouts  267 us (20%)
  blocking collectives  76.1 us (6%)
  other arithmetic  18.9 us (1%)
  between operations  15.7 us (1%)
  matrix products  13.8 us (1%)
    psum x8, waiting for transfers between devices, broadcast(): return lax.psum(kept, axis)  726 us
    gather x1, local copies, waits for them, and re-layouts, zscores(): picked = jnp.take_along_axis(score_tile, cand_ids, axis=1)  261 us
    psum x1, waiting for transfers between devices, on_device(): summed = lax.psum(score_tile, 'spec')  223 us
    unnamed x1, blocking collectives  76.1 us
  transfers between devices with their start and end apart: 11, of which 10 were waited for; matrix products, arithmetic and copies ran while one was open for 0% of the time, Pallas kernels for 0%

commit v1 on v0

v1 whole, which is shorter than its diff:
```python
import jax
import jax.numpy as jnp
from jax import lax
from jax.sharding import PartitionSpec as P

HALF = 75
REGION = 512


def halo(block, axis, width):
    count = lax.axis_size(axis)
    forward = [(i, i + 1) for i in range(count - 1)]
    backward = [(target, source) for source, target in forward]
    low = lax.ppermute(block[:, -width:], axis, forward)
    high = lax.ppermute(block[:, :width], axis, backward)
    return jnp.concatenate([low, block, high], axis=1)


def make_band(widths):
    block_iota = lax.broadcasted_iota(jnp.int32, (3, 128, 128), 0)
    input_iota = lax.broadcasted_iota(jnp.int32, (3, 128, 128), 1)
    output_iota = lax.broadcasted_iota(jnp.int32, (3, 128, 128), 2)
    offset = 128 * (block_iota - 1) + input_iota - output_iota
    return jnp.abs(offset)[None] <= widths[:, None, None, None]


def copies_to_all(value, axis):
    count = lax.axis_size(axis)
    spread = jnp.broadcast_to(value[None], (count,) + value.shape)
    return lax.all_to_all(spread, axis, 0, 0, tiled=True)


def on_device(spectra, theory, cand, half):
    row_count, bin_count = spectra.shape
    spec_count = lax.axis_size("spec")
    bucket_count = lax.axis_size("bucket")
    per_bucket = theory.shape[0]
    peptides_all = per_bucket * bucket_count
    position = lax.axis_index("spec")

    gathered = copies_to_all(theory, "bucket").reshape(peptides_all, bin_count)

    extended = halo(spectra, "spec", 128)
    bin_widths = jnp.repeat(half, REGION)
    tile_count = bin_count // 128
    tile_view = extended.reshape(row_count, tile_count + 2, 128)
    band_weights = make_band(jnp.repeat(half, REGION // 128)).astype(jnp.bfloat16)
    window_sums = jnp.zeros((row_count, tile_count, 128), jnp.float32)
    for k in range(3):
        window_sums = window_sums + jnp.einsum(
            "rtc,tcd->rtd",
            tile_view[:, k : k + tile_count],
            band_weights[:, k],
            preferred_element_type=jnp.float32,
        )
    window_sums = window_sums.reshape(row_count, bin_count)
    divisor = (2 * bin_widths + 1).astype(jnp.float32)
    processed = (spectra.astype(jnp.float32) - window_sums / divisor).astype(jnp.bfloat16)

    partial = lax.dot_general(
        processed, gathered, (((1,), (1,)), ((), ())), preferred_element_type=jnp.float32
    )
    partial = partial - jnp.mean(partial, axis=1, keepdims=True)

    own = row_count // spec_count
    parts = lax.all_to_all(
        partial.astype(jnp.bfloat16).reshape(spec_count, own, peptides_all), "spec", 0, 0, tiled=True
    )
    scores = jnp.sum(parts.astype(jnp.float32), axis=0)
    centred = scores - jnp.mean(scores, axis=1, keepdims=True)
    spread = jnp.mean(jnp.square(centred), axis=1, keepdims=True)
    own_cand = lax.dynamic_slice_in_dim(cand, position * own, own, 0)
    ids = lax.broadcasted_iota(jnp.int32, (1, 1, peptides_all), 2)
    picked = jnp.sum(jnp.where(own_cand[:, :, None] == ids, centred[:, None, :], 0.0), axis=2)
    own_scores = picked * lax.rsqrt(spread + 1e-06)

    cand_scores = copies_to_all(own_scores, "spec").reshape(row_count, cand.shape[1])

    share = peptides_all // spec_count
    kept = position * share + lax.broadcasted_iota(jnp.int32, (share, 1, 1), 0)
    soft = jax.nn.softplus(cand_scores)
    evidence = jnp.sum(jnp.where(cand[None] == kept, soft[None], 0.0), axis=1)
    evidence = lax.all_to_all(
        evidence.reshape(bucket_count, share // bucket_count, cand.shape[1]), "bucket", 0, 0, tiled=True
    )
    mean_load = cand.shape[1] * row_count / per_bucket
    peptide_score = jnp.sum(evidence, axis=(0, 2)) / mean_load
    return (cand_scores, peptide_score)


def solution(mesh):
    return jax.shard_map(
        on_device,
        mesh=mesh,
        in_specs=(P("bucket", "spec"), P("bucket", "spec"), P("bucket", None), P("spec")),
        out_specs=(P("bucket", None), P(("spec", "bucket"))),
        check_vma=False,
    )
```

time: 1350 us -> 99.2 us (0.07)
  waiting for transfers between devices: 952 us -> 51.8 us
  local copies, waits for them, and re-layouts: 267 us -> 6.53 us
  blocking collectives: 76.1 us -> 0 us
  starting transfers between devices: 3.41 us -> 31.1 us
  between operations: 15.7 us -> 0.81 us
  other arithmetic: 18.9 us -> 4.12 us
    psum x9 -> x0, waiting for transfers between devices: 949 us -> none  [the longest x8 726 us: broadcast(): return lax.psum(kept, axis)]
    gather x1 -> x0, local copies, waits for them, and re-layouts: 261 us -> none  [zscores(): picked = jnp.take_along_axis(score_tile, cand_ids, axis=1)]
    unnamed x1 -> x0, blocking collectives: 76.1 us -> none
    all_to_all x0 -> x4, waiting for transfers between devices: none -> 51.8 us  [the longest x2 32.4 us: copies_to_all(): return lax.all_to_all(spread, axis, 0, 0, tiled=True)]
    all_to_all x0 -> x4, starting transfers between devices: none -> 28 us  [the longest x2 11.4 us: copies_to_all(): return lax.all_to_all(spread, axis, 0, 0, tiled=True)]
  transfers between devices with their start and end apart: 11 -> 6, of which waited for: 10 -> 4; matrix products, arithmetic and copies ran while one was open for 0% -> 6% of each run, Pallas kernels for 0% -> 0%
where the time goes in v1:
time: 99.2 us; the launch traced here: 98.8 us
  waiting for transfers between devices  51.8 us (52%)
  starting transfers between devices  31.1 us (31%)
  local copies, waits for them, and re-layouts  6.53 us (7%)
  matrix products  4.43 us (4%)
  other arithmetic  4.12 us (4%)
    all_to_all x2, waiting for transfers between devices, copies_to_all(): return lax.all_to_all(spread, axis, 0, 0, tiled=True)  32.4 us
    all_to_all x1, waiting for transfers between devices, on_device(): lax.all_to_all(partial.astype(jnp.bfloat16).reshape(spec_count, own, pept...  13.1 us
    all_to_all x2, starting transfers between devices, copies_to_all(): return lax.all_to_all(spread, axis, 0, 0, tiled=True)  11.4 us
    all_to_all x1, starting transfers between devices, on_device(): lax.all_to_all(partial.astype(jnp.bfloat16).reshape(spec_count, own, pept...  11.1 us
    all_to_all x1, waiting for transfers between devices, on_device(): lax.all_to_all(evidence.reshape(bucket_count, share // bucket_count, cand...  6.23 us
    all_to_all x1, starting transfers between devices, on_device(): lax.all_to_all(evidence.reshape(bucket_count, share // bucket_count, cand...  5.52 us
    dot_general x1, matrix products, on_device(): lax.dot_general(processed, gathered, (((1,), (1,)), ((), ())), preferred_...  3.09 us
    unnamed x12, local copies, waits for them, and re-layouts  2.27 us
  transfers between devices with their start and end apart: 6, of which 4 were waited for; matrix products, arithmetic and copies ran while one was open for 6% of the time, Pallas kernels for 0%

profile of v1, /device:TPU:8, one launch (start us, length us, event | category | flops | bytes accessed | tf_op | source)
XLA Modules:
  0.0 98.8 jit_solution(11016088349435034228)
XLA Ops:
  0.6 0.0 copy-start.1
  0.6 1.5 %copy.22 = bf16[256,2048]{0,1:T(8,128)(2,1)S(1)} copy(bf16[256,2048]{1,0:T(8,128)(2,1)} %param.4) | data formatting | bytes 2097152 | tf_op args[0]
  2.2 1.7 %collective-permute-start = (bf16[256,128]{0,1:T(8,128)(2,1)S(1)}, bf16[256,128]{0,1:T(8,128)(2,1)S(1)}, u32[]{:S(2)}, u32[]{:S(2)}) collective-permute-start(bf16[256,128]{0,1:T(8,128)(2,1)S(1)} %get-tuple-element.6), channel_id=1, source_target_pairs={{0,8},{8,16},{16,24},{24,32},{32,40},{40,48},{48,56},{56,64},{64,7... | collective-permute-start | bytes 196616 | tf_op jit(solution)/shard_map/ppermute | solution.py:14
  3.9 1.3 %collective-permute-start.1 = (bf16[256,128]{0,1:T(8,128)(2,1)S(1)}, bf16[256,128]{0,1:T(8,128)(2,1)S(1)}, u32[]{:S(2)}, u32[]{:S(2)}) collective-permute-start(bf16[256,128]{0,1:T(8,128)(2,1)S(1)} %get-tuple-element.7), channel_id=1, source_target_pairs={{8,0},{16,8},{24,16},{32,24},{40,32},{48,40},{56,48},{64,56},{72,6... | collective-permute-start | bytes 196616 | tf_op jit(solution)/shard_map/ppermute | solution.py:15
  5.2 0.0 copy-done.1
  5.2 1.6 %broadcast_in_dim.30 = bf16[8,64,2048]{2,1,0:T(8,128)(2,1)} broadcast(bf16[64,2048]{1,0:T(8,128)(2,1)S(1)} %copy-done.1), dimensions={1,2} | broadcast | bytes 2359296 | tf_op jit(solution)/shard_map/broadcast_in_dim | solution.py:29
  6.8 0.0 copy-start.3
  6.8 7.5 %all-to-all-start = ((bf16[8,64,2048]{2,1,0:T(8,128)(2,1)}), bf16[8,64,2048]{2,1,0:T(8,128)(2,1)}, u32[]{:S(2)}, u32[]{:S(2)}) async-start(bf16[8,64,2048]{2,1,0:T(8,128)(2,1)} %broadcast_in_dim.30), calls=%async_computation | async-start | bytes 4194304 | tf_op jit(solution)/shard_map/all_to_all | solution.py:30
  14.3 0.1 subtract_abs_fusion
  14.4 0.0 copy-done.3
  14.4 0.1 broadcast_in_dim.28
  14.5 0.1 le.16
  14.6 0.5 broadcast_compare_fusion
  15.1 0.1 broadcast_bitcast_fusion
  15.2 0.0 collective-permute-done
  15.2 0.0 collective-permute-done.1
  15.2 0.1 pad_maximum_fusion
  15.3 0.4 fusion.1
  15.7 0.4 fusion.3
  16.2 0.5 add_add_fusion
  16.6 0.0 copy-start
  16.7 1.9 %copy.28 = f32[256,2048]{1,0:T(8,128)} copy(f32[256,2048]{0,1:T(8,128)S(1)} %bitcast.26) | data formatting | bytes 4194304 | tf_op jit(solution)/shard_map/reshape | solution.py:56
  18.5 22.0 %all-to-all-done = bf16[8,64,2048]{2,1,0:T(8,128)(2,1)} async-done(((bf16[8,64,2048]{2,1,0:T(8,128)(2,1)}), bf16[8,64,2048]{2,1,0:T(8,128)(2,1)}, u32[]{:S(2)}, u32[]{:S(2)}) %all-to-all-start) | async-done | bytes 2097184 | tf_op jit(solution)/shard_map/all_to_all | solution.py:30
  40.5 0.0 copy-done
  40.5 0.0 copy-start.2
  40.5 3.1 %fusion.8 = (f32[256]{0:T(256)S(1)}, f32[256,512]{1,0:T(8,128)S(1)}) fusion(bf16[512,2048]{1,0:T(8,128)(2,1)} %bitcast.6, f32[256,2048]{1,0:T(8,128)} %copy.28, bf16[256,2048]{1,0:T(8,128)(2,1)S(1)} %copy-done, f32[2048]{0:T(1024)S(1)} %bitcast.28), kind=kOutput, calls=%fused_computation.35 | convolution fusion | flops 539098880 | bytes 5776384 | tf_op jit(solution)/shard_map/dot_general | solution.py:60
  43.6 0.8 fusion.6
  44.4 11.1 %all-to-all-start.1 = ((bf16[32,8,512]{2,1,0:T(8,128)(2,1)}), bf16[32,8,512]{2,1,0:T(8,128)(2,1)S(1)}, u32[]{:S(2)}, u32[]{:S(2)}) async-start(bf16[32,8,512]{2,1,0:T(8,128)(2,1)} %fusion.6), calls=%async_computation.1 | async-start | bytes 524288 | tf_op jit(solution)/shard_map/all_to_all | solution.py:66
  55.6 0.0 copy-done.2
  55.6 13.1 %all-to-all-done.1 = bf16[32,8,512]{2,1,0:T(8,128)(2,1)S(1)} async-done(((bf16[32,8,512]{2,1,0:T(8,128)(2,1)}), bf16[32,8,512]{2,1,0:T(8,128)(2,1)S(1)}, u32[]{:S(2)}, u32[]{:S(2)}) %all-to-all-start.1) | async-done | bytes 262176 | tf_op jit(solution)/shard_map/all_to_all | solution.py:66
  68.7 0.2 convert_reduce_fusion
  69.0 0.2 multiply_reduce_fusion
  69.2 0.5 select_reduce_fusion.1
  69.7 0.1 broadcast_multiply_fusion
  69.7 0.7 broadcast_in_dim.56
  70.4 3.9 %all-to-all-start.2 = ((f32[32,8,128]{2,1,0:T(8,128)}), f32[32,8,128]{2,1,0:T(8,128)S(1)}, u32[]{:S(2)}, u32[]{:S(2)}) async-start(f32[32,8,128]{2,1,0:T(8,128)} %broadcast_in_dim.56), calls=%async_computation.2 | async-start | bytes 262144 | tf_op jit(solution)/shard_map/all_to_all | solution.py:30
  74.3 10.4 %all-to-all-done.2 = f32[32,8,128]{2,1,0:T(8,128)S(1)} async-done(((f32[32,8,128]{2,1,0:T(8,128)}), f32[32,8,128]{2,1,0:T(8,128)S(1)}, u32[]{:S(2)}, u32[]{:S(2)}) %all-to-all-start.2) | async-done | bytes 131104 | tf_op jit(solution)/shard_map/all_to_all | solution.py:30
  84.7 0.1 compare_select_fusion
  84.8 0.9 select_reduce_fusion
  85.7 5.5 %all-to-all-start.3 = ((f32[8,2,128]{2,1,0:T(2,128)}), f32[8,2,128]{2,1,0:T(2,128)S(1)}, u32[]{:S(2)}, u32[]{:S(2)}) async-start(f32[8,2,128]{2,1,0:T(2,128)} %bitcast.9), calls=%async_computation.3 | async-start | bytes 16384 | tf_op jit(solution)/shard_map/all_to_all | solution.py:83
  91.2 6.2 %all-to-all-done.3 = f32[8,2,128]{2,1,0:T(2,128)S(1)} async-done(((f32[8,2,128]{2,1,0:T(2,128)}), f32[8,2,128]{2,1,0:T(2,128)S(1)}, u32[]{:S(2)}, u32[]{:S(2)}) %all-to-all-start.3) | async-done | bytes 8224 | tf_op jit(solution)/shard_map/all_to_all | solution.py:83
  97.5 0.1 reduce_sum.69
  97.6 0.5 broadcast_multiply_fusion.2
  98.1 0.7 copy.37
  (9 shorter events, 0.1 us)
Async XLA Ops:
  0.6 4.6 %copy-start.1 = (bf16[64,2048]{1,0:T(8,128)(2,1)S(1)}, bf16[64,2048]{1,0:T(8,128)(2,1)}, u32[]{:S(2)}) copy-start(bf16[64,2048]{1,0:T(8,128)(2,1)} %param.5) | copy-start | bytes 786436
  2.2 13.0 %collective-permute-start = (bf16[256,128]{0,1:T(8,128)(2,1)S(1)}, bf16[256,128]{0,1:T(8,128)(2,1)S(1)}, u32[]{:S(2)}, u32[]{:S(2)}) collective-permute-start(bf16[256,128]{0,1:T(8,128)(2,1)S(1)} %get-tuple-element.6), channel_id=1, source_target_pairs={{0,8},{8,16},{16,24},{24,32},{32,40},{40,48},{48,56},{56,64},{64,7... | collective-permute-start | bytes 196616 | tf_op jit(solution)/shard_map/ppermute | solution.py:14
  3.9 11.3 %collective-permute-start.1 = (bf16[256,128]{0,1:T(8,128)(2,1)S(1)}, bf16[256,128]{0,1:T(8,128)(2,1)S(1)}, u32[]{:S(2)}, u32[]{:S(2)}) collective-permute-start(bf16[256,128]{0,1:T(8,128)(2,1)S(1)} %get-tuple-element.7), channel_id=1, source_target_pairs={{8,0},{16,8},{24,16},{32,24},{40,32},{48,40},{56,48},{64,56},{72,6... | collective-permute-start | bytes 196616 | tf_op jit(solution)/shard_map/ppermute | solution.py:15
  6.8 7.6 %copy-start.3 = (s32[4]{0:T(128)S(1)}, s32[4]{0:T(128)}, u32[]{:S(2)}) copy-start(s32[4]{0:T(128)} %param.7) | copy-start | bytes 52
  6.8 33.7 %all-to-all-start = ((bf16[8,64,2048]{2,1,0:T(8,128)(2,1)}), bf16[8,64,2048]{2,1,0:T(8,128)(2,1)}, u32[]{:S(2)}, u32[]{:S(2)}) async-start(bf16[8,64,2048]{2,1,0:T(8,128)(2,1)} %broadcast_in_dim.30), calls=%async_computation | async-start | bytes 4194304 | tf_op jit(solution)/shard_map/all_to_all | solution.py:30
  16.6 23.9 %copy-start = (bf16[256,2048]{1,0:T(8,128)(2,1)S(1)}, bf16[256,2048]{1,0:T(8,128)(2,1)}, u32[]{:S(2)}) copy-start(bf16[256,2048]{1,0:T(8,128)(2,1)} %param.4) | copy-start | bytes 3145732
  40.5 15.1 %copy-start.2 = (s32[256,128]{1,0:T(8,128)S(1)}, s32[256,128]{1,0:T(8,128)}, u32[]{:S(2)}) copy-start(s32[256,128]{1,0:T(8,128)} %param.6) | copy-start | bytes 393220
  44.4 24.3 %all-to-all-start.1 = ((bf16[32,8,512]{2,1,0:T(8,128)(2,1)}), bf16[32,8,512]{2,1,0:T(8,128)(2,1)S(1)}, u32[]{:S(2)}, u32[]{:S(2)}) async-start(bf16[32,8,512]{2,1,0:T(8,128)(2,1)} %fusion.6), calls=%async_computation.1 | async-start | bytes 524288 | tf_op jit(solution)/shard_map/all_to_all | solution.py:66
  70.4 14.3 %all-to-all-start.2 = ((f32[32,8,128]{2,1,0:T(8,128)}), f32[32,8,128]{2,1,0:T(8,128)S(1)}, u32[]{:S(2)}, u32[]{:S(2)}) async-start(f32[32,8,128]{2,1,0:T(8,128)} %broadcast_in_dim.56), calls=%async_computation.2 | async-start | bytes 262144 | tf_op jit(solution)/shard_map/all_to_all | solution.py:30
  85.7 11.8 %all-to-all-start.3 = ((f32[8,2,128]{2,1,0:T(2,128)}), f32[8,2,128]{2,1,0:T(2,128)S(1)}, u32[]{:S(2)}, u32[]{:S(2)}) async-start(f32[8,2,128]{2,1,0:T(2,128)} %bitcast.9), calls=%async_computation.3 | async-start | bytes 16384 | tf_op jit(solution)/shard_map/all_to_all | solution.py:83

commit v2 on v1

v2 whole, which is shorter than its diff:
```python
import jax
import jax.numpy as jnp
from jax import lax
from jax.experimental import pallas as pl
from jax.experimental.pallas import tpu as pltpu
from jax.sharding import PartitionSpec as P

REGION = 512
SIDE = 128
TILE = 256

VMEM = pl.BlockSpec(memory_space=pltpu.VMEM)
SMEM = pl.BlockSpec(memory_space=pltpu.SMEM)


def params():
    return pltpu.CompilerParams(vmem_limit_bytes=16 * 1024 * 1024)


def window_kernel(half_ref, spectra_ref, low_ref, high_ref, out_ref, wide_ref):
    bins = spectra_ref.shape[1]
    wide_ref[:, :SIDE] = low_ref[...]
    wide_ref[:, SIDE : SIDE + bins] = spectra_ref[...]
    wide_ref[:, SIDE + bins :] = high_ref[...]
    taken = TILE + 2 * SIDE
    source = lax.broadcasted_iota(jnp.int32, (taken, TILE), 0) - SIDE
    target = lax.broadcasted_iota(jnp.int32, (taken, TILE), 1)
    distance = jnp.abs(source - target)
    for region in range(bins // REGION):
        width = half_ref[region]
        band = jnp.where(distance <= width, 1.0, 0.0).astype(jnp.bfloat16)
        divisor = (2 * width + 1).astype(jnp.float32)
        for tile in range(REGION // TILE):
            at = region * REGION + tile * TILE
            sums = jnp.dot(wide_ref[:, at : at + taken], band, preferred_element_type=jnp.float32)
            middle = wide_ref[:, at + SIDE : at + SIDE + TILE].astype(jnp.float32)
            out_ref[:, at : at + TILE] = (middle - sums / divisor).astype(jnp.bfloat16)


def windowed(half, spectra, low, high):
    rows, bins = spectra.shape
    return pl.pallas_call(
        window_kernel,
        out_shape=jax.ShapeDtypeStruct((rows, bins), jnp.bfloat16),
        in_specs=[SMEM, VMEM, VMEM, VMEM],
        out_specs=VMEM,
        scratch_shapes=[pltpu.VMEM((rows, bins + 2 * SIDE), jnp.bfloat16)],
        compiler_params=params(),
        cost_estimate=pl.CostEstimate(flops=2 * rows * bins * 512, bytes_accessed=4 * rows * bins, transcendentals=0),
    )(half, spectra, low, high)


def score_kernel(processed_ref, theory_ref, out_ref):
    scores = lax.dot_general(
        processed_ref[...],
        theory_ref[...],
        (((1,), (1,)), ((), ())),
        preferred_element_type=jnp.float32,
    )
    scores = scores - jnp.mean(scores, axis=1, keepdims=True)
    out_ref[...] = scores.astype(jnp.bfloat16)


def scored(processed, gathered):
    rows, bins = processed.shape
    peptides = gathered.shape[0]
    return pl.pallas_call(
        score_kernel,
        out_shape=jax.ShapeDtypeStruct((rows, peptides), jnp.bfloat16),
        in_specs=[VMEM, VMEM],
        out_specs=VMEM,
        compiler_params=params(),
        cost_estimate=pl.CostEstimate(
            flops=2 * rows * bins * peptides, bytes_accessed=2 * (rows + peptides) * bins, transcendentals=0
        ),
    )(processed, gathered)


def pick_kernel(position_ref, parts_ref, cand_ref, out_ref):
    count, own, peptides = parts_ref.shape
    lanes = cand_ref.shape[1]
    scores = jnp.sum(parts_ref[...].astype(jnp.float32), axis=0)
    centred = scores - jnp.mean(scores, axis=1, keepdims=True)
    spread = jnp.mean(jnp.square(centred), axis=1, keepdims=True)
    first = pl.multiple_of(position_ref[0] * own, own)
    ids = cand_ref[pl.ds(first, own), :]
    picked = jnp.zeros((own, lanes), jnp.float32)
    for block in range(peptides // lanes):
        part = centred[:, block * lanes : (block + 1) * lanes]
        value = jnp.take_along_axis(part, ids & (lanes - 1), axis=1)
        picked = jnp.where(ids // lanes == block, value, picked)
    result = picked * lax.rsqrt(spread + 1e-06)
    out_ref[...] = jnp.broadcast_to(result[None], out_ref.shape)


def picked_copies(position, parts, cand):
    count, own, peptides = parts.shape
    return pl.pallas_call(
        pick_kernel,
        out_shape=jax.ShapeDtypeStruct((count, own, cand.shape[1]), jnp.float32),
        in_specs=[SMEM, VMEM, VMEM],
        out_specs=VMEM,
        compiler_params=params(),
    )(position, parts, cand)


def evidence_kernel(position_ref, value_ref, cand_ref, out_ref):
    share = out_ref.shape[0]
    rows, lanes = value_ref.shape
    soft = jax.nn.softplus(value_ref[...])
    ids = cand_ref[...] - position_ref[0] * share
    for k in range(share):
        kept = jnp.where(ids == k, soft, 0.0)
        out_ref[k : k + 1, :] = jnp.sum(kept, axis=0, keepdims=True)


def evidence_of(position, values, cand, share):
    return pl.pallas_call(
        evidence_kernel,
        out_shape=jax.ShapeDtypeStruct((share, cand.shape[1]), jnp.float32),
        in_specs=[SMEM, VMEM, VMEM],
        out_specs=VMEM,
        compiler_params=params(),
    )(position, values, cand)


def on_device(spectra, theory, cand, half):
    row_count, bin_count = spectra.shape
    spec_count = lax.axis_size("spec")
    bucket_count = lax.axis_size("bucket")
    per_bucket = theory.shape[0]
    peptides_all = per_bucket * bucket_count
    position = lax.axis_index("spec").astype(jnp.int32).reshape(1)

    copies = jnp.broadcast_to(theory[None], (bucket_count,) + theory.shape)
    copies, observed = lax.optimization_barrier((copies, spectra))
    gathered = lax.all_to_all(copies, "bucket", 0, 0, tiled=True)

    forward = [(i, i + 1) for i in range(spec_count - 1)]
    backward = [(target, source) for source, target in forward]
    low = lax.ppermute(observed[:, -SIDE:], "spec", forward)
    high = lax.ppermute(observed[:, :SIDE], "spec", backward)
    processed = windowed(half, spectra, low, high)

    partial = scored(processed, gathered.reshape(peptides_all, bin_count))

    own = row_count // spec_count
    parts = lax.all_to_all(partial.reshape(spec_count, own, peptides_all), "spec", 0, 0, tiled=True)
    copies = picked_copies(position, parts, cand)
    cand_scores = lax.all_to_all(copies, "spec", 0, 0, tiled=True).reshape(row_count, cand.shape[1])

    share = peptides_all // spec_count
    evidence = evidence_of(position, cand_scores, cand, share)
    evidence = lax.all_to_all(
        evidence.reshape(bucket_count, share // bucket_count, cand.shape[1]), "bucket", 0, 0, tiled=True
    )
    mean_load = cand.shape[1] * row_count / per_bucket
    peptide_score = jnp.sum(evidence, axis=(0, 2)) / mean_load
    return (cand_scores, peptide_score)


def solution(mesh):
    return jax.shard_map(
        on_device,
        mesh=mesh,
        in_specs=(P("bucket", "spec"), P("bucket", "spec"), P("bucket", None), P("spec")),
        out_specs=(P("bucket", None), P(("spec", "bucket"))),
        check_vma=False,
    )
```

time: 99.2 us -> 87.8 us (0.89)
  blocking collectives: 0 us -> 24.5 us
  waiting for transfers between devices: 51.8 us -> 31.9 us
  starting transfers between devices: 31.1 us -> 20.9 us
  matrix products: 4.43 us -> 0 us
  other arithmetic: 4.12 us -> 0.64 us
  Pallas kernels: 0 us -> 3.33 us
  local copies, waits for them, and re-layouts: 6.53 us -> 5.33 us
    all_to_all x0 -> x2, blocking collectives: none -> 24.5 us  [the longest x1 13.4 us: on_device(): lax.all_to_all(copies, 'spec', 0, 0, tiled=True)]
    all_to_all x4 -> x2, waiting for transfers between devices: 51.8 us -> 31 us  [the longest x1 17.9 us: on_device(): gathered = lax.all_to_all(copies, 'bucket', 0, 0, tiled=True)]
    all_to_all x4 -> x2, starting transfers between devices: 28 us -> 16.6 us  [the longest x1 9.1 us: on_device(): lax.all_to_all(partial.reshape(spec_count, own, peptides_all), 'spec', 0,...]
    dot_general x4 -> x0, matrix products: 4.43 us -> none  [the longest x1 3.09 us: on_device(): lax.dot_general(processed, gathered, (((1,), (1,)), ((), ())), preferred_...]
    pallas_call x0 -> x4, Pallas kernels: none -> 3.33 us  [the longest x1 1.52 us: scored(): pl.pallas_call(score_kernel, out_shape=jax.ShapeDtypeStruct((rows, peptid...]
    reshape x1 -> x0, local copies, waits for them, and re-layouts: 1.86 us -> none  [on_device(): window_sums = window_sums.reshape(row_count, bin_count)]
    reduce_sum x4 -> x0, other arithmetic: 1.8 us -> none  [the longest x1 0.89 us: on_device(): evidence = jnp.sum(jnp.where(cand[None] == kept, soft[None], 0.0), axis=1)]
    ppermute x2, starting transfers between devices: 3.03 us -> 4.33 us  [the longest x1 3.03 us: on_device(): low = lax.ppermute(observed[:, -SIDE:], 'spec', forward)]
  transfers between devices with their start and end apart: 6 -> 4, of which waited for: 4 -> 3; matrix products, arithmetic and copies ran while one was open for 6% -> 1% of each run, Pallas kernels for 0% -> 1%
where the time goes in v2:
time: 87.8 us; the launch traced here: 87.4 us
  waiting for transfers between devices  31.9 us (36%)
  blocking collectives  24.5 us (28%)
  starting transfers between devices  20.9 us (24%)
  local copies, waits for them, and re-layouts  5.33 us (6%)
  Pallas kernels  3.33 us (4%)
    all_to_all x1, waiting for transfers between devices, on_device(): gathered = lax.all_to_all(copies, 'bucket', 0, 0, tiled=True)  17.9 us
    all_to_all x1, blocking collectives, on_device(): lax.all_to_all(copies, 'spec', 0, 0, tiled=True)  13.4 us
    all_to_all x1, waiting for transfers between devices, on_device(): lax.all_to_all(partial.reshape(spec_count, own, peptides_all), 'spec', 0,...  13.2 us
    all_to_all x1, blocking collectives, on_device(): lax.all_to_all(evidence.reshape(bucket_count, share // bucket_count, cand...  11.1 us
    all_to_all x1, starting transfers between devices, on_device(): lax.all_to_all(partial.reshape(spec_count, own, peptides_all), 'spec', 0,...  9.1 us
    all_to_all x1, starting transfers between devices, on_device(): gathered = lax.all_to_all(copies, 'bucket', 0, 0, tiled=True)  7.51 us
    ppermute x1, starting transfers between devices, on_device(): low = lax.ppermute(observed[:, -SIDE:], 'spec', forward)  3.03 us
    broadcast_in_dim x1, local copies, waits for them, and re-layouts, on_device(): copies = jnp.broadcast_to(theory[None], (bucket_count,) + theory.shape)  2.55 us
  transfers between devices with their start and end apart: 4, of which 3 were waited for; matrix products, arithmetic and copies ran while one was open for 1% of the time, Pallas kernels for 1%

profile of v2, /device:TPU:8, one launch (start us, length us, event | category | flops | bytes accessed | tf_op | source)
XLA Modules:
  0.0 87.4 jit_solution(11716897125611092953)
XLA Ops:
  0.6 2.6 %broadcast_in_dim.2 = bf16[8,64,2048]{2,1,0:T(8,128)(2,1)} broadcast(bf16[64,2048]{1,0:T(8,128)(2,1)} %param.5), dimensions={1,2} | broadcast | bytes 2359296 | tf_op jit(solution)/shard_map/broadcast_in_dim | solution.py:135
  3.2 0.0 copy-start.2
  3.2 7.5 %all-to-all-start = ((bf16[8,64,2048]{2,1,0:T(8,128)(2,1)}), bf16[8,64,2048]{2,1,0:T(8,128)(2,1)S(1)}, u32[]{:S(2)}, u32[]{:S(2)}) async-start(bf16[8,64,2048]{2,1,0:T(8,128)(2,1)} %broadcast_in_dim.2), calls=%async_computation | async-start | bytes 4194304 | tf_op jit(solution)/shard_map/all_to_all | solution.py:137
  10.7 0.9 %fusion = (bf16[256,128]{1,0:T(8,128)(2,1)S(1)}, bf16[256,128]{1,0:T(8,128)(2,1)S(1)}) fusion(bf16[256,2048]{1,0:T(8,128)(2,1)} %spectra_ref.1), kind=kLoop, calls=%fused_computation.1 | loop fusion | bytes 262144 | tf_op jit(solution)/shard_map/slice | solution.py:142
  11.6 1.3 %collective-permute-start.1 = (bf16[256,128]{1,0:T(8,128)(2,1)S(1)}, bf16[256,128]{1,0:T(8,128)(2,1)S(1)}, u32[]{:S(2)}, u32[]{:S(2)}) collective-permute-start(bf16[256,128]{1,0:T(8,128)(2,1)S(1)} %get-tuple-element.6), channel_id=1, source_target_pairs={{8,0},{16,8},{24,16},{32,24},{40,32},{48,40},{56,48},{64,56},{72,6... | collective-permute-start | bytes 196616 | tf_op jit(solution)/shard_map/ppermute | solution.py:142
  12.9 3.0 %collective-permute-start = (bf16[256,128]{1,0:T(8,128)(2,1)S(1)}, bf16[256,128]{1,0:T(8,128)(2,1)S(1)}, u32[]{:S(2)}, u32[]{:S(2)}) collective-permute-start(bf16[256,128]{1,0:T(8,128)(2,1)S(1)} %get-tuple-element.7), channel_id=1, source_target_pairs={{0,8},{8,16},{16,24},{24,32},{32,40},{40,48},{48,56},{56,64},{64,7... | collective-permute-start | bytes 196616 | tf_op jit(solution)/shard_map/ppermute | solution.py:141
  15.9 0.0 collective-permute-done.1.high_ref
  15.9 0.9 collective-permute-done.low_ref
  16.8 0.0 copy-done.2
  16.8 0.0 copy-start
  16.8 1.2 %copy-done = bf16[256,2048]{1,0:T(8,128)(2,1)S(1)} copy-done((bf16[256,2048]{1,0:T(8,128)(2,1)S(1)}, bf16[256,2048]{1,0:T(8,128)(2,1)}, u32[]{:S(2)}) %copy-start) | copy-done | bytes 1048600
  18.0 1.3 %shard_map.59.processed_ref = bf16[256,2048]{1,0:T(8,128)(2,1)S(1)} custom-call(s32[4]{0:T(128)S(1)} %copy-done.2, bf16[256,2048]{1,0:T(8,128)(2,1)S(1)} %copy-done, bf16[256,128]{1,0:T(8,128)(2,1)S(1)} %collective-permute-done.low_ref, bf16[256,128]{1,0:T(8,128)(2,1)S(1)} %collective-permute-done.1.high_ref), custom_call_target="tpu_custom_call" | custom-call | flops 536870912 | bytes 2097152 | tf_op jit(solution)/shard_map/pallas_call | solution.py:42
  19.3 0.0 copy-start.1
  19.3 17.9 %all-to-all-done = bf16[8,64,2048]{2,1,0:T(8,128)(2,1)S(1)} async-done(((bf16[8,64,2048]{2,1,0:T(8,128)(2,1)}), bf16[8,64,2048]{2,1,0:T(8,128)(2,1)S(1)}, u32[]{:S(2)}, u32[]{:S(2)}) %all-to-all-start) | async-done | bytes 2097184 | tf_op jit(solution)/shard_map/all_to_all | solution.py:137
  37.2 1.5 %shard_map.60 = bf16[256,512]{1,0:T(8,128)(2,1)} custom-call(bf16[256,2048]{1,0:T(8,128)(2,1)S(1)} %shard_map.59.processed_ref, bf16[512,2048]{1,0:T(8,128)(2,1)S(1)} %bitcast.5), custom_call_target="tpu_custom_call" | custom-call | flops 536870912 | bytes 3145728 | tf_op jit(solution)/shard_map/pallas_call | solution.py:67
  38.7 9.1 %all-to-all-start.1 = ((bf16[32,8,512]{2,1,0:T(8,128)(2,1)}), bf16[32,8,512]{2,1,0:T(8,128)(2,1)S(1)}, u32[]{:S(2)}, u32[]{:S(2)}) async-start(bf16[32,8,512]{2,1,0:T(8,128)(2,1)} %bitcast.2), calls=%async_computation.1 | async-start | bytes 524288 | tf_op jit(solution)/shard_map/all_to_all | solution.py:148
  47.8 13.2 %all-to-all-done.1.parts_ref = bf16[32,8,512]{2,1,0:T(8,128)(2,1)S(1)} async-done(((bf16[32,8,512]{2,1,0:T(8,128)(2,1)}), bf16[32,8,512]{2,1,0:T(8,128)(2,1)S(1)}, u32[]{:S(2)}, u32[]{:S(2)}) %all-to-all-start.1) | async-done | bytes 262176 | tf_op jit(solution)/shard_map/all_to_all | solution.py:148
  61.0 0.0 copy-done.1
  61.0 0.2 shard_map.61
  61.2 13.4 %all_to_all.20 = f32[32,8,128]{2,1,0:T(8,128)S(1)} all-to-all(f32[32,8,128]{2,1,0:T(8,128)S(1)} %shard_map.61), channel_id=1, replica_groups=mesh['spec'=32,'bucket'=8] {'spec'}, dimensions={0} | all-to-all | bytes 262144 | tf_op jit(solution)/shard_map/all_to_all | solution.py:150
  74.6 0.3 shard_map.62
  75.0 11.1 %all_to_all.21 = f32[8,2,128]{2,1,0:T(2,128)S(1)} all-to-all(f32[8,2,128]{2,1,0:T(2,128)S(1)} %bitcast.8), channel_id=1, replica_groups=mesh['spec'=32,'bucket'=8] {'bucket'}, dimensions={0} | all-to-all | bytes 16384 | tf_op jit(solution)/shard_map/all_to_all | solution.py:154
  86.1 0.1 reduce_sum.9
  86.2 0.5 broadcast_multiply_fusion
  86.7 0.7 copy.7
Async XLA Ops:
  3.2 13.6 %copy-start.2 = (s32[4]{0:T(128)S(1)}, s32[4]{0:T(128)}, u32[]{:S(2)}) copy-start(s32[4]{0:T(128)} %half_ref.1) | copy-start | bytes 52
  3.2 34.0 %all-to-all-start = ((bf16[8,64,2048]{2,1,0:T(8,128)(2,1)}), bf16[8,64,2048]{2,1,0:T(8,128)(2,1)S(1)}, u32[]{:S(2)}, u32[]{:S(2)}) async-start(bf16[8,64,2048]{2,1,0:T(8,128)(2,1)} %broadcast_in_dim.2), calls=%async_computation | async-start | bytes 4194304 | tf_op jit(solution)/shard_map/all_to_all | solution.py:137
  11.6 4.3 %collective-permute-start.1 = (bf16[256,128]{1,0:T(8,128)(2,1)S(1)}, bf16[256,128]{1,0:T(8,128)(2,1)S(1)}, u32[]{:S(2)}, u32[]{:S(2)}) collective-permute-start(bf16[256,128]{1,0:T(8,128)(2,1)S(1)} %get-tuple-element.6), channel_id=1, source_target_pairs={{8,0},{16,8},{24,16},{32,24},{40,32},{48,40},{56,48},{64,56},{72,6... | collective-permute-start | bytes 196616 | tf_op jit(solution)/shard_map/ppermute | solution.py:142
  12.9 3.9 %collective-permute-start = (bf16[256,128]{1,0:T(8,128)(2,1)S(1)}, bf16[256,128]{1,0:T(8,128)(2,1)S(1)}, u32[]{:S(2)}, u32[]{:S(2)}) collective-permute-start(bf16[256,128]{1,0:T(8,128)(2,1)S(1)} %get-tuple-element.7), channel_id=1, source_target_pairs={{0,8},{8,16},{16,24},{24,32},{32,40},{40,48},{48,56},{56,64},{64,7... | collective-permute-start | bytes 196616 | tf_op jit(solution)/shard_map/ppermute | solution.py:141
  16.8 1.2 %copy-start = (bf16[256,2048]{1,0:T(8,128)(2,1)S(1)}, bf16[256,2048]{1,0:T(8,128)(2,1)}, u32[]{:S(2)}) copy-start(bf16[256,2048]{1,0:T(8,128)(2,1)} %spectra_ref.1) | copy-start | bytes 3145732
  19.3 41.7 %copy-start.1 = (s32[256,128]{1,0:T(8,128)S(1)}, s32[256,128]{1,0:T(8,128)}, u32[]{:S(2)}) copy-start(s32[256,128]{1,0:T(8,128)} %cand_ref.3) | copy-start | bytes 393220
  38.7 22.3 %all-to-all-start.1 = ((bf16[32,8,512]{2,1,0:T(8,128)(2,1)}), bf16[32,8,512]{2,1,0:T(8,128)(2,1)S(1)}, u32[]{:S(2)}, u32[]{:S(2)}) async-start(bf16[32,8,512]{2,1,0:T(8,128)(2,1)} %bitcast.2), calls=%async_computation.1 | async-start | bytes 524288 | tf_op jit(solution)/shard_map/all_to_all | solution.py:148

commit v3 on v2

v3 whole, which is shorter than its diff:
```python
import functools

import jax
import jax.numpy as jnp
from jax import lax
from jax.experimental import pallas as pl
from jax.experimental.pallas import tpu as pltpu
from jax.sharding import PartitionSpec as P

REGION = 512
SIDE = 128
TILE = 256

VMEM = pl.BlockSpec(memory_space=pltpu.VMEM)
SMEM = pl.BlockSpec(memory_space=pltpu.SMEM)


def params():
    return pltpu.CompilerParams(vmem_limit_bytes=16 * 1024 * 1024)


def window_kernel(half_ref, spectra_ref, low_ref, high_ref, out_ref, wide_ref):
    bins = spectra_ref.shape[1]
    wide_ref[:, :SIDE] = low_ref[...]
    wide_ref[:, SIDE : SIDE + bins] = spectra_ref[...]
    wide_ref[:, SIDE + bins :] = high_ref[...]
    taken = TILE + 2 * SIDE
    source = lax.broadcasted_iota(jnp.int32, (taken, TILE), 0) - SIDE
    target = lax.broadcasted_iota(jnp.int32, (taken, TILE), 1)
    distance = jnp.abs(source - target)
    for region in range(bins // REGION):
        width = half_ref[region]
        band = jnp.where(distance <= width, 1.0, 0.0).astype(jnp.bfloat16)
        divisor = (2 * width + 1).astype(jnp.float32)
        for tile in range(REGION // TILE):
            at = region * REGION + tile * TILE
            sums = jnp.dot(wide_ref[:, at : at + taken], band, preferred_element_type=jnp.float32)
            middle = wide_ref[:, at + SIDE : at + SIDE + TILE].astype(jnp.float32)
            out_ref[:, at : at + TILE] = (middle - sums / divisor).astype(jnp.bfloat16)


def windowed(half, spectra, low, high):
    rows, bins = spectra.shape
    return pl.pallas_call(
        window_kernel,
        out_shape=jax.ShapeDtypeStruct((rows, bins), jnp.bfloat16),
        in_specs=[SMEM, VMEM, VMEM, VMEM],
        out_specs=VMEM,
        scratch_shapes=[pltpu.VMEM((rows, bins + 2 * SIDE), jnp.bfloat16)],
        compiler_params=params(),
        cost_estimate=pl.CostEstimate(flops=2 * rows * bins * 512, bytes_accessed=4 * rows * bins, transcendentals=0),
    )(half, spectra, low, high)


def score_kernel(core_ref, processed_ref, *refs):
    pieces, keep_ref, send_ref = refs[:-2], refs[-2], refs[-1]
    blocks, own, peptides = keep_ref.shape
    theory = jnp.concatenate([piece[...] for piece in pieces], axis=0)
    scores = lax.dot_general(
        processed_ref[...], theory, (((1,), (1,)), ((), ())), preferred_element_type=jnp.float32
    )
    scores = scores - jnp.mean(scores, axis=1, keepdims=True)
    halves = scores.reshape(blocks, 2, own, peptides)
    even, odd = halves[:, 0], halves[:, 1]
    first = core_ref[0] == 0
    keep_ref[...] = jnp.where(first, even, odd)
    send_ref[...] = jnp.where(first, odd, even)


def scored(core, processed, pieces, own):
    rows, bins = processed.shape
    peptides = sum(piece.shape[0] for piece in pieces)
    half_rows = jax.ShapeDtypeStruct((rows // own // 2, own, peptides), jnp.float32)
    return pl.pallas_call(
        score_kernel,
        out_shape=(half_rows, half_rows),
        in_specs=[SMEM, VMEM] + [VMEM] * len(pieces),
        out_specs=(VMEM, VMEM),
        compiler_params=params(),
        cost_estimate=pl.CostEstimate(
            flops=2 * rows * bins * peptides, bytes_accessed=2 * (rows + peptides) * bins, transcendentals=0
        ),
    )(core, processed, *pieces)


def pick_kernel(where_ref, parts_ref, cand_ref, out_ref):
    count, own, peptides = parts_ref.shape
    lanes = cand_ref.shape[1]
    per_bucket = lanes // 2
    rounds = peptides // lanes
    scores = jnp.sum(parts_ref[...].astype(jnp.float32), axis=0)
    centred = scores - jnp.mean(scores, axis=1, keepdims=True)
    spread = jnp.mean(jnp.square(centred), axis=1, keepdims=True)
    first = pl.multiple_of(where_ref[0] * own, own)
    ids = cand_ref[pl.ds(first, own), :]
    bucket = where_ref[1]
    block_of = (ids // lanes - bucket // 2) & (rounds - 1)
    lane_of = (ids & (lanes - 1)) ^ ((bucket & 1) * per_bucket)
    picked = jnp.zeros((own, lanes), jnp.float32)
    for block in range(rounds):
        part = centred[:, block * lanes : (block + 1) * lanes]
        value = jnp.take_along_axis(part, lane_of, axis=1)
        picked = jnp.where(block_of == block, value, picked)
    result = (picked * lax.rsqrt(spread + 1e-06)).astype(out_ref.dtype)
    out_ref[...] = jnp.broadcast_to(result[None], out_ref.shape)


def picked_copies(where, parts, cand, count):
    own = parts.shape[1]
    return pl.pallas_call(
        pick_kernel,
        out_shape=jax.ShapeDtypeStruct((count, own, cand.shape[1]), jnp.bfloat16),
        in_specs=[SMEM, VMEM, VMEM],
        out_specs=VMEM,
        compiler_params=params(),
    )(where, parts, cand)


def evidence_kernel(load, where_ref, value_ref, cand_ref, wide_ref, out_ref):
    share = out_ref.shape[0]
    rows, lanes = cand_ref.shape
    values = value_ref[...].astype(jnp.float32).reshape(rows, lanes)
    wide_ref[...] = values
    soft = jax.nn.softplus(values)
    ids = cand_ref[...] - where_ref[0] * share
    for k in range(share):
        kept = jnp.where(ids == k, soft, 0.0)
        out_ref[k : k + 1, :] = jnp.sum(kept, axis=0, keepdims=True) / load


def evidence_of(where, values, cand, share, load):
    return pl.pallas_call(
        functools.partial(evidence_kernel, load),
        out_shape=(
            jax.ShapeDtypeStruct(cand.shape, jnp.float32),
            jax.ShapeDtypeStruct((share, cand.shape[1]), jnp.float32),
        ),
        in_specs=[SMEM, VMEM, VMEM],
        out_specs=(VMEM, VMEM),
        compiler_params=params(),
    )(where, values, cand)


def from_all_buckets(shard):
    count = lax.axis_size("bucket")

    def along_y(value, step):
        return lax.ppermute(value, "bucket", [(b, (b - 2 * step) % count) for b in range(count)])

    def along_x(value):
        return lax.ppermute(value, "bucket", [(b, b ^ 1) for b in range(count)])

    beside = along_x(shard)
    above, below, across = along_y(shard, 1), along_y(shard, 3), along_y(shard, 2)
    across_beside = along_y(beside, 2)
    above_beside, below_beside = along_x(above), along_x(below)
    return [shard, beside, above, above_beside, across, across_beside, below, below_beside]


def on_device(spectra, theory, cand, half):
    row_count, bin_count = spectra.shape
    spec_count = lax.axis_size("spec")
    bucket_count = lax.axis_size("bucket")
    per_bucket = theory.shape[0]
    peptides_all = per_bucket * bucket_count
    spec = lax.axis_index("spec").astype(jnp.int32)
    bucket = lax.axis_index("bucket").astype(jnp.int32)
    where = jnp.stack([spec, bucket])
    core = (spec % 2).reshape(1)

    pieces = from_all_buckets(theory)

    forward = [(i, i + 1) for i in range(spec_count - 1)]
    backward = [(target, source) for source, target in forward]
    low = lax.ppermute(spectra[:, -SIDE:], "spec", forward)
    high = lax.ppermute(spectra[:, :SIDE], "spec", backward)
    processed = windowed(half, spectra, low, high)

    own = row_count // spec_count
    keep, send = scored(core, processed, pieces, own)
    got = lax.ppermute(send, "spec", [(i, i ^ 1) for i in range(spec_count)])
    chip = (keep + got).astype(jnp.bfloat16)
    groups = [list(range(c, spec_count, 2)) for c in range(2)]
    parts = lax.all_to_all(chip, "spec", 0, 0, axis_index_groups=groups, tiled=True)
    copies = picked_copies(where, parts, cand, spec_count)
    values = lax.all_to_all(copies, "spec", 0, 0, tiled=True)

    share = peptides_all // spec_count
    mean_load = cand.shape[1] * row_count / per_bucket
    cand_scores, evidence = evidence_of(where, values, cand, share, mean_load)
    evidence = lax.all_to_all(
        evidence.reshape(bucket_count, share // bucket_count, cand.shape[1]), "bucket", 0, 0, tiled=True
    )
    return (cand_scores, jnp.sum(evidence, axis=(0, 2)))


def solution(mesh):
    return jax.shard_map(
        on_device,
        mesh=mesh,
        in_specs=(P("bucket", "spec"), P("bucket", "spec"), P("bucket", None), P("spec")),
        out_specs=(P("bucket", None), P(("spec", "bucket"))),
        check_vma=False,
    )
```

time: 87.8 us -> 89.1 us (1.015)
  waiting for transfers between devices: 31.9 us -> 12.6 us
  starting transfers between devices: 20.9 us -> 39 us
  blocking collectives: 24.5 us -> 28.8 us
  local copies, waits for them, and re-layouts: 5.33 us -> 2.12 us
    ppermute x2 -> x10, starting transfers between devices: 4.33 us -> 27.2 us  [the longest x4 16.3 us: along_y(): lax.ppermute(value, 'bucket', [(b, (b - 2 * step) % count) for b in range...]
    all_to_all x2 -> x1, waiting for transfers between devices: 31 us -> 8.67 us  [on_device(): lax.all_to_all(chip, 'spec', 0, 0, axis_index_groups=groups, tiled=True)]
    all_to_all x1, blocking collectives: 11.1 us -> 16.2 us  [on_device(): lax.all_to_all(evidence.reshape(bucket_count, share // bucket_count, cand...]
    all_to_all x2 -> x1, starting transfers between devices: 16.6 us -> 11.8 us  [on_device(): lax.all_to_all(chip, 'spec', 0, 0, axis_index_groups=groups, tiled=True)]
    ppermute x2 -> x10, waiting for transfers between devices: 0.87 us -> 3.88 us  [the longest x1 1.85 us: on_device(): high = lax.ppermute(spectra[:, :SIDE], 'spec', backward)]
    broadcast_in_dim x1 -> x0, local copies, waits for them, and re-layouts: 2.55 us -> none  [on_device(): copies = jnp.broadcast_to(theory[None], (bucket_count,) + theory.shape)]
    unnamed x7 -> x8, local copies, waits for them, and re-layouts: 1.89 us -> 1.24 us
  transfers between devices with their start and end apart: 4 -> 11, of which waited for: 3 -> 4; matrix products, arithmetic and copies ran while one was open for 1% -> 1% of each run, Pallas kernels for 1% -> 1%
where the time goes in v3:
time: 89.1 us; the launch traced here: 88.7 us
  starting transfers between devices  39 us (44%)
  blocking collectives  28.8 us (32%)
  waiting for transfers between devices  12.6 us (14%)
  Pallas kernels  4.13 us (5%)
  local copies, waits for them, and re-layouts  2.12 us (2%)
  other arithmetic  1.4 us (2%)
    ppermute x4, starting transfers between devices, along_y(): lax.ppermute(value, 'bucket', [(b, (b - 2 * step) % count) for b in range...  16.3 us
    all_to_all x1, blocking collectives, on_device(): lax.all_to_all(evidence.reshape(bucket_count, share // bucket_count, cand...  16.2 us
    all_to_all x1, blocking collectives, on_device(): values = lax.all_to_all(copies, 'spec', 0, 0, tiled=True)  12.5 us
    all_to_all x1, starting transfers between devices, on_device(): lax.all_to_all(chip, 'spec', 0, 0, axis_index_groups=groups, tiled=True)  11.8 us
    all_to_all x1, waiting for transfers between devices, on_device(): lax.all_to_all(chip, 'spec', 0, 0, axis_index_groups=groups, tiled=True)  8.67 us
    ppermute x1, starting transfers between devices, on_device(): low = lax.ppermute(spectra[:, -SIDE:], 'spec', forward)  4.93 us
    ppermute x3, starting transfers between devices, along_x(): return lax.ppermute(value, 'bucket', [(b, b ^ 1) for b in range(count)])  4.14 us
    ppermute x1, waiting for transfers between devices, on_device(): high = lax.ppermute(spectra[:, :SIDE], 'spec', backward)  1.85 us
  transfers between devices with their start and end apart: 11, of which 4 were waited for; matrix products, arithmetic and copies ran while one was open for 1% of the time, Pallas kernels for 1%

profile of v3, /device:TPU:8, one launch (start us, length us, event | category | flops | bytes accessed | tf_op | source)
XLA Modules:
  0.0 88.7 jit_solution(10599702615441190825)
XLA Ops:
  0.6 2.3 %collective-permute-start.3 = (bf16[64,2048]{1,0:T(8,128)(2,1)}, bf16[64,2048]{1,0:T(8,128)(2,1)S(1)}, u32[]{:S(2)}, u32[]{:S(2)}) collective-permute-start(bf16[64,2048]{1,0:T(8,128)(2,1)} %refs_0_.1), channel_id=1, source_target_pairs={{0,6},{1,7},{2,0},{3,1},{4,2},{5,3},{6,4},{7,5},{8,14},{9,15},{10,... | collective-permute-start | bytes 786440 | tf_op jit(solution)/shard_map/ppermute | solution.py:148
  2.9 1.3 %collective-permute-start.2 = (bf16[64,2048]{1,0:T(8,128)(2,1)}, bf16[64,2048]{1,0:T(8,128)(2,1)S(1)}, u32[]{:S(2)}, u32[]{:S(2)}) collective-permute-start(bf16[64,2048]{1,0:T(8,128)(2,1)} %refs_0_.1), channel_id=1, source_target_pairs={{0,1},{1,0},{2,3},{3,2},{4,5},{5,4},{6,7},{7,6},{8,9},{9,8},{10,11... | collective-permute-start | bytes 786440 | tf_op jit(solution)/shard_map/ppermute | solution.py:151
  4.2 1.6 %collective-permute-start.7 = (bf16[64,2048]{1,0:T(8,128)(2,1)}, bf16[64,2048]{1,0:T(8,128)(2,1)S(1)}, u32[]{:S(2)}, u32[]{:S(2)}) collective-permute-start(bf16[64,2048]{1,0:T(8,128)(2,1)} %refs_0_.1), channel_id=1, source_target_pairs={{0,2},{1,3},{2,4},{3,5},{4,6},{5,7},{6,0},{7,1},{8,10},{9,11},{10,... | collective-permute-start | bytes 786440 | tf_op jit(solution)/shard_map/ppermute | solution.py:148
  5.8 3.5 %collective-permute-start.5 = (bf16[64,2048]{1,0:T(8,128)(2,1)}, bf16[64,2048]{1,0:T(8,128)(2,1)S(1)}, u32[]{:S(2)}, u32[]{:S(2)}) collective-permute-start(bf16[64,2048]{1,0:T(8,128)(2,1)} %refs_0_.1), channel_id=1, source_target_pairs={{0,4},{1,5},{2,6},{3,7},{4,0},{5,1},{6,2},{7,3},{8,12},{9,13},{10,... | collective-permute-start | bytes 786440 | tf_op jit(solution)/shard_map/ppermute | solution.py:148
  9.3 0.0 collective-permute-done.3.refs_2_
  9.3 2.9 %collective-permute-start.4 = (bf16[64,2048]{1,0:T(8,128)(2,1)S(1)}, bf16[64,2048]{1,0:T(8,128)(2,1)S(1)}, u32[]{:S(2)}, u32[]{:S(2)}) collective-permute-start(bf16[64,2048]{1,0:T(8,128)(2,1)S(1)} %collective-permute-done.3.refs_2_), channel_id=1, source_target_pairs={{0,1},{1,0},{2,3},{3,2},{4,5},{5,4},{6,7},{7,6},{8,9},{9,8},{10,11... | collective-permute-start | bytes 786440 | tf_op jit(solution)/shard_map/ppermute | solution.py:151
  12.1 0.0 collective-permute-done.2.refs_1_
  12.1 9.0 %collective-permute-start.6 = (bf16[64,2048]{1,0:T(8,128)(2,1)S(1)}, bf16[64,2048]{1,0:T(8,128)(2,1)S(1)}, u32[]{:S(2)}, u32[]{:S(2)}) collective-permute-start(bf16[64,2048]{1,0:T(8,128)(2,1)S(1)} %collective-permute-done.2.refs_1_), channel_id=1, source_target_pairs={{0,4},{1,5},{2,6},{3,7},{4,0},{5,1},{6,2},{7,3},{8,12},{9,13},{10,... | collective-permute-start | bytes 786440 | tf_op jit(solution)/shard_map/ppermute | solution.py:148
  21.1 0.0 collective-permute-done.7.refs_6_
  21.1 0.0 collective-permute-start.8
  21.1 0.9 fusion
  22.0 1.3 %collective-permute-start.1 = (bf16[256,128]{1,0:T(8,128)(2,1)S(1)}, bf16[256,128]{1,0:T(8,128)(2,1)S(1)}, u32[]{:S(2)}, u32[]{:S(2)}) collective-permute-start(bf16[256,128]{1,0:T(8,128)(2,1)S(1)} %get-tuple-element.10), channel_id=1, source_target_pairs={{8,0},{16,8},{24,16},{32,24},{40,32},{48,40},{56,48},{64,56},{72,6... | collective-permute-start | bytes 196616 | tf_op jit(solution)/shard_map/ppermute | solution.py:176
  23.3 1.8 %collective-permute-done.1.high_ref = bf16[256,128]{1,0:T(8,128)(2,1)S(1)} collective-permute-done((bf16[256,128]{1,0:T(8,128)(2,1)S(1)}, bf16[256,128]{1,0:T(8,128)(2,1)S(1)}, u32[]{:S(2)}, u32[]{:S(2)}) %collective-permute-start.1) | collective-permute-done | bytes 65568 | tf_op jit(solution)/shard_map/ppermute | solution.py:176
  25.2 4.9 %collective-permute-start = (bf16[256,128]{1,0:T(8,128)(2,1)S(1)}, bf16[256,128]{1,0:T(8,128)(2,1)S(1)}, u32[]{:S(2)}, u32[]{:S(2)}) collective-permute-start(bf16[256,128]{1,0:T(8,128)(2,1)S(1)} %get-tuple-element.11), channel_id=1, source_target_pairs={{0,8},{8,16},{16,24},{24,32},{32,40},{40,48},{48,56},{56,64},{64,7... | collective-permute-start | bytes 196616 | tf_op jit(solution)/shard_map/ppermute | solution.py:175
  30.1 0.0 copy-start.3
  30.1 0.9 collective-permute-done.low_ref
  31.0 0.0 copy-done.3
  31.0 0.0 copy-start
  31.0 1.2 %copy-done = bf16[256,2048]{1,0:T(8,128)(2,1)S(1)} copy-done((bf16[256,2048]{1,0:T(8,128)(2,1)S(1)}, bf16[256,2048]{1,0:T(8,128)(2,1)}, u32[]{:S(2)}) %copy-start) | copy-done | bytes 1048600
  32.2 0.0 copy-start.2
  32.2 1.3 %shard_map.59.processed_ref = bf16[256,2048]{1,0:T(8,128)(2,1)S(1)} custom-call(s32[4]{0:T(128)S(1)} %copy-done.3, bf16[256,2048]{1,0:T(8,128)(2,1)S(1)} %copy-done, bf16[256,128]{1,0:T(8,128)(2,1)S(1)} %collective-permute-done.low_ref, bf16[256,128]{1,0:T(8,128)(2,1)S(1)} %collective-permute-done.1.high_ref), custom_call_target="tpu_custom_call" | custom-call | flops 536870912 | bytes 2097152 | tf_op jit(solution)/shard_map/pallas_call | solution.py:44
  33.5 0.0 collective-permute-done.5.refs_4_
  33.5 0.0 collective-permute-done.4.refs_3_
  33.5 0.0 collective-permute-done.6.refs_5_
  33.5 0.0 collective-permute-done.8.refs_7_
  33.5 0.0 copy-done.2
  33.6 0.8 shard_map.60
  34.4 0.5 collective-permute-start.9
  34.9 1.2 %collective-permute-done.9 = f32[16,8,512]{2,1,0:T(8,128)S(1)} collective-permute-done((f32[16,8,512]{2,1,0:T(8,128)S(1)}, f32[16,8,512]{2,1,0:T(8,128)S(1)}, u32[]{:S(2)}, u32[]{:S(2)}) %collective-permute-start.9) | collective-permute-done | bytes 262176 | tf_op jit(solution)/shard_map/ppermute | solution.py:181
  36.1 0.7 add_convert_fusion
  36.8 0.0 copy-start.1
  36.8 11.8 %all-to-all-start = ((bf16[16,8,512]{2,1,0:T(8,128)(2,1)}), bf16[16,8,512]{2,1,0:T(8,128)(2,1)S(1)}, u32[]{:S(2)}, u32[]{:S(2)}) async-start(bf16[16,8,512]{2,1,0:T(8,128)(2,1)} %add_convert_fusion), calls=%async_computation | async-start | bytes 262144 | tf_op jit(solution)/shard_map/all_to_all | solution.py:184
  48.5 0.1 pad_add_fusion.where_ref
  48.6 8.7 %all-to-all-done.parts_ref = bf16[16,8,512]{2,1,0:T(8,128)(2,1)S(1)} async-done(((bf16[16,8,512]{2,1,0:T(8,128)(2,1)}), bf16[16,8,512]{2,1,0:T(8,128)(2,1)S(1)}, u32[]{:S(2)}, u32[]{:S(2)}) %all-to-all-start) | async-done | bytes 131104 | tf_op jit(solution)/shard_map/all_to_all | solution.py:184
  57.3 0.0 copy-done.1
  57.3 0.7 shard_map.61
  58.0 12.5 %all_to_all.15.value_ref = bf16[32,8,128]{2,1,0:T(8,128)(2,1)S(1)} all-to-all(bf16[32,8,128]{2,1,0:T(8,128)(2,1)S(1)} %shard_map.61), channel_id=1, replica_groups=mesh['spec'=32,'bucket'=8] {'spec'}, dimensions={0} | all-to-all | bytes 131072 | tf_op jit(solution)/shard_map/all_to_all | solution.py:186
  70.6 1.3 %shard_map.62 = (f32[256,128]{1,0:T(8,128)}, f32[16,128]{1,0:T(8,128)S(1)}) custom-call(s32[2]{0:T(128)S(1)} %pad_add_fusion.where_ref, bf16[32,8,128]{2,1,0:T(8,128)(2,1)S(1)} %all_to_all.15.value_ref, s32[256,128]{1,0:T(8,128)S(1)} %copy-done.1), custom_call_target="tpu_custom_call" | custom-call | tf_op jit(solution)/shard_map/pallas_call | solution.py:132
  71.8 16.2 %all_to_all.16 = f32[8,2,128]{2,1,0:T(2,128)S(1)} all-to-all(f32[8,2,128]{2,1,0:T(2,128)S(1)} %bitcast.4), channel_id=1, replica_groups=mesh['spec'=32,'bucket'=8] {'bucket'}, dimensions={0} | all-to-all | bytes 16384 | tf_op jit(solution)/shard_map/all_to_all | solution.py:191
  88.1 0.6 reduce_sum.9
Async XLA Ops:
  0.6 8.6 %collective-permute-start.3 = (bf16[64,2048]{1,0:T(8,128)(2,1)}, bf16[64,2048]{1,0:T(8,128)(2,1)S(1)}, u32[]{:S(2)}, u32[]{:S(2)}) collective-permute-start(bf16[64,2048]{1,0:T(8,128)(2,1)} %refs_0_.1), channel_id=1, source_target_pairs={{0,6},{1,7},{2,0},{3,1},{4,2},{5,3},{6,4},{7,5},{8,14},{9,15},{10,... | collective-permute-start | bytes 786440 | tf_op jit(solution)/shard_map/ppermute | solution.py:148
  2.9 9.2 %collective-permute-start.2 = (bf16[64,2048]{1,0:T(8,128)(2,1)}, bf16[64,2048]{1,0:T(8,128)(2,1)S(1)}, u32[]{:S(2)}, u32[]{:S(2)}) collective-permute-start(bf16[64,2048]{1,0:T(8,128)(2,1)} %refs_0_.1), channel_id=1, source_target_pairs={{0,1},{1,0},{2,3},{3,2},{4,5},{5,4},{6,7},{7,6},{8,9},{9,8},{10,11... | collective-permute-start | bytes 786440 | tf_op jit(solution)/shard_map/ppermute | solution.py:151
  4.2 16.9 %collective-permute-start.7 = (bf16[64,2048]{1,0:T(8,128)(2,1)}, bf16[64,2048]{1,0:T(8,128)(2,1)S(1)}, u32[]{:S(2)}, u32[]{:S(2)}) collective-permute-start(bf16[64,2048]{1,0:T(8,128)(2,1)} %refs_0_.1), channel_id=1, source_target_pairs={{0,2},{1,3},{2,4},{3,5},{4,6},{5,7},{6,0},{7,1},{8,10},{9,11},{10,... | collective-permute-start | bytes 786440 | tf_op jit(solution)/shard_map/ppermute | solution.py:148
  5.8 27.8 %collective-permute-start.5 = (bf16[64,2048]{1,0:T(8,128)(2,1)}, bf16[64,2048]{1,0:T(8,128)(2,1)S(1)}, u32[]{:S(2)}, u32[]{:S(2)}) collective-permute-start(bf16[64,2048]{1,0:T(8,128)(2,1)} %refs_0_.1), channel_id=1, source_target_pairs={{0,4},{1,5},{2,6},{3,7},{4,0},{5,1},{6,2},{7,3},{8,12},{9,13},{10,... | collective-permute-start | bytes 786440 | tf_op jit(solution)/shard_map/ppermute | solution.py:148
  9.3 24.3 %collective-permute-start.4 = (bf16[64,2048]{1,0:T(8,128)(2,1)S(1)}, bf16[64,2048]{1,0:T(8,128)(2,1)S(1)}, u32[]{:S(2)}, u32[]{:S(2)}) collective-permute-start(bf16[64,2048]{1,0:T(8,128)(2,1)S(1)} %collective-permute-done.3.refs_2_), channel_id=1, source_target_pairs={{0,1},{1,0},{2,3},{3,2},{4,5},{5,4},{6,7},{7,6},{8,9},{9,8},{10,11... | collective-permute-start | bytes 786440 | tf_op jit(solution)/shard_map/ppermute | solution.py:151
  12.1 21.4 %collective-permute-start.6 = (bf16[64,2048]{1,0:T(8,128)(2,1)S(1)}, bf16[64,2048]{1,0:T(8,128)(2,1)S(1)}, u32[]{:S(2)}, u32[]{:S(2)}) collective-permute-start(bf16[64,2048]{1,0:T(8,128)(2,1)S(1)} %collective-permute-done.2.refs_1_), channel_id=1, source_target_pairs={{0,4},{1,5},{2,6},{3,7},{4,0},{5,1},{6,2},{7,3},{8,12},{9,13},{10,... | collective-permute-start | bytes 786440 | tf_op jit(solution)/shard_map/ppermute | solution.py:148
  21.1 12.4 %collective-permute-start.8 = (bf16[64,2048]{1,0:T(8,128)(2,1)S(1)}, bf16[64,2048]{1,0:T(8,128)(2,1)S(1)}, u32[]{:S(2)}, u32[]{:S(2)}) collective-permute-start(bf16[64,2048]{1,0:T(8,128)(2,1)S(1)} %collective-permute-done.7.refs_6_), channel_id=1, source_target_pairs={{0,1},{1,0},{2,3},{3,2},{4,5},{5,4},{6,7},{7,6},{8,9},{9,8},{10,11... | collective-permute-start | bytes 786440 | tf_op jit(solution)/shard_map/ppermute | solution.py:151
  22.0 3.1 %collective-permute-start.1 = (bf16[256,128]{1,0:T(8,128)(2,1)S(1)}, bf16[256,128]{1,0:T(8,128)(2,1)S(1)}, u32[]{:S(2)}, u32[]{:S(2)}) collective-permute-start(bf16[256,128]{1,0:T(8,128)(2,1)S(1)} %get-tuple-element.10), channel_id=1, source_target_pairs={{8,0},{16,8},{24,16},{32,24},{40,32},{48,40},{56,48},{64,56},{72,6... | collective-permute-start | bytes 196616 | tf_op jit(solution)/shard_map/ppermute | solution.py:176
  25.2 5.8 %collective-permute-start = (bf16[256,128]{1,0:T(8,128)(2,1)S(1)}, bf16[256,128]{1,0:T(8,128)(2,1)S(1)}, u32[]{:S(2)}, u32[]{:S(2)}) collective-permute-start(bf16[256,128]{1,0:T(8,128)(2,1)S(1)} %get-tuple-element.11), channel_id=1, source_target_pairs={{0,8},{8,16},{16,24},{24,32},{32,40},{40,48},{48,56},{56,64},{64,7... | collective-permute-start | bytes 196616 | tf_op jit(solution)/shard_map/ppermute | solution.py:175
  30.1 0.9 copy-start.3
  31.0 1.2 %copy-start = (bf16[256,2048]{1,0:T(8,128)(2,1)S(1)}, bf16[256,2048]{1,0:T(8,128)(2,1)}, u32[]{:S(2)}) copy-start(bf16[256,2048]{1,0:T(8,128)(2,1)} %spectra_ref.1) | copy-start | bytes 3145732
  32.2 1.4 %copy-start.2 = (bf16[64,2048]{1,0:T(8,128)(2,1)S(1)}, bf16[64,2048]{1,0:T(8,128)(2,1)}, u32[]{:S(2)}) copy-start(bf16[64,2048]{1,0:T(8,128)(2,1)} %refs_0_.1) | copy-start | bytes 786436
  34.4 1.7 %collective-permute-start.9 = (f32[16,8,512]{2,1,0:T(8,128)S(1)}, f32[16,8,512]{2,1,0:T(8,128)S(1)}, u32[]{:S(2)}, u32[]{:S(2)}) collective-permute-start(f32[16,8,512]{2,1,0:T(8,128)S(1)} %get-tuple-element.7), channel_id=1, source_target_pairs={{0,8},{8,0},{16,24},{24,16},{32,40},{40,32},{48,56},{56,48},{64,72... | collective-permute-start | bytes 786440 | tf_op jit(solution)/shard_map/ppermute | solution.py:181
  36.8 20.5 %copy-start.1 = (s32[256,128]{1,0:T(8,128)S(1)}, s32[256,128]{1,0:T(8,128)}, u32[]{:S(2)}) copy-start(s32[256,128]{1,0:T(8,128)} %cand_ref.3) | copy-start | bytes 393220
  36.8 20.5 %all-to-all-start = ((bf16[16,8,512]{2,1,0:T(8,128)(2,1)}), bf16[16,8,512]{2,1,0:T(8,128)(2,1)S(1)}, u32[]{:S(2)}, u32[]{:S(2)}) async-start(bf16[16,8,512]{2,1,0:T(8,128)(2,1)} %add_convert_fusion), calls=%async_computation | async-start | bytes 262144 | tf_op jit(solution)/shard_map/all_to_all | solution.py:184

commit v4 on v3

--- a/solution.py
+++ b/solution.py
@@ -52,12 +52,10 @@
     )(half, spectra, low, high)
 
 
-def score_kernel(core_ref, processed_ref, *refs):
-    pieces, keep_ref, send_ref = refs[:-2], refs[-2], refs[-1]
+def score_kernel(core_ref, processed_ref, theory_ref, keep_ref, send_ref):
     blocks, own, peptides = keep_ref.shape
-    theory = jnp.concatenate([piece[...] for piece in pieces], axis=0)
     scores = lax.dot_general(
-        processed_ref[...], theory, (((1,), (1,)), ((), ())), preferred_element_type=jnp.float32
+        processed_ref[...], theory_ref[...], (((1,), (1,)), ((), ())), preferred_element_type=jnp.float32
     )
     scores = scores - jnp.mean(scores, axis=1, keepdims=True)
     halves = scores.reshape(blocks, 2, own, peptides)
@@ -67,37 +65,34 @@
     send_ref[...] = jnp.where(first, odd, even)
 
 
-def scored(core, processed, pieces, own):
+def scored(core, processed, gathered, own):
     rows, bins = processed.shape
-    peptides = sum(piece.shape[0] for piece in pieces)
+    peptides = gathered.shape[0]
     half_rows = jax.ShapeDtypeStruct((rows // own // 2, own, peptides), jnp.float32)
     return pl.pallas_call(
         score_kernel,
         out_shape=(half_rows, half_rows),
-        in_specs=[SMEM, VMEM] + [VMEM] * len(pieces),
+        in_specs=[SMEM, VMEM, VMEM],
         out_specs=(VMEM, VMEM),
         compiler_params=params(),
         cost_estimate=pl.CostEstimate(
             flops=2 * rows * bins * peptides, bytes_accessed=2 * (rows + peptides) * bins, transcendentals=0
         ),
-    )(core, processed, *pieces)
+    )(core, processed, gathered)
 
 
 def pick_kernel(where_ref, parts_ref, cand_ref, out_ref):
     count, own, peptides = parts_ref.shape
     lanes = cand_ref.shape[1]
-    per_bucket = lanes // 2
-    rounds = peptides // lanes
     scores = jnp.sum(parts_ref[...].astype(jnp.float32), axis=0)
     centred = scores - jnp.mean(scores, axis=1, keepdims=True)
     spread = jnp.mean(jnp.square(centred), axis=1, keepdims=True)
     first = pl.multiple_of(where_ref[0] * own, own)
     ids = cand_ref[pl.ds(first, own), :]
-    bucket = where_ref[1]
-    block_of = (ids // lanes - bucket // 2) & (rounds - 1)
-    lane_of = (ids & (lanes - 1)) ^ ((bucket & 1) * per_bucket)
+    block_of = ids // lanes
+    lane_of = ids & (lanes - 1)
     picked = jnp.zeros((own, lanes), jnp.float32)
-    for block in range(rounds):
+    for block in range(peptides // lanes):
         part = centred[:, block * lanes : (block + 1) * lanes]
         value = jnp.take_along_axis(part, lane_of, axis=1)
         picked = jnp.where(block_of == block, value, picked)
@@ -116,11 +111,10 @@
     )(where, parts, cand)
 
 
-def evidence_kernel(load, where_ref, value_ref, cand_ref, wide_ref, out_ref):
+def evidence_kernel(load, where_ref, value_ref, cand_ref, out_ref):
     share = out_ref.shape[0]
     rows, lanes = cand_ref.shape
     values = value_ref[...].astype(jnp.float32).reshape(rows, lanes)
-    wide_ref[...] = values
     soft = jax.nn.softplus(values)
     ids = cand_ref[...] - where_ref[0] * share
     for k in range(share):
@@ -131,30 +125,11 @@
 def evidence_of(where, values, cand, share, load):
     return pl.pallas_call(
         functools.partial(evidence_kernel, load),
-        out_shape=(
-            jax.ShapeDtypeStruct(cand.shape, jnp.float32),
-            jax.ShapeDtypeStruct((share, cand.shape[1]), jnp.float32),
-        ),
+        out_shape=jax.ShapeDtypeStruct((share, cand.shape[1]), jnp.float32),
         in_specs=[SMEM, VMEM, VMEM],
-        out_specs=(VMEM, VMEM),
+        out_specs=VMEM,
         compiler_params=params(),
     )(where, values, cand)
-
-
-def from_all_buckets(shard):
-    count = lax.axis_size("bucket")
-
-    def along_y(value, step):
-        return lax.ppermute(value, "bucket", [(b, (b - 2 * step) % count) for b in range(count)])
-
-    def along_x(value):
-        return lax.ppermute(value, "bucket", [(b, b ^ 1) for b in range(count)])
-
-    beside = along_x(shard)
-    above, below, across = along_y(shard, 1), along_y(shard, 3), along_y(shard, 2)
-    across_beside = along_y(beside, 2)
-    above_beside, below_beside = along_x(above), along_x(below)
-    return [shard, beside, above, above_beside, across, across_beside, below, below_beside]
 
 
 def on_device(spectra, theory, cand, half):
@@ -164,20 +139,21 @@
     per_bucket = theory.shape[0]
     peptides_all = per_bucket * bucket_count
     spec = lax.axis_index("spec").astype(jnp.int32)
-    bucket = lax.axis_index("bucket").astype(jnp.int32)
-    where = jnp.stack([spec, bucket])
+    where = spec.reshape(1)
     core = (spec % 2).reshape(1)
 
-    pieces = from_all_buckets(theory)
+    copies = jnp.broadcast_to(theory[None], (bucket_count,) + theory.shape)
+    copies, observed = lax.optimization_barrier((copies, spectra))
+    gathered = lax.all_to_all(copies, "bucket", 0, 0, tiled=True).reshape(peptides_all, bin_count)
 
     forward = [(i, i + 1) for i in range(spec_count - 1)]
     backward = [(target, source) for source, target in forward]
-    low = lax.ppermute(spectra[:, -SIDE:], "spec", forward)
-    high = lax.ppermute(spectra[:, :SIDE], "spec", backward)
+    low = lax.ppermute(observed[:, -SIDE:], "spec", forward)
+    high = lax.ppermute(observed[:, :SIDE], "spec", backward)
     processed = windowed(half, spectra, low, high)
 
     own = row_count // spec_count
-    keep, send = scored(core, processed, pieces, own)
+    keep, send = scored(core, processed, gathered, own)
     got = lax.ppermute(send, "spec", [(i, i ^ 1) for i in range(spec_count)])
     chip = (keep + got).astype(jnp.bfloat16)
     groups = [list(range(c, spec_count, 2)) for c in range(2)]
@@ -187,7 +163,8 @@
 
     share = peptides_all // spec_count
     mean_load = cand.shape[1] * row_count / per_bucket
-    cand_scores, evidence = evidence_of(where, values, cand, share, mean_load)
+    evidence = evidence_of(where, values, cand, share, mean_load)
+    cand_scores = values.astype(jnp.float32).reshape(row_count, cand.shape[1])
     evidence = lax.all_to_all(
         evidence.reshape(bucket_count, share // bucket_count, cand.shape[1]), "bucket", 0, 0, tiled=True
     )

time: 89.1 us -> 83.1 us (0.933)
  starting transfers between devices: 39 us -> 17 us
  waiting for transfers between devices: 12.6 us -> 25.8 us
  local copies, waits for them, and re-layouts: 2.12 us -> 4.66 us
  blocking collectives: 28.8 us -> 29.9 us
  Pallas kernels: 4.13 us -> 3.2 us
    ppermute x9 -> x2, starting transfers between devices: 26.7 us -> 4.33 us  [the longest x1 3.03 us: on_device(): low = lax.ppermute(observed[:, -SIDE:], 'spec', forward)]
    all_to_all x1 -> x2, waiting for transfers between devices: 8.67 us -> 23.4 us  [the longest x1 17.9 us: on_device(): lax.all_to_all(copies, 'bucket', 0, 0, tiled=True)]
    broadcast_in_dim x0 -> x1, local copies, waits for them, and re-layouts: none -> 2.54 us  [on_device(): copies = jnp.broadcast_to(theory[None], (bucket_count,) + theory.shape)]
    ppermute x9 -> x2, waiting for transfers between devices: 2.72 us -> 0.86 us  [the longest x1 0.86 us: on_device(): low = lax.ppermute(observed[:, -SIDE:], 'spec', forward)]
    all_to_all x1, blocking collectives: 16.2 us -> 17.4 us  [on_device(): lax.all_to_all(chip, 'spec', 0, 0, axis_index_groups=groups, tiled=True)]
    all_to_all x1 -> x2, starting transfers between devices: 11.8 us -> 12.6 us  [the longest x1 7.51 us: on_device(): lax.all_to_all(copies, 'bucket', 0, 0, tiled=True)]
  transfers between devices with their start and end apart: 11 -> 5, of which waited for: 4 -> 4; matrix products, arithmetic and copies ran while one was open for 1% -> 2% of each run, Pallas kernels for 1% -> 2%
where the time goes in v4:
time: 83.1 us; the launch traced here: 82.6 us
  blocking collectives  29.9 us (36%)
  waiting for transfers between devices  25.8 us (31%)
  starting transfers between devices  17 us (20%)
  local copies, waits for them, and re-layouts  4.66 us (6%)
  Pallas kernels  3.2 us (4%)
  other arithmetic  1.34 us (2%)
    all_to_all x1, waiting for transfers between devices, on_device(): lax.all_to_all(copies, 'bucket', 0, 0, tiled=True)  17.9 us
    all_to_all x1, blocking collectives, on_device(): lax.all_to_all(chip, 'spec', 0, 0, axis_index_groups=groups, tiled=True)  17.4 us
    all_to_all x1, blocking collectives, on_device(): values = lax.all_to_all(copies, 'spec', 0, 0, tiled=True)  12.5 us
    all_to_all x1, starting transfers between devices, on_device(): lax.all_to_all(copies, 'bucket', 0, 0, tiled=True)  7.51 us
    all_to_all x1, waiting for transfers between devices, on_device(): lax.all_to_all(evidence.reshape(bucket_count, share // bucket_count, cand...  5.57 us
    all_to_all x1, starting transfers between devices, on_device(): lax.all_to_all(evidence.reshape(bucket_count, share // bucket_count, cand...  5.06 us
    ppermute x1, starting transfers between devices, on_device(): low = lax.ppermute(observed[:, -SIDE:], 'spec', forward)  3.03 us
    broadcast_in_dim x1, local copies, waits for them, and re-layouts, on_device(): copies = jnp.broadcast_to(theory[None], (bucket_count,) + theory.shape)  2.54 us
  transfers between devices with their start and end apart: 5, of which 4 were waited for; matrix products, arithmetic and copies ran while one was open for 2% of the time, Pallas kernels for 2%

profile of v4, /device:TPU:8, one launch (start us, length us, event | category | flops | bytes accessed | tf_op | source)
XLA Modules:
  0.0 82.6 jit_solution(17801544071442571521)
XLA Ops:
  0.6 2.5 %broadcast_in_dim.2 = bf16[8,64,2048]{2,1,0:T(8,128)(2,1)} broadcast(bf16[64,2048]{1,0:T(8,128)(2,1)} %param.5), dimensions={1,2} | broadcast | bytes 2359296 | tf_op jit(solution)/shard_map/broadcast_in_dim | solution.py:145
  3.2 0.0 copy-start.2
  3.2 7.5 %all-to-all-start = ((bf16[8,64,2048]{2,1,0:T(8,128)(2,1)}), bf16[8,64,2048]{2,1,0:T(8,128)(2,1)S(1)}, u32[]{:S(2)}, u32[]{:S(2)}) async-start(bf16[8,64,2048]{2,1,0:T(8,128)(2,1)} %broadcast_in_dim.2), calls=%async_computation | async-start | bytes 4194304 | tf_op jit(solution)/shard_map/all_to_all | solution.py:147
  10.7 0.9 %fusion = (bf16[256,128]{1,0:T(8,128)(2,1)S(1)}, bf16[256,128]{1,0:T(8,128)(2,1)S(1)}) fusion(bf16[256,2048]{1,0:T(8,128)(2,1)} %spectra_ref.1), kind=kLoop, calls=%fused_computation.2 | loop fusion | bytes 262144 | tf_op jit(solution)/shard_map/slice | solution.py:152
  11.6 1.3 %collective-permute-start.1 = (bf16[256,128]{1,0:T(8,128)(2,1)S(1)}, bf16[256,128]{1,0:T(8,128)(2,1)S(1)}, u32[]{:S(2)}, u32[]{:S(2)}) collective-permute-start(bf16[256,128]{1,0:T(8,128)(2,1)S(1)} %get-tuple-element.10), channel_id=1, source_target_pairs={{8,0},{16,8},{24,16},{32,24},{40,32},{48,40},{56,48},{64,56},{72,6... | collective-permute-start | bytes 196616 | tf_op jit(solution)/shard_map/ppermute | solution.py:152
  12.9 3.0 %collective-permute-start = (bf16[256,128]{1,0:T(8,128)(2,1)S(1)}, bf16[256,128]{1,0:T(8,128)(2,1)S(1)}, u32[]{:S(2)}, u32[]{:S(2)}) collective-permute-start(bf16[256,128]{1,0:T(8,128)(2,1)S(1)} %get-tuple-element.11), channel_id=1, source_target_pairs={{0,8},{8,16},{16,24},{24,32},{32,40},{40,48},{48,56},{56,64},{64,7... | collective-permute-start | bytes 196616 | tf_op jit(solution)/shard_map/ppermute | solution.py:151
  15.9 0.0 collective-permute-done.1.high_ref
  15.9 0.9 %collective-permute-done.low_ref = bf16[256,128]{1,0:T(8,128)(2,1)S(1)} collective-permute-done((bf16[256,128]{1,0:T(8,128)(2,1)S(1)}, bf16[256,128]{1,0:T(8,128)(2,1)S(1)}, u32[]{:S(2)}, u32[]{:S(2)}) %collective-permute-start) | collective-permute-done | bytes 65568 | tf_op jit(solution)/shard_map/ppermute | solution.py:151
  16.8 0.0 copy-done.2
  16.8 0.0 copy-start
  16.8 1.2 %copy-done = bf16[256,2048]{1,0:T(8,128)(2,1)S(1)} copy-done((bf16[256,2048]{1,0:T(8,128)(2,1)S(1)}, bf16[256,2048]{1,0:T(8,128)(2,1)}, u32[]{:S(2)}) %copy-start) | copy-done | bytes 1048600
  18.0 1.3 %shard_map.59.processed_ref = bf16[256,2048]{1,0:T(8,128)(2,1)S(1)} custom-call(s32[4]{0:T(128)S(1)} %copy-done.2, bf16[256,2048]{1,0:T(8,128)(2,1)S(1)} %copy-done, bf16[256,128]{1,0:T(8,128)(2,1)S(1)} %collective-permute-done.low_ref, bf16[256,128]{1,0:T(8,128)(2,1)S(1)} %collective-permute-done.1.high_ref), custom_call_target="tpu_custom_call" | custom-call | flops 536870912 | bytes 2097152 | tf_op jit(solution)/shard_map/pallas_call | solution.py:44
  19.3 0.0 copy-start.1
  19.3 17.9 %all-to-all-done = bf16[8,64,2048]{2,1,0:T(8,128)(2,1)S(1)} async-done(((bf16[8,64,2048]{2,1,0:T(8,128)(2,1)}), bf16[8,64,2048]{2,1,0:T(8,128)(2,1)S(1)}, u32[]{:S(2)}, u32[]{:S(2)}) %all-to-all-start) | async-done | bytes 2097184 | tf_op jit(solution)/shard_map/all_to_all | solution.py:147
  37.2 0.8 shard_map.60
  38.0 0.1 collective-permute-start.2
  38.1 1.5 %collective-permute-done.2 = f32[16,8,512]{2,1,0:T(8,128)S(1)} collective-permute-done((f32[16,8,512]{2,1,0:T(8,128)S(1)}, f32[16,8,512]{2,1,0:T(8,128)S(1)}, u32[]{:S(2)}, u32[]{:S(2)}) %collective-permute-start.2) | collective-permute-done | bytes 262176 | tf_op jit(solution)/shard_map/ppermute | solution.py:157
  39.7 17.4 %all_to_all.20.parts_ref = bf16[16,8,512]{2,1,0:T(8,128)(2,1)S(1)} all-to-all(bf16[16,8,512]{2,1,0:T(8,128)(2,1)S(1)} %add_convert_fusion), channel_id=1, replica_groups={{0,16,32,48,64,80,96,112,128,144,160,176,192,208,224,240},{8,24,40,56,7..., dimensions={0} | all-to-all | bytes 262144 | tf_op jit(solution)/shard_map/all_to_all | solution.py:160
  57.0 0.0 copy-done.1
  57.0 0.2 shard_map.61
  57.2 12.5 %all_to_all.21.value_ref = bf16[32,8,128]{2,1,0:T(8,128)(2,1)S(1)} all-to-all(bf16[32,8,128]{2,1,0:T(8,128)(2,1)S(1)} %shard_map.61), channel_id=1, replica_groups=mesh['spec'=32,'bucket'=8] {'spec'}, dimensions={0} | all-to-all | bytes 131072 | tf_op jit(solution)/shard_map/all_to_all | solution.py:162
  69.8 0.9 %shard_map.62 = f32[16,128]{1,0:T(8,128)} custom-call(s32[1]{0:T(128)} %bitcast.where_ref, bf16[32,8,128]{2,1,0:T(8,128)(2,1)S(1)} %all_to_all.21.value_ref, s32[256,128]{1,0:T(8,128)S(1)} %copy-done.1), custom_call_target="tpu_custom_call" | custom-call | tf_op jit(solution)/shard_map/pallas_call | solution.py:126
  70.7 5.1 %all-to-all-start.3 = ((f32[8,2,128]{2,1,0:T(2,128)}), f32[8,2,128]{2,1,0:T(2,128)S(1)}, u32[]{:S(2)}, u32[]{:S(2)}) async-start(f32[8,2,128]{2,1,0:T(2,128)} %bitcast.4), calls=%async_computation.3 | async-start | bytes 16384 | tf_op jit(solution)/shard_map/all_to_all | solution.py:168
  75.8 0.7 bitcast_convert_fusion
  76.4 5.6 %all-to-all-done.3 = f32[8,2,128]{2,1,0:T(2,128)S(1)} async-done(((f32[8,2,128]{2,1,0:T(2,128)}), f32[8,2,128]{2,1,0:T(2,128)S(1)}, u32[]{:S(2)}, u32[]{:S(2)}) %all-to-all-start.3) | async-done | bytes 8224 | tf_op jit(solution)/shard_map/all_to_all | solution.py:168
  82.0 0.6 reduce_sum.9
  (1 shorter events, 0.0 us)
Async XLA Ops:
  3.2 13.6 %copy-start.2 = (s32[4]{0:T(128)S(1)}, s32[4]{0:T(128)}, u32[]{:S(2)}) copy-start(s32[4]{0:T(128)} %half_ref.1) | copy-start | bytes 52
  3.2 34.0 %all-to-all-start = ((bf16[8,64,2048]{2,1,0:T(8,128)(2,1)}), bf16[8,64,2048]{2,1,0:T(8,128)(2,1)S(1)}, u32[]{:S(2)}, u32[]{:S(2)}) async-start(bf16[8,64,2048]{2,1,0:T(8,128)(2,1)} %broadcast_in_dim.2), calls=%async_computation | async-start | bytes 4194304 | tf_op jit(solution)/shard_map/all_to_all | solution.py:147
  11.6 4.4 %collective-permute-start.1 = (bf16[256,128]{1,0:T(8,128)(2,1)S(1)}, bf16[256,128]{1,0:T(8,128)(2,1)S(1)}, u32[]{:S(2)}, u32[]{:S(2)}) collective-permute-start(bf16[256,128]{1,0:T(8,128)(2,1)S(1)} %get-tuple-element.10), channel_id=1, source_target_pairs={{8,0},{16,8},{24,16},{32,24},{40,32},{48,40},{56,48},{64,56},{72,6... | collective-permute-start | bytes 196616 | tf_op jit(solution)/shard_map/ppermute | solution.py:152
  12.9 3.9 %collective-permute-start = (bf16[256,128]{1,0:T(8,128)(2,1)S(1)}, bf16[256,128]{1,0:T(8,128)(2,1)S(1)}, u32[]{:S(2)}, u32[]{:S(2)}) collective-permute-start(bf16[256,128]{1,0:T(8,128)(2,1)S(1)} %get-tuple-element.11), channel_id=1, source_target_pairs={{0,8},{8,16},{16,24},{24,32},{32,40},{40,48},{48,56},{56,64},{64,7... | collective-permute-start | bytes 196616 | tf_op jit(solution)/shard_map/ppermute | solution.py:151
  16.8 1.2 %copy-start = (bf16[256,2048]{1,0:T(8,128)(2,1)S(1)}, bf16[256,2048]{1,0:T(8,128)(2,1)}, u32[]{:S(2)}) copy-start(bf16[256,2048]{1,0:T(8,128)(2,1)} %spectra_ref.1) | copy-start | bytes 3145732
  19.3 37.7 %copy-start.1 = (s32[256,128]{1,0:T(8,128)S(1)}, s32[256,128]{1,0:T(8,128)}, u32[]{:S(2)}) copy-start(s32[256,128]{1,0:T(8,128)} %cand_ref.3) | copy-start | bytes 393220
  38.0 1.6 %collective-permute-start.2 = (f32[16,8,512]{2,1,0:T(8,128)S(1)}, f32[16,8,512]{2,1,0:T(8,128)S(1)}, u32[]{:S(2)}, u32[]{:S(2)}) collective-permute-start(f32[16,8,512]{2,1,0:T(8,128)S(1)} %get-tuple-element.9), channel_id=1, source_target_pairs={{0,8},{8,0},{16,24},{24,16},{32,40},{40,32},{48,56},{56,48},{64,72... | collective-permute-start | bytes 786440 | tf_op jit(solution)/shard_map/ppermute | solution.py:157
  70.7 11.3 %all-to-all-start.3 = ((f32[8,2,128]{2,1,0:T(2,128)}), f32[8,2,128]{2,1,0:T(2,128)S(1)}, u32[]{:S(2)}, u32[]{:S(2)}) async-start(f32[8,2,128]{2,1,0:T(2,128)} %bitcast.4), calls=%async_computation.3 | async-start | bytes 16384 | tf_op jit(solution)/shard_map/all_to_all | solution.py:168

commit v5 on v3

--- a/solution.py
+++ b/solution.py
@@ -83,7 +83,7 @@
     )(core, processed, *pieces)
 
 
-def pick_kernel(where_ref, parts_ref, cand_ref, out_ref):
+def pick_kernel(spec_ref, bucket_ref, parts_ref, cand_ref, out_ref):
     count, own, peptides = parts_ref.shape
     lanes = cand_ref.shape[1]
     per_bucket = lanes // 2
@@ -91,9 +91,9 @@
     scores = jnp.sum(parts_ref[...].astype(jnp.float32), axis=0)
     centred = scores - jnp.mean(scores, axis=1, keepdims=True)
     spread = jnp.mean(jnp.square(centred), axis=1, keepdims=True)
-    first = pl.multiple_of(where_ref[0] * own, own)
+    first = pl.multiple_of(spec_ref[0] * own, own)
     ids = cand_ref[pl.ds(first, own), :]
-    bucket = where_ref[1]
+    bucket = bucket_ref[0]
     block_of = (ids // lanes - bucket // 2) & (rounds - 1)
     lane_of = (ids & (lanes - 1)) ^ ((bucket & 1) * per_bucket)
     picked = jnp.zeros((own, lanes), jnp.float32)
@@ -110,19 +110,18 @@
     return pl.pallas_call(
         pick_kernel,
         out_shape=jax.ShapeDtypeStruct((count, own, cand.shape[1]), jnp.bfloat16),
-        in_specs=[SMEM, VMEM, VMEM],
+        in_specs=[SMEM, SMEM, VMEM, VMEM],
         out_specs=VMEM,
         compiler_params=params(),
-    )(where, parts, cand)
-
-
-def evidence_kernel(load, where_ref, value_ref, cand_ref, wide_ref, out_ref):
+    )(*where, parts, cand)
+
+
+def evidence_kernel(load, spec_ref, value_ref, cand_ref, out_ref):
     share = out_ref.shape[0]
     rows, lanes = cand_ref.shape
     values = value_ref[...].astype(jnp.float32).reshape(rows, lanes)
-    wide_ref[...] = values
     soft = jax.nn.softplus(values)
-    ids = cand_ref[...] - where_ref[0] * share
+    ids = cand_ref[...] - spec_ref[0] * share
     for k in range(share):
         kept = jnp.where(ids == k, soft, 0.0)
         out_ref[k : k + 1, :] = jnp.sum(kept, axis=0, keepdims=True) / load
@@ -131,17 +130,33 @@
 def evidence_of(where, values, cand, share, load):
     return pl.pallas_call(
         functools.partial(evidence_kernel, load),
+        out_shape=jax.ShapeDtypeStruct((share, cand.shape[1]), jnp.float32),
+        in_specs=[SMEM, VMEM, VMEM],
+        out_specs=VMEM,
+        compiler_params=params(),
+    )(where[0], values, cand)
+
+
+def last_kernel(value_ref, evidence_ref, wide_ref, out_ref):
+    wide_ref[...] = value_ref[...].astype(jnp.float32).reshape(wide_ref.shape)
+    total = jnp.sum(jnp.sum(evidence_ref[...], axis=0), axis=1, keepdims=True)
+    out_ref[...] = jnp.broadcast_to(total, out_ref.shape)
+
+
+def last_step(values, evidence):
+    return pl.pallas_call(
+        last_kernel,
         out_shape=(
-            jax.ShapeDtypeStruct(cand.shape, jnp.float32),
-            jax.ShapeDtypeStruct((share, cand.shape[1]), jnp.float32),
+            jax.ShapeDtypeStruct((values.shape[0] * values.shape[1], values.shape[2]), jnp.float32),
+            jax.ShapeDtypeStruct(evidence.shape[1:], jnp.float32),
         ),
-        in_specs=[SMEM, VMEM, VMEM],
+        in_specs=[VMEM, VMEM],
         out_specs=(VMEM, VMEM),
         compiler_params=params(),
-    )(where, values, cand)
-
-
-def from_all_buckets(shard):
+    )(values, evidence)
+
+
+def from_all_buckets(shard, beside_work):
     count = lax.axis_size("bucket")
 
     def along_y(value, step):
@@ -152,9 +167,10 @@
 
     beside = along_x(shard)
     above, below, across = along_y(shard, 1), along_y(shard, 3), along_y(shard, 2)
-    across_beside = along_y(beside, 2)
-    above_beside, below_beside = along_x(above), along_x(below)
-    return [shard, beside, above, above_beside, across, across_beside, below, below_beside]
+    beside, across, processed = lax.optimization_barrier((beside, across, beside_work))
+    above_beside, below_beside = along_y(beside, 1), along_y(beside, 3)
+    across_beside = along_x(across)
+    return processed, [shard, beside, above, above_beside, across, across_beside, below, below_beside]
 
 
 def on_device(spectra, theory, cand, half):
@@ -165,16 +181,17 @@
     peptides_all = per_bucket * bucket_count
     spec = lax.axis_index("spec").astype(jnp.int32)
     bucket = lax.axis_index("bucket").astype(jnp.int32)
-    where = jnp.stack([spec, bucket])
+    where = spec.reshape(1), bucket.reshape(1)
     core = (spec % 2).reshape(1)
 
-    pieces = from_all_buckets(theory)
+    theory, low, high = lax.optimization_barrier((theory, spectra[:, -SIDE:], spectra[:, :SIDE]))
 
     forward = [(i, i + 1) for i in range(spec_count - 1)]
     backward = [(target, source) for source, target in forward]
-    low = lax.ppermute(spectra[:, -SIDE:], "spec", forward)
-    high = lax.ppermute(spectra[:, :SIDE], "spec", backward)
+    low = lax.ppermute(low, "spec", forward)
+    high = lax.ppermute(high, "spec", backward)
     processed = windowed(half, spectra, low, high)
+    processed, pieces = from_all_buckets(theory, processed)
 
     own = row_count // spec_count
     keep, send = scored(core, processed, pieces, own)
@@ -187,11 +204,12 @@
 
     share = peptides_all // spec_count
     mean_load = cand.shape[1] * row_count / per_bucket
-    cand_scores, evidence = evidence_of(where, values, cand, share, mean_load)
+    evidence = evidence_of(where, values, cand, share, mean_load)
     evidence = lax.all_to_all(
         evidence.reshape(bucket_count, share // bucket_count, cand.shape[1]), "bucket", 0, 0, tiled=True
     )
-    return (cand_scores, jnp.sum(evidence, axis=(0, 2)))
+    cand_scores, totals = last_step(values, evidence)
+    return (cand_scores, totals[:, 0])
 
 
 def solution(mesh):

time: 89.1 us -> 78.1 us (0.88)
  starting transfers between devices: 39 us -> 25.1 us
  waiting for transfers between devices: 12.6 us -> 17.8 us
  blocking collectives: 28.8 us -> 27.3 us
    ppermute x4 -> x5, starting transfers between devices: 16.3 us -> 6.44 us  [along_y(): lax.ppermute(value, 'bucket', [(b, (b - 2 * step) % count) for b in range...]
    ppermute x3 -> x2, waiting for transfers between devices: 0.01 us -> 5.95 us  [along_x(): return lax.ppermute(value, 'bucket', [(b, b ^ 1) for b in range(count)])]
    ppermute x2, starting transfers between devices: 6.22 us -> 2.57 us  [the longest x1 1.29 us: on_device(): high = lax.ppermute(high, 'spec', backward)]
    ppermute x1, starting transfers between devices: 0.53 us -> 2.11 us  [on_device(): got = lax.ppermute(send, 'spec', [(i, i ^ 1) for i in range(spec_count)])]
    all_to_all x1, blocking collectives: 16.2 us -> 14.8 us  [on_device(): lax.all_to_all(evidence.reshape(bucket_count, share // bucket_count, cand...]
    all_to_all x1, starting transfers between devices: 11.8 us -> 10.3 us  [on_device(): lax.all_to_all(chip, 'spec', 0, 0, axis_index_groups=groups, tiled=True)]
    ppermute x3 -> x2, starting transfers between devices: 4.14 us -> 3.62 us  [along_x(): return lax.ppermute(value, 'bucket', [(b, b ^ 1) for b in range(count)])]
  transfers between devices with their start and end apart: 11 -> 11, of which waited for: 4 -> 4; matrix products, arithmetic and copies ran while one was open for 1% -> 0% of each run, Pallas kernels for 1% -> 2%
where the time goes in v5:
time: 78.1 us; the launch traced here: 77.8 us
  blocking collectives  27.3 us (35%)
  starting transfers between devices  25.1 us (32%)
  waiting for transfers between devices  17.8 us (23%)
  Pallas kernels  3.29 us (4%)
  local copies, waits for them, and re-layouts  2.85 us (4%)
    all_to_all x1, blocking collectives, on_device(): lax.all_to_all(evidence.reshape(bucket_count, share // bucket_count, cand...  14.8 us
    all_to_all x1, blocking collectives, on_device(): values = lax.all_to_all(copies, 'spec', 0, 0, tiled=True)  12.5 us
    all_to_all x1, starting transfers between devices, on_device(): lax.all_to_all(chip, 'spec', 0, 0, axis_index_groups=groups, tiled=True)  10.3 us
    all_to_all x1, waiting for transfers between devices, on_device(): lax.all_to_all(chip, 'spec', 0, 0, axis_index_groups=groups, tiled=True)  8.74 us
    ppermute x5, starting transfers between devices, along_y(): lax.ppermute(value, 'bucket', [(b, (b - 2 * step) % count) for b in range...  6.44 us
    ppermute x2, waiting for transfers between devices, along_x(): return lax.ppermute(value, 'bucket', [(b, b ^ 1) for b in range(count)])  5.95 us
    ppermute x2, starting transfers between devices, along_x(): return lax.ppermute(value, 'bucket', [(b, b ^ 1) for b in range(count)])  3.62 us
    ppermute x1, starting transfers between devices, on_device(): got = lax.ppermute(send, 'spec', [(i, i ^ 1) for i in range(spec_count)])  2.11 us
  transfers between devices with their start and end apart: 11, of which 4 were waited for; matrix products, arithmetic and copies ran while one was open for 0% of the time, Pallas kernels for 2%

profile of v5, /device:TPU:8, one launch (start us, length us, event | category | flops | bytes accessed | tf_op | source)
XLA Modules:
  0.0 77.8 jit_solution(885039301097005808)
XLA Ops:
  0.6 0.0 copy-start.2
  0.6 0.9 %fusion = (bf16[256,128]{1,0:T(8,128)(2,1)S(1)}, bf16[256,128]{1,0:T(8,128)(2,1)S(1)}) fusion(bf16[256,2048]{1,0:T(8,128)(2,1)} %spectra_ref.1), kind=kLoop, calls=%fused_computation.2 | loop fusion | bytes 262144 | tf_op jit(solution)/shard_map/slice | solution.py:187
  1.6 0.0 copy-start.3
  1.6 0.1 copy-done.2
  1.6 2.3 %collective-permute-start.1 = (bf16[64,2048]{1,0:T(8,128)(2,1)S(1)}, bf16[64,2048]{1,0:T(8,128)(2,1)S(1)}, u32[]{:S(2)}, u32[]{:S(2)}) collective-permute-start(bf16[64,2048]{1,0:T(8,128)(2,1)S(1)} %copy-done.2), channel_id=1, source_target_pairs={{0,4},{1,5},{2,6},{3,7},{4,0},{5,1},{6,2},{7,3},{8,12},{9,13},{10,... | collective-permute-start | bytes 786440 | tf_op jit(solution)/shard_map/ppermute | solution.py:163
  4.0 3.0 %collective-permute-start = (bf16[64,2048]{1,0:T(8,128)(2,1)S(1)}, bf16[64,2048]{1,0:T(8,128)(2,1)S(1)}, u32[]{:S(2)}, u32[]{:S(2)}) collective-permute-start(bf16[64,2048]{1,0:T(8,128)(2,1)S(1)} %copy-done.2), channel_id=1, source_target_pairs={{0,1},{1,0},{2,3},{3,2},{4,5},{5,4},{6,7},{7,6},{8,9},{9,8},{10,11... | collective-permute-start | bytes 786440 | tf_op jit(solution)/shard_map/ppermute | solution.py:166
  7.0 1.3 %collective-permute-start.2 = (bf16[256,128]{1,0:T(8,128)(2,1)S(1)}, bf16[256,128]{1,0:T(8,128)(2,1)S(1)}, u32[]{:S(2)}, u32[]{:S(2)}) collective-permute-start(bf16[256,128]{1,0:T(8,128)(2,1)S(1)} %get-tuple-element.13), channel_id=1, source_target_pairs={{0,8},{8,16},{16,24},{24,32},{32,40},{40,48},{48,56},{56,64},{64,7... | collective-permute-start | bytes 196616 | tf_op jit(solution)/shard_map/ppermute | solution.py:191
  8.3 1.3 %collective-permute-start.3 = (bf16[256,128]{1,0:T(8,128)(2,1)S(1)}, bf16[256,128]{1,0:T(8,128)(2,1)S(1)}, u32[]{:S(2)}, u32[]{:S(2)}) collective-permute-start(bf16[256,128]{1,0:T(8,128)(2,1)S(1)} %get-tuple-element.14), channel_id=1, source_target_pairs={{8,0},{16,8},{24,16},{32,24},{40,32},{48,40},{56,48},{64,56},{72,6... | collective-permute-start | bytes 196616 | tf_op jit(solution)/shard_map/ppermute | solution.py:192
  9.6 0.1 collective-permute-start.7
  9.7 0.0 collective-permute-done.2.low_ref
  9.7 2.0 %collective-permute-start.4 = (bf16[64,2048]{1,0:T(8,128)(2,1)S(1)}, bf16[64,2048]{1,0:T(8,128)(2,1)S(1)}, u32[]{:S(2)}, u32[]{:S(2)}) collective-permute-start(bf16[64,2048]{1,0:T(8,128)(2,1)S(1)} %copy-done.2), channel_id=1, source_target_pairs={{0,6},{1,7},{2,0},{3,1},{4,2},{5,3},{6,4},{7,5},{8,14},{9,15},{10,... | collective-permute-start | bytes 786440 | tf_op jit(solution)/shard_map/ppermute | solution.py:163
  11.7 1.9 %collective-permute-done.3.high_ref = bf16[256,128]{1,0:T(8,128)(2,1)S(1)} collective-permute-done((bf16[256,128]{1,0:T(8,128)(2,1)S(1)}, bf16[256,128]{1,0:T(8,128)(2,1)S(1)}, u32[]{:S(2)}, u32[]{:S(2)}) %collective-permute-start.3) | collective-permute-done | bytes 65568 | tf_op jit(solution)/shard_map/ppermute | solution.py:192
  13.6 0.0 copy-done.3
  13.6 0.0 copy-start
  13.6 1.2 %copy-done = bf16[256,2048]{1,0:T(8,128)(2,1)S(1)} copy-done((bf16[256,2048]{1,0:T(8,128)(2,1)S(1)}, bf16[256,2048]{1,0:T(8,128)(2,1)}, u32[]{:S(2)}) %copy-start) | copy-done | bytes 1048600
  14.8 1.3 %shard_map.59.processed_ref = bf16[256,2048]{1,0:T(8,128)(2,1)S(1)} custom-call(s32[4]{0:T(128)S(1)} %copy-done.3, bf16[256,2048]{1,0:T(8,128)(2,1)S(1)} %copy-done, bf16[256,128]{1,0:T(8,128)(2,1)S(1)} %collective-permute-done.2.low_ref, bf16[256,128]{1,0:T(8,128)(2,1)S(1)} %collective-permute-done.3.high_ref), custom_call_target="tpu_custom_call" | custom-call | flops 536870912 | bytes 2097152 | tf_op jit(solution)/shard_map/pallas_call | solution.py:44
  16.1 0.0 collective-permute-done.1.refs_4_
  16.1 0.0 collective-permute-done.refs_1_
  16.1 0.6 collective-permute-start.6
  16.7 0.0 collective-permute-start.8
  16.7 2.0 %collective-permute-start.5 = (bf16[64,2048]{1,0:T(8,128)(2,1)S(1)}, bf16[64,2048]{1,0:T(8,128)(2,1)S(1)}, u32[]{:S(2)}, u32[]{:S(2)}) collective-permute-start(bf16[64,2048]{1,0:T(8,128)(2,1)S(1)} %collective-permute-done.refs_1_), channel_id=1, source_target_pairs={{0,6},{1,7},{2,0},{3,1},{4,2},{5,3},{6,4},{7,5},{8,14},{9,15},{10,... | collective-permute-start | bytes 786440 | tf_op jit(solution)/shard_map/ppermute | solution.py:163
  18.8 0.0 collective-permute-done.7.refs_6_
  18.8 0.0 collective-permute-done.4.refs_2_
  18.8 5.9 %collective-permute-done.6.refs_5_ = bf16[64,2048]{1,0:T(8,128)(2,1)S(1)} collective-permute-done((bf16[64,2048]{1,0:T(8,128)(2,1)S(1)}, bf16[64,2048]{1,0:T(8,128)(2,1)S(1)}, u32[]{:S(2)}, u32[]{:S(2)}) %collective-permute-start.6) | collective-permute-done | bytes 262176 | tf_op jit(solution)/shard_map/ppermute | solution.py:166
  24.7 0.0 collective-permute-done.8.refs_7_
  24.7 0.0 collective-permute-done.5.refs_3_
  24.7 0.8 %shard_map.60 = (f32[16,8,512]{2,1,0:T(8,128)S(1)}, f32[16,8,512]{2,1,0:T(8,128)S(1)}) custom-call(s32[1]{0:T(128)} %bitcast.2.core_ref, bf16[256,2048]{1,0:T(8,128)(2,1)S(1)} %shard_map.59.processed_ref, bf16[64,2048]{1,0:T(8,128)(2,1)S(1)} %copy-done.2, bf16[64,2048]{1,0:T(8,128)(2,1)S(1)} %collective-permute-done.refs_1_, ...), custom_call_target="tpu_custom_call" | custom-call | flops 536870912 | bytes 3145728 | tf_op jit(solution)/shard_map/pallas_call | solution.py:74
  25.5 2.1 %collective-permute-start.9 = (f32[16,8,512]{2,1,0:T(8,128)S(1)}, f32[16,8,512]{2,1,0:T(8,128)S(1)}, u32[]{:S(2)}, u32[]{:S(2)}) collective-permute-start(f32[16,8,512]{2,1,0:T(8,128)S(1)} %get-tuple-element.19), channel_id=1, source_target_pairs={{0,8},{8,0},{16,24},{24,16},{32,40},{40,32},{48,56},{56,48},{64,72... | collective-permute-start | bytes 786440 | tf_op jit(solution)/shard_map/ppermute | solution.py:198
  27.7 1.2 %collective-permute-done.9 = f32[16,8,512]{2,1,0:T(8,128)S(1)} collective-permute-done((f32[16,8,512]{2,1,0:T(8,128)S(1)}, f32[16,8,512]{2,1,0:T(8,128)S(1)}, u32[]{:S(2)}, u32[]{:S(2)}) %collective-permute-start.9) | collective-permute-done | bytes 262176 | tf_op jit(solution)/shard_map/ppermute | solution.py:198
  28.8 0.7 add_convert_fusion
  29.5 0.0 copy-start.1
  29.5 10.3 %all-to-all-start = ((bf16[16,8,512]{2,1,0:T(8,128)(2,1)}), bf16[16,8,512]{2,1,0:T(8,128)(2,1)S(1)}, u32[]{:S(2)}, u32[]{:S(2)}) async-start(bf16[16,8,512]{2,1,0:T(8,128)(2,1)} %add_convert_fusion), calls=%async_computation | async-start | bytes 262144 | tf_op jit(solution)/shard_map/all_to_all | solution.py:201
  39.9 8.7 %all-to-all-done.parts_ref = bf16[16,8,512]{2,1,0:T(8,128)(2,1)S(1)} async-done(((bf16[16,8,512]{2,1,0:T(8,128)(2,1)}), bf16[16,8,512]{2,1,0:T(8,128)(2,1)S(1)}, u32[]{:S(2)}, u32[]{:S(2)}) %all-to-all-start) | async-done | bytes 131104 | tf_op jit(solution)/shard_map/all_to_all | solution.py:201
  48.6 0.0 copy-done.1
  48.6 0.2 shard_map.61
  48.8 12.5 %all_to_all.15.value_ref = bf16[32,8,128]{2,1,0:T(8,128)(2,1)S(1)} all-to-all(bf16[32,8,128]{2,1,0:T(8,128)(2,1)S(1)} %shard_map.61), channel_id=1, replica_groups=mesh['spec'=32,'bucket'=8] {'spec'}, dimensions={0} | all-to-all | bytes 131072 | tf_op jit(solution)/shard_map/all_to_all | solution.py:203
  61.4 0.3 shard_map.62
  61.7 14.8 %all_to_all.16.evidence_ref = f32[8,2,128]{2,1,0:T(2,128)S(1)} all-to-all(f32[8,2,128]{2,1,0:T(2,128)S(1)} %bitcast.4), channel_id=1, replica_groups=mesh['spec'=32,'bucket'=8] {'bucket'}, dimensions={0} | all-to-all | bytes 16384 | tf_op jit(solution)/shard_map/all_to_all | solution.py:208
  76.5 0.7 shard_map.63
  77.1 0.6 slice_reduce_fusion
Async XLA Ops:
  0.6 1.0 %copy-start.2 = (bf16[64,2048]{1,0:T(8,128)(2,1)S(1)}, bf16[64,2048]{1,0:T(8,128)(2,1)}, u32[]{:S(2)}) copy-start(bf16[64,2048]{1,0:T(8,128)(2,1)} %refs_0_) | copy-start | bytes 786436
  1.6 12.0 %copy-start.3 = (s32[4]{0:T(128)S(1)}, s32[4]{0:T(128)}, u32[]{:S(2)}) copy-start(s32[4]{0:T(128)} %half_ref.1) | copy-start | bytes 52
  1.6 14.5 %collective-permute-start.1 = (bf16[64,2048]{1,0:T(8,128)(2,1)S(1)}, bf16[64,2048]{1,0:T(8,128)(2,1)S(1)}, u32[]{:S(2)}, u32[]{:S(2)}) collective-permute-start(bf16[64,2048]{1,0:T(8,128)(2,1)S(1)} %copy-done.2), channel_id=1, source_target_pairs={{0,4},{1,5},{2,6},{3,7},{4,0},{5,1},{6,2},{7,3},{8,12},{9,13},{10,... | collective-permute-start | bytes 786440 | tf_op jit(solution)/shard_map/ppermute | solution.py:163
  4.0 12.2 %collective-permute-start = (bf16[64,2048]{1,0:T(8,128)(2,1)S(1)}, bf16[64,2048]{1,0:T(8,128)(2,1)S(1)}, u32[]{:S(2)}, u32[]{:S(2)}) collective-permute-start(bf16[64,2048]{1,0:T(8,128)(2,1)S(1)} %copy-done.2), channel_id=1, source_target_pairs={{0,1},{1,0},{2,3},{3,2},{4,5},{5,4},{6,7},{7,6},{8,9},{9,8},{10,11... | collective-permute-start | bytes 786440 | tf_op jit(solution)/shard_map/ppermute | solution.py:166
  7.0 2.7 %collective-permute-start.2 = (bf16[256,128]{1,0:T(8,128)(2,1)S(1)}, bf16[256,128]{1,0:T(8,128)(2,1)S(1)}, u32[]{:S(2)}, u32[]{:S(2)}) collective-permute-start(bf16[256,128]{1,0:T(8,128)(2,1)S(1)} %get-tuple-element.13), channel_id=1, source_target_pairs={{0,8},{8,16},{16,24},{24,32},{32,40},{40,48},{48,56},{56,64},{64,7... | collective-permute-start | bytes 196616 | tf_op jit(solution)/shard_map/ppermute | solution.py:191
  8.3 5.3 %collective-permute-start.3 = (bf16[256,128]{1,0:T(8,128)(2,1)S(1)}, bf16[256,128]{1,0:T(8,128)(2,1)S(1)}, u32[]{:S(2)}, u32[]{:S(2)}) collective-permute-start(bf16[256,128]{1,0:T(8,128)(2,1)S(1)} %get-tuple-element.14), channel_id=1, source_target_pairs={{8,0},{16,8},{24,16},{32,24},{40,32},{48,40},{56,48},{64,56},{72,6... | collective-permute-start | bytes 196616 | tf_op jit(solution)/shard_map/ppermute | solution.py:192
  9.6 9.2 %collective-permute-start.7 = (bf16[64,2048]{1,0:T(8,128)(2,1)S(1)}, bf16[64,2048]{1,0:T(8,128)(2,1)S(1)}, u32[]{:S(2)}, u32[]{:S(2)}) collective-permute-start(bf16[64,2048]{1,0:T(8,128)(2,1)S(1)} %copy-done.2), channel_id=1, source_target_pairs={{0,2},{1,3},{2,4},{3,5},{4,6},{5,7},{6,0},{7,1},{8,10},{9,11},{10,... | collective-permute-start | bytes 786440 | tf_op jit(solution)/shard_map/ppermute | solution.py:163
  9.7 9.1 %collective-permute-start.4 = (bf16[64,2048]{1,0:T(8,128)(2,1)S(1)}, bf16[64,2048]{1,0:T(8,128)(2,1)S(1)}, u32[]{:S(2)}, u32[]{:S(2)}) collective-permute-start(bf16[64,2048]{1,0:T(8,128)(2,1)S(1)} %copy-done.2), channel_id=1, source_target_pairs={{0,6},{1,7},{2,0},{3,1},{4,2},{5,3},{6,4},{7,5},{8,14},{9,15},{10,... | collective-permute-start | bytes 786440 | tf_op jit(solution)/shard_map/ppermute | solution.py:163
  13.6 1.2 %copy-start = (bf16[256,2048]{1,0:T(8,128)(2,1)S(1)}, bf16[256,2048]{1,0:T(8,128)(2,1)}, u32[]{:S(2)}) copy-start(bf16[256,2048]{1,0:T(8,128)(2,1)} %spectra_ref.1) | copy-start | bytes 3145732
  16.1 8.6 %collective-permute-start.6 = (bf16[64,2048]{1,0:T(8,128)(2,1)S(1)}, bf16[64,2048]{1,0:T(8,128)(2,1)S(1)}, u32[]{:S(2)}, u32[]{:S(2)}) collective-permute-start(bf16[64,2048]{1,0:T(8,128)(2,1)S(1)} %collective-permute-done.1.refs_4_), channel_id=1, source_target_pairs={{0,1},{1,0},{2,3},{3,2},{4,5},{5,4},{6,7},{7,6},{8,9},{9,8},{10,11... | collective-permute-start | bytes 786440 | tf_op jit(solution)/shard_map/ppermute | solution.py:166
  16.7 8.0 %collective-permute-start.8 = (bf16[64,2048]{1,0:T(8,128)(2,1)S(1)}, bf16[64,2048]{1,0:T(8,128)(2,1)S(1)}, u32[]{:S(2)}, u32[]{:S(2)}) collective-permute-start(bf16[64,2048]{1,0:T(8,128)(2,1)S(1)} %collective-permute-done.refs_1_), channel_id=1, source_target_pairs={{0,2},{1,3},{2,4},{3,5},{4,6},{5,7},{6,0},{7,1},{8,10},{9,11},{10,... | collective-permute-start | bytes 786440 | tf_op jit(solution)/shard_map/ppermute | solution.py:163
  16.7 8.0 %collective-permute-start.5 = (bf16[64,2048]{1,0:T(8,128)(2,1)S(1)}, bf16[64,2048]{1,0:T(8,128)(2,1)S(1)}, u32[]{:S(2)}, u32[]{:S(2)}) collective-permute-start(bf16[64,2048]{1,0:T(8,128)(2,1)S(1)} %collective-permute-done.refs_1_), channel_id=1, source_target_pairs={{0,6},{1,7},{2,0},{3,1},{4,2},{5,3},{6,4},{7,5},{8,14},{9,15},{10,... | collective-permute-start | bytes 786440 | tf_op jit(solution)/shard_map/ppermute | solution.py:163
  25.5 3.3 %collective-permute-start.9 = (f32[16,8,512]{2,1,0:T(8,128)S(1)}, f32[16,8,512]{2,1,0:T(8,128)S(1)}, u32[]{:S(2)}, u32[]{:S(2)}) collective-permute-start(f32[16,8,512]{2,1,0:T(8,128)S(1)} %get-tuple-element.19), channel_id=1, source_target_pairs={{0,8},{8,0},{16,24},{24,16},{32,40},{40,32},{48,56},{56,48},{64,72... | collective-permute-start | bytes 786440 | tf_op jit(solution)/shard_map/ppermute | solution.py:198
  29.5 19.1 %copy-start.1 = (s32[256,128]{1,0:T(8,128)S(1)}, s32[256,128]{1,0:T(8,128)}, u32[]{:S(2)}) copy-start(s32[256,128]{1,0:T(8,128)} %cand_ref.3) | copy-start | bytes 393220
  29.5 19.1 %all-to-all-start = ((bf16[16,8,512]{2,1,0:T(8,128)(2,1)}), bf16[16,8,512]{2,1,0:T(8,128)(2,1)S(1)}, u32[]{:S(2)}, u32[]{:S(2)}) async-start(bf16[16,8,512]{2,1,0:T(8,128)(2,1)} %add_convert_fusion), calls=%async_computation | async-start | bytes 262144 | tf_op jit(solution)/shard_map/all_to_all | solution.py:201

commit v6 on v5

--- a/solution.py
+++ b/solution.py
@@ -19,7 +19,8 @@
     return pltpu.CompilerParams(vmem_limit_bytes=16 * 1024 * 1024)
 
 
-def window_kernel(half_ref, spectra_ref, low_ref, high_ref, out_ref, wide_ref):
+def window_kernel(half_ref, spec_ref, bucket_ref, spectra_ref, low_ref, high_ref, cand_ref, out_ref, near_ref, wide_ref):
+    near_ref[...] = cand_ref[...]
     bins = spectra_ref.shape[1]
     wide_ref[:, :SIDE] = low_ref[...]
     wide_ref[:, SIDE : SIDE + bins] = spectra_ref[...]
@@ -39,17 +40,17 @@
             out_ref[:, at : at + TILE] = (middle - sums / divisor).astype(jnp.bfloat16)
 
 
-def windowed(half, spectra, low, high):
+def windowed(half, where, spectra, low, high, cand):
     rows, bins = spectra.shape
     return pl.pallas_call(
         window_kernel,
-        out_shape=jax.ShapeDtypeStruct((rows, bins), jnp.bfloat16),
-        in_specs=[SMEM, VMEM, VMEM, VMEM],
-        out_specs=VMEM,
+        out_shape=(jax.ShapeDtypeStruct((rows, bins), jnp.bfloat16), jax.ShapeDtypeStruct(cand.shape, cand.dtype)),
+        in_specs=[SMEM, SMEM, SMEM, VMEM, VMEM, VMEM, VMEM],
+        out_specs=(VMEM, VMEM),
         scratch_shapes=[pltpu.VMEM((rows, bins + 2 * SIDE), jnp.bfloat16)],
         compiler_params=params(),
         cost_estimate=pl.CostEstimate(flops=2 * rows * bins * 512, bytes_accessed=4 * rows * bins, transcendentals=0),
-    )(half, spectra, low, high)
+    )(half, *where, spectra, low, high, cand)
 
 
 def score_kernel(core_ref, processed_ref, *refs):
@@ -140,7 +141,11 @@
 def last_kernel(value_ref, evidence_ref, wide_ref, out_ref):
     wide_ref[...] = value_ref[...].astype(jnp.float32).reshape(wide_ref.shape)
     total = jnp.sum(jnp.sum(evidence_ref[...], axis=0), axis=1, keepdims=True)
-    out_ref[...] = jnp.broadcast_to(total, out_ref.shape)
+    column = lax.broadcasted_iota(jnp.int32, out_ref.shape, 1)
+    row = jnp.zeros(out_ref.shape, jnp.float32)
+    for k in range(out_ref.shape[1]):
+        row = jnp.where(column == k, total[k : k + 1], row)
+    out_ref[...] = row
 
 
 def last_step(values, evidence):
@@ -148,7 +153,7 @@
         last_kernel,
         out_shape=(
             jax.ShapeDtypeStruct((values.shape[0] * values.shape[1], values.shape[2]), jnp.float32),
-            jax.ShapeDtypeStruct(evidence.shape[1:], jnp.float32),
+            jax.ShapeDtypeStruct((1, evidence.shape[1]), jnp.float32),
         ),
         in_specs=[VMEM, VMEM],
         out_specs=(VMEM, VMEM),
@@ -156,7 +161,7 @@
     )(values, evidence)
 
 
-def from_all_buckets(shard, beside_work):
+def from_all_buckets(shard, low, high):
     count = lax.axis_size("bucket")
 
     def along_y(value, step):
@@ -167,10 +172,10 @@
 
     beside = along_x(shard)
     above, below, across = along_y(shard, 1), along_y(shard, 3), along_y(shard, 2)
-    beside, across, processed = lax.optimization_barrier((beside, across, beside_work))
+    beside, across, low, high = lax.optimization_barrier((beside, across, low, high))
     above_beside, below_beside = along_y(beside, 1), along_y(beside, 3)
     across_beside = along_x(across)
-    return processed, [shard, beside, above, above_beside, across, across_beside, below, below_beside]
+    return low, high, [shard, beside, above, above_beside, across, across_beside, below, below_beside]
 
 
 def on_device(spectra, theory, cand, half):
@@ -190,8 +195,8 @@
     backward = [(target, source) for source, target in forward]
     low = lax.ppermute(low, "spec", forward)
     high = lax.ppermute(high, "spec", backward)
-    processed = windowed(half, spectra, low, high)
-    processed, pieces = from_all_buckets(theory, processed)
+    low, high, pieces = from_all_buckets(theory, low, high)
+    processed, cand = windowed(half, where, spectra, low, high, cand)
 
     own = row_count // spec_count
     keep, send = scored(core, processed, pieces, own)
@@ -209,7 +214,7 @@
         evidence.reshape(bucket_count, share // bucket_count, cand.shape[1]), "bucket", 0, 0, tiled=True
     )
     cand_scores, totals = last_step(values, evidence)
-    return (cand_scores, totals[:, 0])
+    return (cand_scores, totals.reshape(-1))
 
 
 def solution(mesh):

time: 78.1 us -> 74.1 us (0.949)
  blocking collectives: 27.3 us -> 44.8 us
  waiting for transfers between devices: 17.8 us -> 6.28 us
  starting transfers between devices: 25.1 us -> 14.8 us
  local copies, waits for them, and re-layouts: 2.85 us -> 3.79 us
    all_to_all x0 -> x1, blocking collectives: none -> 17.9 us  [on_device(): lax.all_to_all(chip, 'spec', 0, 0, axis_index_groups=groups, tiled=True)]
    all_to_all x1 -> x0, starting transfers between devices: 10.3 us -> none  [on_device(): lax.all_to_all(chip, 'spec', 0, 0, axis_index_groups=groups, tiled=True)]
    all_to_all x1 -> x0, waiting for transfers between devices: 8.74 us -> none  [on_device(): lax.all_to_all(chip, 'spec', 0, 0, axis_index_groups=groups, tiled=True)]
    ppermute x2, waiting for transfers between devices: 5.95 us -> 0.47 us  [along_x(): return lax.ppermute(value, 'bucket', [(b, b ^ 1) for b in range(count)])]
    ppermute x5, waiting for transfers between devices: 0.01 us -> 2.4 us  [along_y(): lax.ppermute(value, 'bucket', [(b, (b - 2 * step) % count) for b in range...]
    ppermute x2, starting transfers between devices: 3.62 us -> 5.7 us  [along_x(): return lax.ppermute(value, 'bucket', [(b, b ^ 1) for b in range(count)])]
    ppermute x1, starting transfers between devices: 2.11 us -> 0.09 us  [on_device(): got = lax.ppermute(send, 'spec', [(i, i ^ 1) for i in range(spec_count)])]
    unnamed x8, local copies, waits for them, and re-layouts: 1.3 us -> 2.86 us
  transfers between devices with their start and end apart: 11 -> 10, of which waited for: 4 -> 4; matrix products, arithmetic and copies ran while one was open for 0% -> 0% of each run, Pallas kernels for 2% -> 2%
where the time goes in v6:
time: 74.1 us; the launch traced here: 73.7 us
  blocking collectives  44.8 us (60%)
  starting transfers between devices  14.8 us (20%)
  waiting for transfers between devices  6.28 us (8%)
  local copies, waits for them, and re-layouts  3.79 us (5%)
  Pallas kernels  3.3 us (4%)
    all_to_all x1, blocking collectives, on_device(): lax.all_to_all(chip, 'spec', 0, 0, axis_index_groups=groups, tiled=True)  17.9 us
    all_to_all x1, blocking collectives, on_device(): lax.all_to_all(evidence.reshape(bucket_count, share // bucket_count, cand...  14.4 us
    all_to_all x1, blocking collectives, on_device(): values = lax.all_to_all(copies, 'spec', 0, 0, tiled=True)  12.5 us
    ppermute x5, starting transfers between devices, along_y(): lax.ppermute(value, 'bucket', [(b, (b - 2 * step) % count) for b in range...  6.43 us
    ppermute x2, starting transfers between devices, along_x(): return lax.ppermute(value, 'bucket', [(b, b ^ 1) for b in range(count)])  5.7 us
    unnamed x8, local copies, waits for them, and re-layouts  2.86 us
    ppermute x5, waiting for transfers between devices, along_y(): lax.ppermute(value, 'bucket', [(b, (b - 2 * step) % count) for b in range...  2.4 us
    ppermute x1, waiting for transfers between devices, on_device(): high = lax.ppermute(high, 'spec', backward)  1.89 us
  transfers between devices with their start and end apart: 10, of which 4 were waited for; matrix products, arithmetic and copies ran while one was open for 0% of the time, Pallas kernels for 2%

profile of v6, /device:TPU:8, one launch (start us, length us, event | category | flops | bytes accessed | tf_op | source)
XLA Modules:
  0.0 73.7 jit_solution(591890143320297214)
XLA Ops:
  0.6 0.0 copy-start
  0.6 0.9 %fusion = (bf16[256,128]{1,0:T(8,128)(2,1)S(1)}, bf16[256,128]{1,0:T(8,128)(2,1)S(1)}) fusion(bf16[256,2048]{1,0:T(8,128)(2,1)} %spectra_ref.1), kind=kLoop, calls=%fused_computation.1 | loop fusion | bytes 262144 | tf_op jit(solution)/shard_map/slice | solution.py:192
  1.6 0.1 copy-done
  1.6 2.3 %collective-permute-start.1 = (bf16[64,2048]{1,0:T(8,128)(2,1)S(1)}, bf16[64,2048]{1,0:T(8,128)(2,1)S(1)}, u32[]{:S(2)}, u32[]{:S(2)}) collective-permute-start(bf16[64,2048]{1,0:T(8,128)(2,1)S(1)} %copy-done), channel_id=1, source_target_pairs={{0,4},{1,5},{2,6},{3,7},{4,0},{5,1},{6,2},{7,3},{8,12},{9,13},{10,... | collective-permute-start | bytes 786440 | tf_op jit(solution)/shard_map/ppermute | solution.py:168
  4.0 3.0 %collective-permute-start = (bf16[64,2048]{1,0:T(8,128)(2,1)S(1)}, bf16[64,2048]{1,0:T(8,128)(2,1)S(1)}, u32[]{:S(2)}, u32[]{:S(2)}) collective-permute-start(bf16[64,2048]{1,0:T(8,128)(2,1)S(1)} %copy-done), channel_id=1, source_target_pairs={{0,1},{1,0},{2,3},{3,2},{4,5},{5,4},{6,7},{7,6},{8,9},{9,8},{10,11... | collective-permute-start | bytes 786440 | tf_op jit(solution)/shard_map/ppermute | solution.py:171
  7.0 1.3 %collective-permute-start.2 = (bf16[256,128]{1,0:T(8,128)(2,1)S(1)}, bf16[256,128]{1,0:T(8,128)(2,1)S(1)}, u32[]{:S(2)}, u32[]{:S(2)}) collective-permute-start(bf16[256,128]{1,0:T(8,128)(2,1)S(1)} %get-tuple-element.16), channel_id=1, source_target_pairs={{0,8},{8,16},{16,24},{24,32},{32,40},{40,48},{48,56},{56,64},{64,7... | collective-permute-start | bytes 196616 | tf_op jit(solution)/shard_map/ppermute | solution.py:196
  8.3 1.3 %collective-permute-start.3 = (bf16[256,128]{1,0:T(8,128)(2,1)S(1)}, bf16[256,128]{1,0:T(8,128)(2,1)S(1)}, u32[]{:S(2)}, u32[]{:S(2)}) collective-permute-start(bf16[256,128]{1,0:T(8,128)(2,1)S(1)} %get-tuple-element.17), channel_id=1, source_target_pairs={{8,0},{16,8},{24,16},{32,24},{40,32},{48,40},{56,48},{64,56},{72,6... | collective-permute-start | bytes 196616 | tf_op jit(solution)/shard_map/ppermute | solution.py:197
  9.6 0.1 collective-permute-start.7
  9.7 0.0 collective-permute-done.2.low_ref
  9.7 2.0 %collective-permute-start.4 = (bf16[64,2048]{1,0:T(8,128)(2,1)S(1)}, bf16[64,2048]{1,0:T(8,128)(2,1)S(1)}, u32[]{:S(2)}, u32[]{:S(2)}) collective-permute-start(bf16[64,2048]{1,0:T(8,128)(2,1)S(1)} %copy-done), channel_id=1, source_target_pairs={{0,6},{1,7},{2,0},{3,1},{4,2},{5,3},{6,4},{7,5},{8,14},{9,15},{10,... | collective-permute-start | bytes 786440 | tf_op jit(solution)/shard_map/ppermute | solution.py:168
  11.7 1.9 %collective-permute-done.3.high_ref = bf16[256,128]{1,0:T(8,128)(2,1)S(1)} collective-permute-done((bf16[256,128]{1,0:T(8,128)(2,1)S(1)}, bf16[256,128]{1,0:T(8,128)(2,1)S(1)}, u32[]{:S(2)}, u32[]{:S(2)}) %collective-permute-start.3) | collective-permute-done | bytes 65568 | tf_op jit(solution)/shard_map/ppermute | solution.py:197
  13.6 0.0 collective-permute-done.1.refs_4_
  13.6 0.0 collective-permute-done.refs_1_
  13.6 2.7 %collective-permute-start.6 = (bf16[64,2048]{1,0:T(8,128)(2,1)S(1)}, bf16[64,2048]{1,0:T(8,128)(2,1)S(1)}, u32[]{:S(2)}, u32[]{:S(2)}) collective-permute-start(bf16[64,2048]{1,0:T(8,128)(2,1)S(1)} %collective-permute-done.1.refs_4_), channel_id=1, source_target_pairs={{0,1},{1,0},{2,3},{3,2},{4,5},{5,4},{6,7},{7,6},{8,9},{9,8},{10,11... | collective-permute-start | bytes 786440 | tf_op jit(solution)/shard_map/ppermute | solution.py:171
  16.3 0.0 collective-permute-start.8
  16.3 2.0 %collective-permute-start.5 = (bf16[64,2048]{1,0:T(8,128)(2,1)S(1)}, bf16[64,2048]{1,0:T(8,128)(2,1)S(1)}, u32[]{:S(2)}, u32[]{:S(2)}) collective-permute-start(bf16[64,2048]{1,0:T(8,128)(2,1)S(1)} %collective-permute-done.refs_1_), channel_id=1, source_target_pairs={{0,6},{1,7},{2,0},{3,1},{4,2},{5,3},{6,4},{7,5},{8,14},{9,15},{10,... | collective-permute-start | bytes 786440 | tf_op jit(solution)/shard_map/ppermute | solution.py:168
  18.3 0.0 copy-start.3
  18.3 0.7 copy-done.3
  18.9 0.0 copy-start.1
  18.9 1.2 %copy-done.1 = bf16[256,2048]{1,0:T(8,128)(2,1)S(1)} copy-done((bf16[256,2048]{1,0:T(8,128)(2,1)S(1)}, bf16[256,2048]{1,0:T(8,128)(2,1)}, u32[]{:S(2)}) %copy-start.1) | copy-done | bytes 1048600
  20.2 0.0 copy-start.2
  20.2 0.9 %copy-done.2 = s32[256,128]{1,0:T(8,128)S(1)} copy-done((s32[256,128]{1,0:T(8,128)S(1)}, s32[256,128]{1,0:T(8,128)}, u32[]{:S(2)}) %copy-start.2) | copy-done | bytes 131096
  21.1 1.3 %shard_map.59 = (bf16[256,2048]{1,0:T(8,128)(2,1)S(1)}, s32[256,128]{1,0:T(8,128)S(1)}) custom-call(s32[4]{0:T(128)S(1)} %copy-done.3, s32[1]{0:T(128)} %bitcast.spec_ref, s32[1]{0:T(128)} %bitcast.1.bucket_ref, bf16[256,2048]{1,0:T(8,128)(2,1)S(1)} %copy-done.1, bf16[256,128]{1,0:T(8,128)(2,1)S(1)} %collective-permute-done.2.low_ref, ...), custom_call_target="tpu_custom_call" | custom-call | flops 536870912 | bytes 2097152 | tf_op jit(solution)/shard_map/pallas_call | solution.py:45
  22.4 0.0 collective-permute-done.7.refs_6_
  22.4 0.0 collective-permute-done.4.refs_2_
  22.4 0.5 collective-permute-done.6.refs_5_
  22.9 2.4 %collective-permute-done.8.refs_7_ = bf16[64,2048]{1,0:T(8,128)(2,1)S(1)} collective-permute-done((bf16[64,2048]{1,0:T(8,128)(2,1)S(1)}, bf16[64,2048]{1,0:T(8,128)(2,1)S(1)}, u32[]{:S(2)}, u32[]{:S(2)}) %collective-permute-start.8) | collective-permute-done | bytes 262176 | tf_op jit(solution)/shard_map/ppermute | solution.py:168
  25.2 0.0 collective-permute-done.5.refs_3_
  25.3 0.8 %shard_map.60 = (f32[16,8,512]{2,1,0:T(8,128)S(1)}, f32[16,8,512]{2,1,0:T(8,128)S(1)}) custom-call(s32[1]{0:T(128)} %bitcast.2.core_ref, bf16[256,2048]{1,0:T(8,128)(2,1)S(1)} %get-tuple-element.20.processed_ref, bf16[64,2048]{1,0:T(8,128)(2,1)S(1)} %copy-done, bf16[64,2048]{1,0:T(8,128)(2,1)S(1)} %collective-permute-done.refs_1_, ...), custom_call_target="tpu_custom_call" | custom-call | flops 536870912 | bytes 3145728 | tf_op jit(solution)/shard_map/pallas_call | solution.py:75
  26.1 0.1 collective-permute-start.9
  26.2 1.5 %collective-permute-done.9 = f32[16,8,512]{2,1,0:T(8,128)S(1)} collective-permute-done((f32[16,8,512]{2,1,0:T(8,128)S(1)}, f32[16,8,512]{2,1,0:T(8,128)S(1)}, u32[]{:S(2)}, u32[]{:S(2)}) %collective-permute-start.9) | collective-permute-done | bytes 262176 | tf_op jit(solution)/shard_map/ppermute | solution.py:203
  27.7 17.9 %all_to_all.15.parts_ref = bf16[16,8,512]{2,1,0:T(8,128)(2,1)S(1)} all-to-all(bf16[16,8,512]{2,1,0:T(8,128)(2,1)S(1)} %add_convert_fusion), channel_id=1, replica_groups={{0,16,32,48,64,80,96,112,128,144,160,176,192,208,224,240},{8,24,40,56,7..., dimensions={0} | all-to-all | bytes 262144 | tf_op jit(solution)/shard_map/all_to_all | solution.py:206
  45.6 0.2 shard_map.61
  45.8 12.5 %all_to_all.16.value_ref = bf16[32,8,128]{2,1,0:T(8,128)(2,1)S(1)} all-to-all(bf16[32,8,128]{2,1,0:T(8,128)(2,1)S(1)} %shard_map.61), channel_id=1, replica_groups=mesh['spec'=32,'bucket'=8] {'spec'}, dimensions={0} | all-to-all | bytes 131072 | tf_op jit(solution)/shard_map/all_to_all | solution.py:208
  58.3 0.3 shard_map.62
  58.7 14.4 %all_to_all.17.evidence_ref = f32[8,2,128]{2,1,0:T(2,128)S(1)} all-to-all(f32[8,2,128]{2,1,0:T(2,128)S(1)} %bitcast.5), channel_id=1, replica_groups=mesh['spec'=32,'bucket'=8] {'bucket'}, dimensions={0} | all-to-all | bytes 16384 | tf_op jit(solution)/shard_map/all_to_all | solution.py:213
  73.1 0.7 shard_map.63
  (1 shorter events, 0.0 us)
Async XLA Ops:
  0.6 1.0 %copy-start = (bf16[64,2048]{1,0:T(8,128)(2,1)S(1)}, bf16[64,2048]{1,0:T(8,128)(2,1)}, u32[]{:S(2)}) copy-start(bf16[64,2048]{1,0:T(8,128)(2,1)} %refs_0_) | copy-start | bytes 786436
  1.6 11.9 %collective-permute-start.1 = (bf16[64,2048]{1,0:T(8,128)(2,1)S(1)}, bf16[64,2048]{1,0:T(8,128)(2,1)S(1)}, u32[]{:S(2)}, u32[]{:S(2)}) collective-permute-start(bf16[64,2048]{1,0:T(8,128)(2,1)S(1)} %copy-done), channel_id=1, source_target_pairs={{0,4},{1,5},{2,6},{3,7},{4,0},{5,1},{6,2},{7,3},{8,12},{9,13},{10,... | collective-permute-start | bytes 786440 | tf_op jit(solution)/shard_map/ppermute | solution.py:168
  4.0 9.6 %collective-permute-start = (bf16[64,2048]{1,0:T(8,128)(2,1)S(1)}, bf16[64,2048]{1,0:T(8,128)(2,1)S(1)}, u32[]{:S(2)}, u32[]{:S(2)}) collective-permute-start(bf16[64,2048]{1,0:T(8,128)(2,1)S(1)} %copy-done), channel_id=1, source_target_pairs={{0,1},{1,0},{2,3},{3,2},{4,5},{5,4},{6,7},{7,6},{8,9},{9,8},{10,11... | collective-permute-start | bytes 786440 | tf_op jit(solution)/shard_map/ppermute | solution.py:171
  7.0 2.7 %collective-permute-start.2 = (bf16[256,128]{1,0:T(8,128)(2,1)S(1)}, bf16[256,128]{1,0:T(8,128)(2,1)S(1)}, u32[]{:S(2)}, u32[]{:S(2)}) collective-permute-start(bf16[256,128]{1,0:T(8,128)(2,1)S(1)} %get-tuple-element.16), channel_id=1, source_target_pairs={{0,8},{8,16},{16,24},{24,32},{32,40},{40,48},{48,56},{56,64},{64,7... | collective-permute-start | bytes 196616 | tf_op jit(solution)/shard_map/ppermute | solution.py:196
  8.3 5.3 %collective-permute-start.3 = (bf16[256,128]{1,0:T(8,128)(2,1)S(1)}, bf16[256,128]{1,0:T(8,128)(2,1)S(1)}, u32[]{:S(2)}, u32[]{:S(2)}) collective-permute-start(bf16[256,128]{1,0:T(8,128)(2,1)S(1)} %get-tuple-element.17), channel_id=1, source_target_pairs={{8,0},{16,8},{24,16},{32,24},{40,32},{48,40},{56,48},{64,56},{72,6... | collective-permute-start | bytes 196616 | tf_op jit(solution)/shard_map/ppermute | solution.py:197
  9.6 12.8 %collective-permute-start.7 = (bf16[64,2048]{1,0:T(8,128)(2,1)S(1)}, bf16[64,2048]{1,0:T(8,128)(2,1)S(1)}, u32[]{:S(2)}, u32[]{:S(2)}) collective-permute-start(bf16[64,2048]{1,0:T(8,128)(2,1)S(1)} %copy-done), channel_id=1, source_target_pairs={{0,2},{1,3},{2,4},{3,5},{4,6},{5,7},{6,0},{7,1},{8,10},{9,11},{10,... | collective-permute-start | bytes 786440 | tf_op jit(solution)/shard_map/ppermute | solution.py:168
  9.7 12.7 %collective-permute-start.4 = (bf16[64,2048]{1,0:T(8,128)(2,1)S(1)}, bf16[64,2048]{1,0:T(8,128)(2,1)S(1)}, u32[]{:S(2)}, u32[]{:S(2)}) collective-permute-start(bf16[64,2048]{1,0:T(8,128)(2,1)S(1)} %copy-done), channel_id=1, source_target_pairs={{0,6},{1,7},{2,0},{3,1},{4,2},{5,3},{6,4},{7,5},{8,14},{9,15},{10,... | collective-permute-start | bytes 786440 | tf_op jit(solution)/shard_map/ppermute | solution.py:168
  13.6 9.3 %collective-permute-start.6 = (bf16[64,2048]{1,0:T(8,128)(2,1)S(1)}, bf16[64,2048]{1,0:T(8,128)(2,1)S(1)}, u32[]{:S(2)}, u32[]{:S(2)}) collective-permute-start(bf16[64,2048]{1,0:T(8,128)(2,1)S(1)} %collective-permute-done.1.refs_4_), channel_id=1, source_target_pairs={{0,1},{1,0},{2,3},{3,2},{4,5},{5,4},{6,7},{7,6},{8,9},{9,8},{10,11... | collective-permute-start | bytes 786440 | tf_op jit(solution)/shard_map/ppermute | solution.py:171
  16.3 9.0 %collective-permute-start.8 = (bf16[64,2048]{1,0:T(8,128)(2,1)S(1)}, bf16[64,2048]{1,0:T(8,128)(2,1)S(1)}, u32[]{:S(2)}, u32[]{:S(2)}) collective-permute-start(bf16[64,2048]{1,0:T(8,128)(2,1)S(1)} %collective-permute-done.refs_1_), channel_id=1, source_target_pairs={{0,2},{1,3},{2,4},{3,5},{4,6},{5,7},{6,0},{7,1},{8,10},{9,11},{10,... | collective-permute-start | bytes 786440 | tf_op jit(solution)/shard_map/ppermute | solution.py:168
  16.3 9.0 %collective-permute-start.5 = (bf16[64,2048]{1,0:T(8,128)(2,1)S(1)}, bf16[64,2048]{1,0:T(8,128)(2,1)S(1)}, u32[]{:S(2)}, u32[]{:S(2)}) collective-permute-start(bf16[64,2048]{1,0:T(8,128)(2,1)S(1)} %collective-permute-done.refs_1_), channel_id=1, source_target_pairs={{0,6},{1,7},{2,0},{3,1},{4,2},{5,3},{6,4},{7,5},{8,14},{9,15},{10,... | collective-permute-start | bytes 786440 | tf_op jit(solution)/shard_map/ppermute | solution.py:168
  18.3 0.7 copy-start.3
  18.9 1.2 %copy-start.1 = (bf16[256,2048]{1,0:T(8,128)(2,1)S(1)}, bf16[256,2048]{1,0:T(8,128)(2,1)}, u32[]{:S(2)}) copy-start(bf16[256,2048]{1,0:T(8,128)(2,1)} %spectra_ref.1) | copy-start | bytes 3145732
  20.2 0.9 %copy-start.2 = (s32[256,128]{1,0:T(8,128)S(1)}, s32[256,128]{1,0:T(8,128)}, u32[]{:S(2)}) copy-start(s32[256,128]{1,0:T(8,128)} %cand_ref.1) | copy-start | bytes 393220
  26.1 1.6 %collective-permute-start.9 = (f32[16,8,512]{2,1,0:T(8,128)S(1)}, f32[16,8,512]{2,1,0:T(8,128)S(1)}, u32[]{:S(2)}, u32[]{:S(2)}) collective-permute-start(f32[16,8,512]{2,1,0:T(8,128)S(1)} %get-tuple-element.24), channel_id=1, source_target_pairs={{0,8},{8,0},{16,24},{24,16},{32,40},{40,32},{48,56},{56,48},{64,72... | collective-permute-start | bytes 786440 | tf_op jit(solution)/shard_map/ppermute | solution.py:203

commit v7 on v6

--- a/solution.py
+++ b/solution.py
@@ -19,12 +19,14 @@
     return pltpu.CompilerParams(vmem_limit_bytes=16 * 1024 * 1024)
 
 
-def window_kernel(half_ref, spec_ref, bucket_ref, spectra_ref, low_ref, high_ref, cand_ref, out_ref, near_ref, wide_ref):
+def window_kernel(half_ref, spec_ref, bucket_ref, spectra_ref, inner_ref, outer_ref, cand_ref, out_ref, near_ref, wide_ref):
     near_ref[...] = cand_ref[...]
     bins = spectra_ref.shape[1]
-    wide_ref[:, :SIDE] = low_ref[...]
+    inner, outer = inner_ref[...], outer_ref[...]
+    even_core = spec_ref[0] % 2 == 0
+    wide_ref[:, :SIDE] = jnp.where(even_core, outer, inner)
     wide_ref[:, SIDE : SIDE + bins] = spectra_ref[...]
-    wide_ref[:, SIDE + bins :] = high_ref[...]
+    wide_ref[:, SIDE + bins :] = jnp.where(even_core, inner, outer)
     taken = TILE + 2 * SIDE
     source = lax.broadcasted_iota(jnp.int32, (taken, TILE), 0) - SIDE
     target = lax.broadcasted_iota(jnp.int32, (taken, TILE), 1)
@@ -40,7 +42,7 @@
             out_ref[:, at : at + TILE] = (middle - sums / divisor).astype(jnp.bfloat16)
 
 
-def windowed(half, where, spectra, low, high, cand):
+def windowed(half, where, spectra, inner, outer, cand):
     rows, bins = spectra.shape
     return pl.pallas_call(
         window_kernel,
@@ -50,7 +52,7 @@
         scratch_shapes=[pltpu.VMEM((rows, bins + 2 * SIDE), jnp.bfloat16)],
         compiler_params=params(),
         cost_estimate=pl.CostEstimate(flops=2 * rows * bins * 512, bytes_accessed=4 * rows * bins, transcendentals=0),
-    )(half, *where, spectra, low, high, cand)
+    )(half, *where, spectra, inner, outer, cand)
 
 
 def score_kernel(core_ref, processed_ref, *refs):
@@ -161,21 +163,13 @@
     )(values, evidence)
 
 
-def from_all_buckets(shard, low, high):
+def swapped_along_x(shard):
+    return lax.ppermute(shard, "bucket", [(b, b ^ 1) for b in range(lax.axis_size("bucket"))])
+
+
+def shifted_along_y(shard, step):
     count = lax.axis_size("bucket")
-
-    def along_y(value, step):
-        return lax.ppermute(value, "bucket", [(b, (b - 2 * step) % count) for b in range(count)])
-
-    def along_x(value):
-        return lax.ppermute(value, "bucket", [(b, b ^ 1) for b in range(count)])
-
-    beside = along_x(shard)
-    above, below, across = along_y(shard, 1), along_y(shard, 3), along_y(shard, 2)
-    beside, across, low, high = lax.optimization_barrier((beside, across, low, high))
-    above_beside, below_beside = along_y(beside, 1), along_y(beside, 3)
-    across_beside = along_x(across)
-    return low, high, [shard, beside, above, above_beside, across, across_beside, below, below_beside]
+    return lax.ppermute(shard, "bucket", [(b, (b - 2 * step) % count) for b in range(count)])
 
 
 def on_device(spectra, theory, cand, half):
@@ -189,18 +183,24 @@
     where = spec.reshape(1), bucket.reshape(1)
     core = (spec % 2).reshape(1)
 
-    theory, low, high = lax.optimization_barrier((theory, spectra[:, -SIDE:], spectra[:, :SIDE]))
-
-    forward = [(i, i + 1) for i in range(spec_count - 1)]
-    backward = [(target, source) for source, target in forward]
-    low = lax.ppermute(low, "spec", forward)
-    high = lax.ppermute(high, "spec", backward)
-    low, high, pieces = from_all_buckets(theory, low, high)
-    processed, cand = windowed(half, where, spectra, low, high, cand)
+    inside = [(i, i ^ 1) for i in range(spec_count)]
+    outside = [(i, i + 1) for i in range(1, spec_count - 1, 2)]
+    outside += [(target, source) for source, target in outside]
+    first, last = spectra[:, :SIDE], spectra[:, -SIDE:]
+    beside = swapped_along_x(theory)
+    above, below = shifted_along_y(theory, 1), shifted_along_y(theory, 3)
+    across = shifted_along_y(theory, 2)
+    even_core = spec % 2 == 0
+    inner = lax.ppermute(jnp.where(even_core, last, first), "spec", inside)
+    outer = lax.ppermute(jnp.where(even_core, first, last), "spec", outside)
+    above_beside, below_beside = shifted_along_y(beside, 1), shifted_along_y(beside, 3)
+    across_beside = swapped_along_x(across)
+    processed, cand = windowed(half, where, spectra, inner, outer, cand)
+    pieces = [theory, beside, above, above_beside, across, across_beside, below, below_beside]
 
     own = row_count // spec_count
     keep, send = scored(core, processed, pieces, own)
-    got = lax.ppermute(send, "spec", [(i, i ^ 1) for i in range(spec_count)])
+    got = lax.ppermute(send, "spec", inside)
     chip = (keep + got).astype(jnp.bfloat16)
     groups = [list(range(c, spec_count, 2)) for c in range(2)]
     parts = lax.all_to_all(chip, "spec", 0, 0, axis_index_groups=groups, tiled=True)

time: 74.1 us -> 71.6 us (0.966)
  blocking collectives: 44.8 us -> 40.9 us
  waiting for transfers between devices: 6.28 us -> 8.53 us
  local copies, waits for them, and re-layouts: 3.79 us -> 2.79 us
  other arithmetic: 0.04 us -> 0.92 us
    all_to_all x1, blocking collectives: 14.4 us -> 11.9 us  [on_device(): lax.all_to_all(evidence.reshape(bucket_count, share // bucket_count, cand...]
    ppermute x10, waiting for transfers between devices: 6.28 us -> 8.53 us  [the longest x5 5.89 us: shifted_along_y(): lax.ppermute(shard, 'bucket', [(b, (b - 2 * step) % count) for b in range...]
    all_to_all x1, blocking collectives: 17.9 us -> 16.5 us  [on_device(): lax.all_to_all(chip, 'spec', 0, 0, axis_index_groups=groups, tiled=True)]
    slice x1 -> x0, local copies, waits for them, and re-layouts: 0.93 us -> none  [on_device(): spectra[:, :SIDE]]
    select_n x0 -> x1, other arithmetic: none -> 0.89 us  [on_device(): outer = lax.ppermute(jnp.where(even_core, first, last), 'spec', outside)]
  transfers between devices with their start and end apart: 10 -> 10, of which waited for: 4 -> 5; matrix products, arithmetic and copies ran while one was open for 0% -> 1% of each run, Pallas kernels for 2% -> 2%
where the time goes in v7:
time: 71.6 us; the launch traced here: 71.3 us
  blocking collectives  40.9 us (57%)
  starting transfers between devices  14.1 us (20%)
  waiting for transfers between devices  8.53 us (12%)
  Pallas kernels  3.31 us (5%)
  local copies, waits for them, and re-layouts  2.79 us (4%)
  other arithmetic  0.92 us (1%)
    all_to_all x1, blocking collectives, on_device(): lax.all_to_all(chip, 'spec', 0, 0, axis_index_groups=groups, tiled=True)  16.5 us
    all_to_all x1, blocking collectives, on_device(): values = lax.all_to_all(copies, 'spec', 0, 0, tiled=True)  12.5 us
    all_to_all x1, blocking collectives, on_device(): lax.all_to_all(evidence.reshape(bucket_count, share // bucket_count, cand...  11.9 us
    ppermute x5, starting transfers between devices, shifted_along_y(): lax.ppermute(shard, 'bucket', [(b, (b - 2 * step) % count) for b in range...  6.44 us
    ppermute x5, waiting for transfers between devices, shifted_along_y(): lax.ppermute(shard, 'bucket', [(b, (b - 2 * step) % count) for b in range...  5.89 us
    ppermute x2, starting transfers between devices, swapped_along_x(): lax.ppermute(shard, 'bucket', [(b, b ^ 1) for b in range(lax.axis_size('b...  3.53 us
    ppermute x1, starting transfers between devices, on_device(): inner = lax.ppermute(jnp.where(even_core, last, first), 'spec', inside)  3.36 us
    unnamed x8, local copies, waits for them, and re-layouts  2.79 us
  transfers between devices with their start and end apart: 10, of which 5 were waited for; matrix products, arithmetic and copies ran while one was open for 1% of the time, Pallas kernels for 2%

profile of v7, /device:TPU:8, one launch (start us, length us, event | category | flops | bytes accessed | tf_op | source)
XLA Modules:
  0.0 71.3 jit_solution(12306244748589339324)
XLA Ops:
  0.6 0.0 copy-start
  0.6 2.4 %collective-permute-start.5 = (bf16[64,2048]{1,0:T(8,128)(2,1)}, bf16[64,2048]{1,0:T(8,128)(2,1)S(1)}, u32[]{:S(2)}, u32[]{:S(2)}) collective-permute-start(bf16[64,2048]{1,0:T(8,128)(2,1)} %refs_0_.1), channel_id=1, source_target_pairs={{0,4},{1,5},{2,6},{3,7},{4,0},{5,1},{6,2},{7,3},{8,12},{9,13},{10,... | collective-permute-start | bytes 786440 | tf_op jit(solution)/shard_map/ppermute | solution.py:172
  3.0 3.0 %collective-permute-start.2 = (bf16[64,2048]{1,0:T(8,128)(2,1)}, bf16[64,2048]{1,0:T(8,128)(2,1)S(1)}, u32[]{:S(2)}, u32[]{:S(2)}) collective-permute-start(bf16[64,2048]{1,0:T(8,128)(2,1)} %refs_0_.1), channel_id=1, source_target_pairs={{0,1},{1,0},{2,3},{3,2},{4,5},{5,4},{6,7},{7,6},{8,9},{9,8},{10,11... | collective-permute-start | bytes 786440 | tf_op jit(solution)/shard_map/ppermute | solution.py:167
  6.0 0.9 %broadcast_select_fusion = (bf16[256,128]{1,0:T(8,128)(2,1)S(1)}, bf16[256,128]{1,0:T(8,128)(2,1)S(1)}) fusion(pred[]{:T(512)S(6)} %eq.6, bf16[256,2048]{1,0:T(8,128)(2,1)} %spectra_ref.1), kind=kLoop, calls=%fused_computation.1 | loop fusion | flops 65536 | bytes 262145 | tf_op jit(solution)/shard_map/jit(_where)/select_n | solution.py:195
  6.9 0.7 collective-permute-start.1
  7.6 3.4 %collective-permute-start = (bf16[256,128]{1,0:T(8,128)(2,1)S(1)}, bf16[256,128]{1,0:T(8,128)(2,1)S(1)}, u32[]{:S(2)}, u32[]{:S(2)}) collective-permute-start(bf16[256,128]{1,0:T(8,128)(2,1)S(1)} %get-tuple-element.15), channel_id=1, source_target_pairs={{0,8},{8,0},{16,24},{24,16},{32,40},{40,32},{48,56},{56,48},{64,72... | collective-permute-start | bytes 196616 | tf_op jit(solution)/shard_map/ppermute | solution.py:194
  11.0 0.0 copy-done
  11.0 1.3 %collective-permute-start.3 = (bf16[64,2048]{1,0:T(8,128)(2,1)S(1)}, bf16[64,2048]{1,0:T(8,128)(2,1)S(1)}, u32[]{:S(2)}, u32[]{:S(2)}) collective-permute-start(bf16[64,2048]{1,0:T(8,128)(2,1)S(1)} %copy-done), channel_id=1, source_target_pairs={{0,6},{1,7},{2,0},{3,1},{4,2},{5,3},{6,4},{7,5},{8,14},{9,15},{10,... | collective-permute-start | bytes 786440 | tf_op jit(solution)/shard_map/ppermute | solution.py:172
  12.3 0.0 collective-permute-done.1.outer_ref
  12.3 0.7 collective-permute-start.7
  13.0 0.0 collective-permute-done.5.refs_4_
  13.0 0.5 collective-permute-start.6
  13.5 0.0 collective-permute-done.2.refs_1_
  13.5 1.6 %collective-permute-start.8 = (bf16[64,2048]{1,0:T(8,128)(2,1)S(1)}, bf16[64,2048]{1,0:T(8,128)(2,1)S(1)}, u32[]{:S(2)}, u32[]{:S(2)}) collective-permute-start(bf16[64,2048]{1,0:T(8,128)(2,1)S(1)} %collective-permute-done.2.refs_1_), channel_id=1, source_target_pairs={{0,2},{1,3},{2,4},{3,5},{4,6},{5,7},{6,0},{7,1},{8,10},{9,11},{10,... | collective-permute-start | bytes 786440 | tf_op jit(solution)/shard_map/ppermute | solution.py:172
  15.1 0.0 collective-permute-done.inner_ref
  15.1 0.5 collective-permute-start.4
  15.5 0.0 copy-start.3
  15.6 0.7 copy-done.3
  16.2 0.0 copy-start.1
  16.2 1.2 %copy-done.1 = bf16[256,2048]{1,0:T(8,128)(2,1)S(1)} copy-done((bf16[256,2048]{1,0:T(8,128)(2,1)S(1)}, bf16[256,2048]{1,0:T(8,128)(2,1)}, u32[]{:S(2)}) %copy-start.1) | copy-done | bytes 1048600
  17.4 0.0 copy-start.2
  17.4 0.9 %copy-done.2 = s32[256,128]{1,0:T(8,128)S(1)} copy-done((s32[256,128]{1,0:T(8,128)S(1)}, s32[256,128]{1,0:T(8,128)}, u32[]{:S(2)}) %copy-start.2) | copy-done | bytes 131096
  18.3 1.3 %shard_map.59 = (bf16[256,2048]{1,0:T(8,128)(2,1)S(1)}, s32[256,128]{1,0:T(8,128)S(1)}) custom-call(s32[4]{0:T(128)S(1)} %copy-done.3, s32[1]{0:T(128)} %bitcast.spec_ref, s32[1]{0:T(128)} %bitcast.1.bucket_ref, bf16[256,2048]{1,0:T(8,128)(2,1)S(1)} %copy-done.1, bf16[256,128]{1,0:T(8,128)(2,1)S(1)} %collective-permute-done.inner_ref, ...), custom_call_target="tpu_custom_call" | custom-call | flops 536870912 | bytes 2097152 | tf_op jit(solution)/shard_map/pallas_call | solution.py:47
  19.6 0.5 collective-permute-done.3.refs_2_
  20.1 1.3 %collective-permute-done.7.refs_6_ = bf16[64,2048]{1,0:T(8,128)(2,1)S(1)} collective-permute-done((bf16[64,2048]{1,0:T(8,128)(2,1)S(1)}, bf16[64,2048]{1,0:T(8,128)(2,1)S(1)}, u32[]{:S(2)}, u32[]{:S(2)}) %collective-permute-start.7) | collective-permute-done | bytes 262176 | tf_op jit(solution)/shard_map/ppermute | solution.py:172
  21.4 1.1 %collective-permute-done.6.refs_5_ = bf16[64,2048]{1,0:T(8,128)(2,1)S(1)} collective-permute-done((bf16[64,2048]{1,0:T(8,128)(2,1)S(1)}, bf16[64,2048]{1,0:T(8,128)(2,1)S(1)}, u32[]{:S(2)}, u32[]{:S(2)}) %collective-permute-start.6) | collective-permute-done | bytes 262176 | tf_op jit(solution)/shard_map/ppermute | solution.py:167
  22.5 4.1 %collective-permute-done.8.refs_7_ = bf16[64,2048]{1,0:T(8,128)(2,1)S(1)} collective-permute-done((bf16[64,2048]{1,0:T(8,128)(2,1)S(1)}, bf16[64,2048]{1,0:T(8,128)(2,1)S(1)}, u32[]{:S(2)}, u32[]{:S(2)}) %collective-permute-start.8) | collective-permute-done | bytes 262176 | tf_op jit(solution)/shard_map/ppermute | solution.py:172
  26.6 0.0 collective-permute-done.4.refs_3_
  26.7 0.8 %shard_map.60 = (f32[16,8,512]{2,1,0:T(8,128)S(1)}, f32[16,8,512]{2,1,0:T(8,128)S(1)}) custom-call(s32[1]{0:T(128)} %bitcast.2.core_ref, bf16[256,2048]{1,0:T(8,128)(2,1)S(1)} %get-tuple-element.8.processed_ref, bf16[64,2048]{1,0:T(8,128)(2,1)S(1)} %copy-done, bf16[64,2048]{1,0:T(8,128)(2,1)S(1)} %collective-permute-done.2.refs_1_, ...), custom_call_target="tpu_custom_call" | custom-call | flops 536870912 | bytes 3145728 | tf_op jit(solution)/shard_map/pallas_call | solution.py:77
  27.5 0.1 collective-permute-start.9
  27.6 1.5 %collective-permute-done.9 = f32[16,8,512]{2,1,0:T(8,128)S(1)} collective-permute-done((f32[16,8,512]{2,1,0:T(8,128)S(1)}, f32[16,8,512]{2,1,0:T(8,128)S(1)}, u32[]{:S(2)}, u32[]{:S(2)}) %collective-permute-start.9) | collective-permute-done | bytes 262176 | tf_op jit(solution)/shard_map/ppermute | solution.py:203
  29.1 16.5 %all_to_all.15.parts_ref = bf16[16,8,512]{2,1,0:T(8,128)(2,1)S(1)} all-to-all(bf16[16,8,512]{2,1,0:T(8,128)(2,1)S(1)} %add_convert_fusion), channel_id=1, replica_groups={{0,16,32,48,64,80,96,112,128,144,160,176,192,208,224,240},{8,24,40,56,7..., dimensions={0} | all-to-all | bytes 262144 | tf_op jit(solution)/shard_map/all_to_all | solution.py:206
  45.7 0.2 shard_map.61
  45.9 12.5 %all_to_all.16.value_ref = bf16[32,8,128]{2,1,0:T(8,128)(2,1)S(1)} all-to-all(bf16[32,8,128]{2,1,0:T(8,128)(2,1)S(1)} %shard_map.61), channel_id=1, replica_groups=mesh['spec'=32,'bucket'=8] {'spec'}, dimensions={0} | all-to-all | bytes 131072 | tf_op jit(solution)/shard_map/all_to_all | solution.py:208
  58.4 0.3 shard_map.62
  58.7 11.9 %all_to_all.17.evidence_ref = f32[8,2,128]{2,1,0:T(2,128)S(1)} all-to-all(f32[8,2,128]{2,1,0:T(2,128)S(1)} %bitcast.5), channel_id=1, replica_groups=mesh['spec'=32,'bucket'=8] {'bucket'}, dimensions={0} | all-to-all | bytes 16384 | tf_op jit(solution)/shard_map/all_to_all | solution.py:213
  70.6 0.7 shard_map.63
  (1 shorter events, 0.0 us)
Async XLA Ops:
  0.6 10.3 %copy-start = (bf16[64,2048]{1,0:T(8,128)(2,1)S(1)}, bf16[64,2048]{1,0:T(8,128)(2,1)}, u32[]{:S(2)}) copy-start(bf16[64,2048]{1,0:T(8,128)(2,1)} %refs_0_.1) | copy-start | bytes 786436
  0.6 12.4 %collective-permute-start.5 = (bf16[64,2048]{1,0:T(8,128)(2,1)}, bf16[64,2048]{1,0:T(8,128)(2,1)S(1)}, u32[]{:S(2)}, u32[]{:S(2)}) collective-permute-start(bf16[64,2048]{1,0:T(8,128)(2,1)} %refs_0_.1), channel_id=1, source_target_pairs={{0,4},{1,5},{2,6},{3,7},{4,0},{5,1},{6,2},{7,3},{8,12},{9,13},{10,... | collective-permute-start | bytes 786440 | tf_op jit(solution)/shard_map/ppermute | solution.py:172
  3.0 10.5 %collective-permute-start.2 = (bf16[64,2048]{1,0:T(8,128)(2,1)}, bf16[64,2048]{1,0:T(8,128)(2,1)S(1)}, u32[]{:S(2)}, u32[]{:S(2)}) collective-permute-start(bf16[64,2048]{1,0:T(8,128)(2,1)} %refs_0_.1), channel_id=1, source_target_pairs={{0,1},{1,0},{2,3},{3,2},{4,5},{5,4},{6,7},{7,6},{8,9},{9,8},{10,11... | collective-permute-start | bytes 786440 | tf_op jit(solution)/shard_map/ppermute | solution.py:167
  6.9 5.4 %collective-permute-start.1 = (bf16[256,128]{1,0:T(8,128)(2,1)S(1)}, bf16[256,128]{1,0:T(8,128)(2,1)S(1)}, u32[]{:S(2)}, u32[]{:S(2)}) collective-permute-start(bf16[256,128]{1,0:T(8,128)(2,1)S(1)} %get-tuple-element.14), channel_id=1, source_target_pairs={{8,16},{24,32},{40,48},{56,64},{72,80},{88,96},{104,112},{120,128}... | collective-permute-start | bytes 196616 | tf_op jit(solution)/shard_map/ppermute | solution.py:195
  7.6 7.5 %collective-permute-start = (bf16[256,128]{1,0:T(8,128)(2,1)S(1)}, bf16[256,128]{1,0:T(8,128)(2,1)S(1)}, u32[]{:S(2)}, u32[]{:S(2)}) collective-permute-start(bf16[256,128]{1,0:T(8,128)(2,1)S(1)} %get-tuple-element.15), channel_id=1, source_target_pairs={{0,8},{8,0},{16,24},{24,16},{32,40},{40,32},{48,56},{56,48},{64,72... | collective-permute-start | bytes 196616 | tf_op jit(solution)/shard_map/ppermute | solution.py:194
  11.0 9.2 %collective-permute-start.3 = (bf16[64,2048]{1,0:T(8,128)(2,1)S(1)}, bf16[64,2048]{1,0:T(8,128)(2,1)S(1)}, u32[]{:S(2)}, u32[]{:S(2)}) collective-permute-start(bf16[64,2048]{1,0:T(8,128)(2,1)S(1)} %copy-done), channel_id=1, source_target_pairs={{0,6},{1,7},{2,0},{3,1},{4,2},{5,3},{6,4},{7,5},{8,14},{9,15},{10,... | collective-permute-start | bytes 786440 | tf_op jit(solution)/shard_map/ppermute | solution.py:172
  12.3 9.1 %collective-permute-start.7 = (bf16[64,2048]{1,0:T(8,128)(2,1)S(1)}, bf16[64,2048]{1,0:T(8,128)(2,1)S(1)}, u32[]{:S(2)}, u32[]{:S(2)}) collective-permute-start(bf16[64,2048]{1,0:T(8,128)(2,1)S(1)} %copy-done), channel_id=1, source_target_pairs={{0,2},{1,3},{2,4},{3,5},{4,6},{5,7},{6,0},{7,1},{8,10},{9,11},{10,... | collective-permute-start | bytes 786440 | tf_op jit(solution)/shard_map/ppermute | solution.py:172
  13.0 9.5 %collective-permute-start.6 = (bf16[64,2048]{1,0:T(8,128)(2,1)S(1)}, bf16[64,2048]{1,0:T(8,128)(2,1)S(1)}, u32[]{:S(2)}, u32[]{:S(2)}) collective-permute-start(bf16[64,2048]{1,0:T(8,128)(2,1)S(1)} %collective-permute-done.5.refs_4_), channel_id=1, source_target_pairs={{0,1},{1,0},{2,3},{3,2},{4,5},{5,4},{6,7},{7,6},{8,9},{9,8},{10,11... | collective-permute-start | bytes 786440 | tf_op jit(solution)/shard_map/ppermute | solution.py:167
  13.5 13.1 %collective-permute-start.8 = (bf16[64,2048]{1,0:T(8,128)(2,1)S(1)}, bf16[64,2048]{1,0:T(8,128)(2,1)S(1)}, u32[]{:S(2)}, u32[]{:S(2)}) collective-permute-start(bf16[64,2048]{1,0:T(8,128)(2,1)S(1)} %collective-permute-done.2.refs_1_), channel_id=1, source_target_pairs={{0,2},{1,3},{2,4},{3,5},{4,6},{5,7},{6,0},{7,1},{8,10},{9,11},{10,... | collective-permute-start | bytes 786440 | tf_op jit(solution)/shard_map/ppermute | solution.py:172
  15.1 11.6 %collective-permute-start.4 = (bf16[64,2048]{1,0:T(8,128)(2,1)S(1)}, bf16[64,2048]{1,0:T(8,128)(2,1)S(1)}, u32[]{:S(2)}, u32[]{:S(2)}) collective-permute-start(bf16[64,2048]{1,0:T(8,128)(2,1)S(1)} %collective-permute-done.2.refs_1_), channel_id=1, source_target_pairs={{0,6},{1,7},{2,0},{3,1},{4,2},{5,3},{6,4},{7,5},{8,14},{9,15},{10,... | collective-permute-start | bytes 786440 | tf_op jit(solution)/shard_map/ppermute | solution.py:172
  15.5 0.7 copy-start.3
  16.2 1.2 %copy-start.1 = (bf16[256,2048]{1,0:T(8,128)(2,1)S(1)}, bf16[256,2048]{1,0:T(8,128)(2,1)}, u32[]{:S(2)}) copy-start(bf16[256,2048]{1,0:T(8,128)(2,1)} %spectra_ref.1) | copy-start | bytes 3145732
  17.4 0.9 %copy-start.2 = (s32[256,128]{1,0:T(8,128)S(1)}, s32[256,128]{1,0:T(8,128)}, u32[]{:S(2)}) copy-start(s32[256,128]{1,0:T(8,128)} %cand_ref.1) | copy-start | bytes 393220
  27.5 1.6 %collective-permute-start.9 = (f32[16,8,512]{2,1,0:T(8,128)S(1)}, f32[16,8,512]{2,1,0:T(8,128)S(1)}, u32[]{:S(2)}, u32[]{:S(2)}) collective-permute-start(f32[16,8,512]{2,1,0:T(8,128)S(1)} %get-tuple-element.10), channel_id=1, source_target_pairs={{0,8},{8,0},{16,24},{24,16},{32,40},{40,32},{48,56},{56,48},{64,72... | collective-permute-start | bytes 786440 | tf_op jit(solution)/shard_map/ppermute | solution.py:203

commit v8 on v7

--- a/solution.py
+++ b/solution.py
@@ -187,13 +187,16 @@
     outside = [(i, i + 1) for i in range(1, spec_count - 1, 2)]
     outside += [(target, source) for source, target in outside]
     first, last = spectra[:, :SIDE], spectra[:, -SIDE:]
+    even_core = spec % 2 == 0
+    above = shifted_along_y(theory, 1)
+    below = shifted_along_y(theory, 3)
     beside = swapped_along_x(theory)
-    above, below = shifted_along_y(theory, 1), shifted_along_y(theory, 3)
     across = shifted_along_y(theory, 2)
-    even_core = spec % 2 == 0
     inner = lax.ppermute(jnp.where(even_core, last, first), "spec", inside)
     outer = lax.ppermute(jnp.where(even_core, first, last), "spec", outside)
-    above_beside, below_beside = shifted_along_y(beside, 1), shifted_along_y(beside, 3)
+    beside, across, inner = lax.optimization_barrier((beside, across, inner))
+    above_beside = shifted_along_y(beside, 1)
+    below_beside = shifted_along_y(beside, 3)
     across_beside = swapped_along_x(across)
     processed, cand = windowed(half, where, spectra, inner, outer, cand)
     pieces = [theory, beside, above, above_beside, across, across_beside, below, below_beside]

time: 71.6 us -> 70.3 us (0.982)
  waiting for transfers between devices: 8.53 us -> 6.48 us
  blocking collectives: 40.9 us -> 42.4 us
    ppermute x5, waiting for transfers between devices: 5.89 us -> 2.22 us  [shifted_along_y(): lax.ppermute(shard, 'bucket', [(b, (b - 2 * step) % count) for b in range...]
    ppermute x1, starting transfers between devices: 3.36 us -> 0.09 us  [on_device(): inner = lax.ppermute(jnp.where(even_core, last, first), 'spec', inside)]
    ppermute x2, starting transfers between devices: 3.53 us -> 6.05 us  [swapped_along_x(): lax.ppermute(shard, 'bucket', [(b, b ^ 1) for b in range(lax.axis_size('b...]
    all_to_all x1, blocking collectives: 16.5 us -> 18.3 us  [on_device(): lax.all_to_all(chip, 'spec', 0, 0, axis_index_groups=groups, tiled=True)]
    ppermute x2, waiting for transfers between devices: 1.11 us -> 2.73 us  [swapped_along_x(): lax.ppermute(shard, 'bucket', [(b, b ^ 1) for b in range(lax.axis_size('b...]
where the time goes in v8:
time: 70.3 us; the launch traced here: 70 us
  blocking collectives  42.4 us (60%)
  starting transfers between devices  13.4 us (19%)
  waiting for transfers between devices  6.48 us (9%)
  Pallas kernels  3.32 us (5%)
  local copies, waits for them, and re-layouts  2.79 us (4%)
  other arithmetic  0.92 us (1%)
  between operations  0.73 us (1%)
    all_to_all x1, blocking collectives, on_device(): lax.all_to_all(chip, 'spec', 0, 0, axis_index_groups=groups, tiled=True)  18.3 us
    all_to_all x1, blocking collectives, on_device(): values = lax.all_to_all(copies, 'spec', 0, 0, tiled=True)  12.5 us
    all_to_all x1, blocking collectives, on_device(): lax.all_to_all(evidence.reshape(bucket_count, share // bucket_count, cand...  11.6 us
    ppermute x5, starting transfers between devices, shifted_along_y(): lax.ppermute(shard, 'bucket', [(b, (b - 2 * step) % count) for b in range...  6.51 us
    ppermute x2, starting transfers between devices, swapped_along_x(): lax.ppermute(shard, 'bucket', [(b, b ^ 1) for b in range(lax.axis_size('b...  6.05 us
    unnamed x8, local copies, waits for them, and re-layouts  2.79 us
    ppermute x2, waiting for transfers between devices, swapped_along_x(): lax.ppermute(shard, 'bucket', [(b, b ^ 1) for b in range(lax.axis_size('b...  2.73 us
    ppermute x5, waiting for transfers between devices, shifted_along_y(): lax.ppermute(shard, 'bucket', [(b, (b - 2 * step) % count) for b in range...  2.22 us
  transfers between devices with their start and end apart: 10, of which 5 were waited for; matrix products, arithmetic and copies ran while one was open for 1% of the time, Pallas kernels for 2%

profile of v8, /device:TPU:8, one launch (start us, length us, event | category | flops | bytes accessed | tf_op | source)
XLA Modules:
  0.0 70.0 jit_solution(16137522904749595137)
XLA Ops:
  0.6 0.0 copy-start
  0.6 2.4 %collective-permute-start.1 = (bf16[64,2048]{1,0:T(8,128)(2,1)}, bf16[64,2048]{1,0:T(8,128)(2,1)S(1)}, u32[]{:S(2)}, u32[]{:S(2)}) collective-permute-start(bf16[64,2048]{1,0:T(8,128)(2,1)} %refs_0_.1), channel_id=1, source_target_pairs={{0,4},{1,5},{2,6},{3,7},{4,0},{5,1},{6,2},{7,3},{8,12},{9,13},{10,... | collective-permute-start | bytes 786440 | tf_op jit(solution)/shard_map/ppermute | solution.py:172
  3.0 3.0 %collective-permute-start = (bf16[64,2048]{1,0:T(8,128)(2,1)}, bf16[64,2048]{1,0:T(8,128)(2,1)S(1)}, u32[]{:S(2)}, u32[]{:S(2)}) collective-permute-start(bf16[64,2048]{1,0:T(8,128)(2,1)} %refs_0_.1), channel_id=1, source_target_pairs={{0,1},{1,0},{2,3},{3,2},{4,5},{5,4},{6,7},{7,6},{8,9},{9,8},{10,11... | collective-permute-start | bytes 786440 | tf_op jit(solution)/shard_map/ppermute | solution.py:167
  6.0 0.9 %broadcast_select_fusion = (bf16[256,128]{1,0:T(8,128)(2,1)S(1)}, bf16[256,128]{1,0:T(8,128)(2,1)S(1)}) fusion(pred[]{:T(512)S(6)} %eq.6, bf16[256,2048]{1,0:T(8,128)(2,1)} %spectra_ref.1), kind=kLoop, calls=%fused_computation.1 | loop fusion | flops 65536 | bytes 262145 | tf_op jit(solution)/shard_map/jit(_where)/select_n | solution.py:196
  6.9 0.1 collective-permute-start.2
  7.0 0.7 collective-permute-start.3
  7.7 0.0 copy-done
  7.7 1.4 %collective-permute-start.4 = (bf16[64,2048]{1,0:T(8,128)(2,1)S(1)}, bf16[64,2048]{1,0:T(8,128)(2,1)S(1)}, u32[]{:S(2)}, u32[]{:S(2)}) collective-permute-start(bf16[64,2048]{1,0:T(8,128)(2,1)S(1)} %copy-done), channel_id=1, source_target_pairs={{0,6},{1,7},{2,0},{3,1},{4,2},{5,3},{6,4},{7,5},{8,14},{9,15},{10,... | collective-permute-start | bytes 786440 | tf_op jit(solution)/shard_map/ppermute | solution.py:172
  9.1 0.0 collective-permute-done.2.inner_ref
  9.1 0.7 collective-permute-start.7
  9.8 0.7 collective-permute-done.1.refs_4_
  10.5 2.0 %collective-permute-done.refs_1_ = bf16[64,2048]{1,0:T(8,128)(2,1)S(1)} collective-permute-done((bf16[64,2048]{1,0:T(8,128)(2,1)}, bf16[64,2048]{1,0:T(8,128)(2,1)S(1)}, u32[]{:S(2)}, u32[]{:S(2)}) %collective-permute-start) | collective-permute-done | bytes 262176 | tf_op jit(solution)/shard_map/ppermute | solution.py:167
  12.5 3.0 %collective-permute-start.6 = (bf16[64,2048]{1,0:T(8,128)(2,1)S(1)}, bf16[64,2048]{1,0:T(8,128)(2,1)S(1)}, u32[]{:S(2)}, u32[]{:S(2)}) collective-permute-start(bf16[64,2048]{1,0:T(8,128)(2,1)S(1)} %collective-permute-done.1.refs_4_), channel_id=1, source_target_pairs={{0,1},{1,0},{2,3},{3,2},{4,5},{5,4},{6,7},{7,6},{8,9},{9,8},{10,11... | collective-permute-start | bytes 786440 | tf_op jit(solution)/shard_map/ppermute | solution.py:167
  15.5 0.0 collective-permute-start.8
  15.5 0.0 collective-permute-done.3.outer_ref
  15.5 2.0 %collective-permute-start.5 = (bf16[64,2048]{1,0:T(8,128)(2,1)S(1)}, bf16[64,2048]{1,0:T(8,128)(2,1)S(1)}, u32[]{:S(2)}, u32[]{:S(2)}) collective-permute-start(bf16[64,2048]{1,0:T(8,128)(2,1)S(1)} %collective-permute-done.refs_1_), channel_id=1, source_target_pairs={{0,6},{1,7},{2,0},{3,1},{4,2},{5,3},{6,4},{7,5},{8,14},{9,15},{10,... | collective-permute-start | bytes 786440 | tf_op jit(solution)/shard_map/ppermute | solution.py:172
  17.6 0.0 copy-start.3
  17.6 0.7 copy-done.3
  18.2 0.0 copy-start.1
  18.2 1.2 %copy-done.1 = bf16[256,2048]{1,0:T(8,128)(2,1)S(1)} copy-done((bf16[256,2048]{1,0:T(8,128)(2,1)S(1)}, bf16[256,2048]{1,0:T(8,128)(2,1)}, u32[]{:S(2)}) %copy-start.1) | copy-done | bytes 1048600
  19.4 0.0 copy-start.2
  19.4 0.9 %copy-done.2 = s32[256,128]{1,0:T(8,128)S(1)} copy-done((s32[256,128]{1,0:T(8,128)S(1)}, s32[256,128]{1,0:T(8,128)}, u32[]{:S(2)}) %copy-start.2) | copy-done | bytes 131096
  20.3 1.3 %shard_map.59 = (bf16[256,2048]{1,0:T(8,128)(2,1)S(1)}, s32[256,128]{1,0:T(8,128)S(1)}) custom-call(s32[4]{0:T(128)S(1)} %copy-done.3, s32[1]{0:T(128)} %bitcast.spec_ref, s32[1]{0:T(128)} %bitcast.1.bucket_ref, bf16[256,2048]{1,0:T(8,128)(2,1)S(1)} %copy-done.1, bf16[256,128]{1,0:T(8,128)(2,1)S(1)} %collective-permute-done.2.inner_ref, ...), custom_call_target="tpu_custom_call" | custom-call | flops 536870912 | bytes 2097152 | tf_op jit(solution)/shard_map/pallas_call | solution.py:47
  21.7 0.0 collective-permute-done.4.refs_2_
  21.7 0.0 collective-permute-done.7.refs_6_
  21.7 0.7 %collective-permute-done.6.refs_5_ = bf16[64,2048]{1,0:T(8,128)(2,1)S(1)} collective-permute-done((bf16[64,2048]{1,0:T(8,128)(2,1)S(1)}, bf16[64,2048]{1,0:T(8,128)(2,1)S(1)}, u32[]{:S(2)}, u32[]{:S(2)}) %collective-permute-start.6) | collective-permute-done | bytes 262176 | tf_op jit(solution)/shard_map/ppermute | solution.py:167
  22.4 1.6 %collective-permute-done.8.refs_7_ = bf16[64,2048]{1,0:T(8,128)(2,1)S(1)} collective-permute-done((bf16[64,2048]{1,0:T(8,128)(2,1)S(1)}, bf16[64,2048]{1,0:T(8,128)(2,1)S(1)}, u32[]{:S(2)}, u32[]{:S(2)}) %collective-permute-start.8) | collective-permute-done | bytes 262176 | tf_op jit(solution)/shard_map/ppermute | solution.py:172
  23.9 0.0 collective-permute-done.5.refs_3_
  24.0 0.8 %shard_map.60 = (f32[16,8,512]{2,1,0:T(8,128)S(1)}, f32[16,8,512]{2,1,0:T(8,128)S(1)}) custom-call(s32[1]{0:T(128)} %bitcast.2.core_ref, bf16[256,2048]{1,0:T(8,128)(2,1)S(1)} %get-tuple-element.12.processed_ref, bf16[64,2048]{1,0:T(8,128)(2,1)S(1)} %copy-done, bf16[64,2048]{1,0:T(8,128)(2,1)S(1)} %collective-permute-done.refs_1_, ...), custom_call_target="tpu_custom_call" | custom-call | flops 536870912 | bytes 3145728 | tf_op jit(solution)/shard_map/pallas_call | solution.py:77
  24.8 0.1 collective-permute-start.9
  24.9 1.5 %collective-permute-done.9 = f32[16,8,512]{2,1,0:T(8,128)S(1)} collective-permute-done((f32[16,8,512]{2,1,0:T(8,128)S(1)}, f32[16,8,512]{2,1,0:T(8,128)S(1)}, u32[]{:S(2)}, u32[]{:S(2)}) %collective-permute-start.9) | collective-permute-done | bytes 262176 | tf_op jit(solution)/shard_map/ppermute | solution.py:206
  26.5 18.3 %all_to_all.15.parts_ref = bf16[16,8,512]{2,1,0:T(8,128)(2,1)S(1)} all-to-all(bf16[16,8,512]{2,1,0:T(8,128)(2,1)S(1)} %add_convert_fusion), channel_id=1, replica_groups={{0,16,32,48,64,80,96,112,128,144,160,176,192,208,224,240},{8,24,40,56,7..., dimensions={0} | all-to-all | bytes 262144 | tf_op jit(solution)/shard_map/all_to_all | solution.py:209
  44.7 0.2 shard_map.61
  44.9 12.5 %all_to_all.16.value_ref = bf16[32,8,128]{2,1,0:T(8,128)(2,1)S(1)} all-to-all(bf16[32,8,128]{2,1,0:T(8,128)(2,1)S(1)} %shard_map.61), channel_id=1, replica_groups=mesh['spec'=32,'bucket'=8] {'spec'}, dimensions={0} | all-to-all | bytes 131072 | tf_op jit(solution)/shard_map/all_to_all | solution.py:211
  57.5 0.3 shard_map.62
  57.8 11.6 %all_to_all.17.evidence_ref = f32[8,2,128]{2,1,0:T(2,128)S(1)} all-to-all(f32[8,2,128]{2,1,0:T(2,128)S(1)} %bitcast.5), channel_id=1, replica_groups=mesh['spec'=32,'bucket'=8] {'bucket'}, dimensions={0} | all-to-all | bytes 16384 | tf_op jit(solution)/shard_map/all_to_all | solution.py:216
  69.3 0.7 shard_map.63
  (1 shorter events, 0.0 us)
Async XLA Ops:
  0.6 7.1 %copy-start = (bf16[64,2048]{1,0:T(8,128)(2,1)S(1)}, bf16[64,2048]{1,0:T(8,128)(2,1)}, u32[]{:S(2)}) copy-start(bf16[64,2048]{1,0:T(8,128)(2,1)} %refs_0_.1) | copy-start | bytes 786436
  0.6 9.8 %collective-permute-start.1 = (bf16[64,2048]{1,0:T(8,128)(2,1)}, bf16[64,2048]{1,0:T(8,128)(2,1)S(1)}, u32[]{:S(2)}, u32[]{:S(2)}) collective-permute-start(bf16[64,2048]{1,0:T(8,128)(2,1)} %refs_0_.1), channel_id=1, source_target_pairs={{0,4},{1,5},{2,6},{3,7},{4,0},{5,1},{6,2},{7,3},{8,12},{9,13},{10,... | collective-permute-start | bytes 786440 | tf_op jit(solution)/shard_map/ppermute | solution.py:172
  3.0 9.5 %collective-permute-start = (bf16[64,2048]{1,0:T(8,128)(2,1)}, bf16[64,2048]{1,0:T(8,128)(2,1)S(1)}, u32[]{:S(2)}, u32[]{:S(2)}) collective-permute-start(bf16[64,2048]{1,0:T(8,128)(2,1)} %refs_0_.1), channel_id=1, source_target_pairs={{0,1},{1,0},{2,3},{3,2},{4,5},{5,4},{6,7},{7,6},{8,9},{9,8},{10,11... | collective-permute-start | bytes 786440 | tf_op jit(solution)/shard_map/ppermute | solution.py:167
  6.9 2.2 %collective-permute-start.2 = (bf16[256,128]{1,0:T(8,128)(2,1)S(1)}, bf16[256,128]{1,0:T(8,128)(2,1)S(1)}, u32[]{:S(2)}, u32[]{:S(2)}) collective-permute-start(bf16[256,128]{1,0:T(8,128)(2,1)S(1)} %get-tuple-element.21), channel_id=1, source_target_pairs={{0,8},{8,0},{16,24},{24,16},{32,40},{40,32},{48,56},{56,48},{64,72... | collective-permute-start | bytes 196616 | tf_op jit(solution)/shard_map/ppermute | solution.py:195
  7.0 8.5 %collective-permute-start.3 = (bf16[256,128]{1,0:T(8,128)(2,1)S(1)}, bf16[256,128]{1,0:T(8,128)(2,1)S(1)}, u32[]{:S(2)}, u32[]{:S(2)}) collective-permute-start(bf16[256,128]{1,0:T(8,128)(2,1)S(1)} %get-tuple-element.20), channel_id=1, source_target_pairs={{8,16},{24,32},{40,48},{56,64},{72,80},{88,96},{104,112},{120,128}... | collective-permute-start | bytes 196616 | tf_op jit(solution)/shard_map/ppermute | solution.py:196
  7.7 13.9 %collective-permute-start.4 = (bf16[64,2048]{1,0:T(8,128)(2,1)S(1)}, bf16[64,2048]{1,0:T(8,128)(2,1)S(1)}, u32[]{:S(2)}, u32[]{:S(2)}) collective-permute-start(bf16[64,2048]{1,0:T(8,128)(2,1)S(1)} %copy-done), channel_id=1, source_target_pairs={{0,6},{1,7},{2,0},{3,1},{4,2},{5,3},{6,4},{7,5},{8,14},{9,15},{10,... | collective-permute-start | bytes 786440 | tf_op jit(solution)/shard_map/ppermute | solution.py:172
  9.1 12.5 %collective-permute-start.7 = (bf16[64,2048]{1,0:T(8,128)(2,1)S(1)}, bf16[64,2048]{1,0:T(8,128)(2,1)S(1)}, u32[]{:S(2)}, u32[]{:S(2)}) collective-permute-start(bf16[64,2048]{1,0:T(8,128)(2,1)S(1)} %copy-done), channel_id=1, source_target_pairs={{0,2},{1,3},{2,4},{3,5},{4,6},{5,7},{6,0},{7,1},{8,10},{9,11},{10,... | collective-permute-start | bytes 786440 | tf_op jit(solution)/shard_map/ppermute | solution.py:172
  12.5 9.9 %collective-permute-start.6 = (bf16[64,2048]{1,0:T(8,128)(2,1)S(1)}, bf16[64,2048]{1,0:T(8,128)(2,1)S(1)}, u32[]{:S(2)}, u32[]{:S(2)}) collective-permute-start(bf16[64,2048]{1,0:T(8,128)(2,1)S(1)} %collective-permute-done.1.refs_4_), channel_id=1, source_target_pairs={{0,1},{1,0},{2,3},{3,2},{4,5},{5,4},{6,7},{7,6},{8,9},{9,8},{10,11... | collective-permute-start | bytes 786440 | tf_op jit(solution)/shard_map/ppermute | solution.py:167
  15.5 8.4 %collective-permute-start.8 = (bf16[64,2048]{1,0:T(8,128)(2,1)S(1)}, bf16[64,2048]{1,0:T(8,128)(2,1)S(1)}, u32[]{:S(2)}, u32[]{:S(2)}) collective-permute-start(bf16[64,2048]{1,0:T(8,128)(2,1)S(1)} %collective-permute-done.refs_1_), channel_id=1, source_target_pairs={{0,2},{1,3},{2,4},{3,5},{4,6},{5,7},{6,0},{7,1},{8,10},{9,11},{10,... | collective-permute-start | bytes 786440 | tf_op jit(solution)/shard_map/ppermute | solution.py:172
  15.5 8.4 %collective-permute-start.5 = (bf16[64,2048]{1,0:T(8,128)(2,1)S(1)}, bf16[64,2048]{1,0:T(8,128)(2,1)S(1)}, u32[]{:S(2)}, u32[]{:S(2)}) collective-permute-start(bf16[64,2048]{1,0:T(8,128)(2,1)S(1)} %collective-permute-done.refs_1_), channel_id=1, source_target_pairs={{0,6},{1,7},{2,0},{3,1},{4,2},{5,3},{6,4},{7,5},{8,14},{9,15},{10,... | collective-permute-start | bytes 786440 | tf_op jit(solution)/shard_map/ppermute | solution.py:172
  17.6 0.7 copy-start.3
  18.2 1.2 %copy-start.1 = (bf16[256,2048]{1,0:T(8,128)(2,1)S(1)}, bf16[256,2048]{1,0:T(8,128)(2,1)}, u32[]{:S(2)}) copy-start(bf16[256,2048]{1,0:T(8,128)(2,1)} %spectra_ref.1) | copy-start | bytes 3145732
  19.4 0.9 %copy-start.2 = (s32[256,128]{1,0:T(8,128)S(1)}, s32[256,128]{1,0:T(8,128)}, u32[]{:S(2)}) copy-start(s32[256,128]{1,0:T(8,128)} %cand_ref.1) | copy-start | bytes 393220
  24.8 1.6 %collective-permute-start.9 = (f32[16,8,512]{2,1,0:T(8,128)S(1)}, f32[16,8,512]{2,1,0:T(8,128)S(1)}, u32[]{:S(2)}, u32[]{:S(2)}) collective-permute-start(f32[16,8,512]{2,1,0:T(8,128)S(1)} %get-tuple-element.16), channel_id=1, source_target_pairs={{0,8},{8,0},{16,24},{24,16},{32,40},{40,32},{48,56},{56,48},{64,72... | collective-permute-start | bytes 786440 | tf_op jit(solution)/shard_map/ppermute | solution.py:206

commit v9 on v8

--- a/solution.py
+++ b/solution.py
@@ -55,13 +55,36 @@
     )(half, *where, spectra, inner, outer, cand)
 
 
-def score_kernel(core_ref, processed_ref, *refs):
+def product(processed_ref, piece_refs):
+    theory = jnp.concatenate([piece[...] for piece in piece_refs], axis=0)
+    return lax.dot_general(
+        processed_ref[...], theory, (((1,), (1,)), ((), ())), preferred_element_type=jnp.float32
+    )
+
+
+def early_kernel(processed_ref, *refs):
+    refs[-1][...] = product(processed_ref, refs[:-1])
+
+
+def early_scores(processed, pieces):
+    rows, bins = processed.shape
+    peptides = sum(piece.shape[0] for piece in pieces)
+    return pl.pallas_call(
+        early_kernel,
+        out_shape=jax.ShapeDtypeStruct((rows, peptides), jnp.float32),
+        in_specs=[VMEM] * (1 + len(pieces)),
+        out_specs=VMEM,
+        compiler_params=params(),
+        cost_estimate=pl.CostEstimate(
+            flops=2 * rows * bins * peptides, bytes_accessed=2 * (rows + peptides) * bins, transcendentals=0
+        ),
+    )(processed, *pieces)
+
+
+def score_kernel(core_ref, early_ref, processed_ref, *refs):
     pieces, keep_ref, send_ref = refs[:-2], refs[-2], refs[-1]
     blocks, own, peptides = keep_ref.shape
-    theory = jnp.concatenate([piece[...] for piece in pieces], axis=0)
-    scores = lax.dot_general(
-        processed_ref[...], theory, (((1,), (1,)), ((), ())), preferred_element_type=jnp.float32
-    )
+    scores = jnp.concatenate([early_ref[...], product(processed_ref, pieces)], axis=1)
     scores = scores - jnp.mean(scores, axis=1, keepdims=True)
     halves = scores.reshape(blocks, 2, own, peptides)
     even, odd = halves[:, 0], halves[:, 1]
@@ -70,20 +93,20 @@
     send_ref[...] = jnp.where(first, odd, even)
 
 
-def scored(core, processed, pieces, own):
+def scored(core, early, processed, pieces, own):
     rows, bins = processed.shape
-    peptides = sum(piece.shape[0] for piece in pieces)
-    half_rows = jax.ShapeDtypeStruct((rows // own // 2, own, peptides), jnp.float32)
+    late = sum(piece.shape[0] for piece in pieces)
+    half_rows = jax.ShapeDtypeStruct((rows // own // 2, own, early.shape[1] + late), jnp.float32)
     return pl.pallas_call(
         score_kernel,
         out_shape=(half_rows, half_rows),
-        in_specs=[SMEM, VMEM] + [VMEM] * len(pieces),
+        in_specs=[SMEM, VMEM, VMEM] + [VMEM] * len(pieces),
         out_specs=(VMEM, VMEM),
         compiler_params=params(),
         cost_estimate=pl.CostEstimate(
-            flops=2 * rows * bins * peptides, bytes_accessed=2 * (rows + peptides) * bins, transcendentals=0
+            flops=2 * rows * bins * late, bytes_accessed=2 * (rows + late) * bins, transcendentals=0
         ),
-    )(core, processed, *pieces)
+    )(core, early, processed, *pieces)
 
 
 def pick_kernel(spec_ref, bucket_ref, parts_ref, cand_ref, out_ref):
@@ -97,8 +120,12 @@
     first = pl.multiple_of(spec_ref[0] * own, own)
     ids = cand_ref[pl.ds(first, own), :]
     bucket = bucket_ref[0]
-    block_of = (ids // lanes - bucket // 2) & (rounds - 1)
-    lane_of = (ids & (lanes - 1)) ^ ((bucket & 1) * per_bucket)
+    steps_y = (ids // lanes - bucket // 2) & (rounds - 1)
+    steps_x = (ids // per_bucket ^ bucket) & 1
+    slot_same = jnp.where(steps_y == 1, 3, jnp.where(steps_y == 3, 4, steps_y))
+    slot_beside = jnp.where(steps_y == 0, 1, steps_y + 4)
+    column = jnp.where(steps_x == 0, slot_same, slot_beside) * per_bucket + ids % per_bucket
+    block_of, lane_of = column // lanes, column % lanes
     picked = jnp.zeros((own, lanes), jnp.float32)
     for block in range(rounds):
         part = centred[:, block * lanes : (block + 1) * lanes]
@@ -199,10 +226,11 @@
     below_beside = shifted_along_y(beside, 3)
     across_beside = swapped_along_x(across)
     processed, cand = windowed(half, where, spectra, inner, outer, cand)
-    pieces = [theory, beside, above, above_beside, across, across_beside, below, below_beside]
+    early = early_scores(processed, [theory, beside, across, above])
+    pieces = [below, above_beside, across_beside, below_beside]
 
     own = row_count // spec_count
-    keep, send = scored(core, processed, pieces, own)
+    keep, send = scored(core, early, processed, pieces, own)
     got = lax.ppermute(send, "spec", inside)
     chip = (keep + got).astype(jnp.bfloat16)
     groups = [list(range(c, spec_count, 2)) for c in range(2)]

time: 70.3 us -> 70.3 us (level)
  waiting for transfers between devices: 6.48 us -> 8.99 us
  starting transfers between devices: 13.4 us -> 11 us
    ppermute x5, waiting for transfers between devices: 2.22 us -> 6.9 us  [shifted_along_y(): lax.ppermute(shard, 'bucket', [(b, (b - 2 * step) % count) for b in range...]
    ppermute x2, starting transfers between devices: 6.05 us -> 3.94 us  [swapped_along_x(): lax.ppermute(shard, 'bucket', [(b, b ^ 1) for b in range(lax.axis_size('b...]
    ppermute x2, waiting for transfers between devices: 2.73 us -> 0.66 us  [swapped_along_x(): lax.ppermute(shard, 'bucket', [(b, b ^ 1) for b in range(lax.axis_size('b...]
  transfers between devices with their start and end apart: 10 -> 10, of which waited for: 5 -> 5; matrix products, arithmetic and copies ran while one was open for 1% -> 1% of each run, Pallas kernels for 2% -> 3%
where the time goes in v9:
time: 70.3 us; the launch traced here: 69.9 us
  blocking collectives  42 us (60%)
  starting transfers between devices  11 us (16%)
  waiting for transfers between devices  8.99 us (13%)
  Pallas kernels  3.51 us (5%)
  local copies, waits for them, and re-layouts  2.79 us (4%)
  other arithmetic  0.92 us (1%)
  between operations  0.73 us (1%)
    all_to_all x1, blocking collectives, on_device(): lax.all_to_all(chip, 'spec', 0, 0, axis_index_groups=groups, tiled=True)  17.7 us
    all_to_all x1, blocking collectives, on_device(): values = lax.all_to_all(copies, 'spec', 0, 0, tiled=True)  12.5 us
    all_to_all x1, blocking collectives, on_device(): lax.all_to_all(evidence.reshape(bucket_count, share // bucket_count, cand...  11.8 us
    ppermute x5, waiting for transfers between devices, shifted_along_y(): lax.ppermute(shard, 'bucket', [(b, (b - 2 * step) % count) for b in range...  6.9 us
    ppermute x5, starting transfers between devices, shifted_along_y(): lax.ppermute(shard, 'bucket', [(b, (b - 2 * step) % count) for b in range...  6.1 us
    ppermute x2, starting transfers between devices, swapped_along_x(): lax.ppermute(shard, 'bucket', [(b, b ^ 1) for b in range(lax.axis_size('b...  3.94 us
    unnamed x8, local copies, waits for them, and re-layouts  2.79 us
    ppermute x1, waiting for transfers between devices, on_device(): got = lax.ppermute(send, 'spec', inside)  1.42 us
  transfers between devices with their start and end apart: 10, of which 5 were waited for; matrix products, arithmetic and copies ran while one was open for 1% of the time, Pallas kernels for 3%

profile of v9, /device:TPU:8, one launch (start us, length us, event | category | flops | bytes accessed | tf_op | source)
XLA Modules:
  0.0 69.9 jit_solution(1335481858498943842)
XLA Ops:
  0.6 0.0 copy-start
  0.6 3.1 %collective-permute-start = (bf16[64,2048]{1,0:T(8,128)(2,1)}, bf16[64,2048]{1,0:T(8,128)(2,1)S(1)}, u32[]{:S(2)}, u32[]{:S(2)}) collective-permute-start(bf16[64,2048]{1,0:T(8,128)(2,1)} %refs_0_.1), channel_id=1, source_target_pairs={{0,1},{1,0},{2,3},{3,2},{4,5},{5,4},{6,7},{7,6},{8,9},{9,8},{10,11... | collective-permute-start | bytes 786440 | tf_op jit(solution)/shard_map/ppermute | solution.py:194
  3.8 2.3 %collective-permute-start.1 = (bf16[64,2048]{1,0:T(8,128)(2,1)}, bf16[64,2048]{1,0:T(8,128)(2,1)S(1)}, u32[]{:S(2)}, u32[]{:S(2)}) collective-permute-start(bf16[64,2048]{1,0:T(8,128)(2,1)} %refs_0_.1), channel_id=1, source_target_pairs={{0,4},{1,5},{2,6},{3,7},{4,0},{5,1},{6,2},{7,3},{8,12},{9,13},{10,... | collective-permute-start | bytes 786440 | tf_op jit(solution)/shard_map/ppermute | solution.py:199
  6.0 0.9 %broadcast_select_fusion = (bf16[256,128]{1,0:T(8,128)(2,1)S(1)}, bf16[256,128]{1,0:T(8,128)(2,1)S(1)}) fusion(pred[]{:T(512)S(6)} %eq.6, bf16[256,2048]{1,0:T(8,128)(2,1)} %spectra_ref.1), kind=kLoop, calls=%fused_computation.1 | loop fusion | flops 65536 | bytes 262145 | tf_op jit(solution)/shard_map/jit(_where)/select_n | solution.py:223
  6.9 0.1 collective-permute-start.2
  7.0 0.7 collective-permute-start.3
  7.7 0.0 copy-done
  7.7 1.4 %collective-permute-start.4 = (bf16[64,2048]{1,0:T(8,128)(2,1)S(1)}, bf16[64,2048]{1,0:T(8,128)(2,1)S(1)}, u32[]{:S(2)}, u32[]{:S(2)}) collective-permute-start(bf16[64,2048]{1,0:T(8,128)(2,1)S(1)} %copy-done), channel_id=1, source_target_pairs={{0,6},{1,7},{2,0},{3,1},{4,2},{5,3},{6,4},{7,5},{8,14},{9,15},{10,... | collective-permute-start | bytes 786440 | tf_op jit(solution)/shard_map/ppermute | solution.py:199
  9.1 0.0 collective-permute-done.2.inner_ref
  9.1 0.7 collective-permute-start.5
  9.8 0.7 collective-permute-done.refs_1_
  10.5 2.8 %collective-permute-done.1.refs_2_ = bf16[64,2048]{1,0:T(8,128)(2,1)S(1)} collective-permute-done((bf16[64,2048]{1,0:T(8,128)(2,1)}, bf16[64,2048]{1,0:T(8,128)(2,1)S(1)}, u32[]{:S(2)}, u32[]{:S(2)}) %collective-permute-start.1) | collective-permute-done | bytes 262176 | tf_op jit(solution)/shard_map/ppermute | solution.py:199
  13.3 0.4 collective-permute-start.6
  13.7 0.8 %collective-permute-start.7 = (bf16[64,2048]{1,0:T(8,128)(2,1)S(1)}, bf16[64,2048]{1,0:T(8,128)(2,1)S(1)}, u32[]{:S(2)}, u32[]{:S(2)}) collective-permute-start(bf16[64,2048]{1,0:T(8,128)(2,1)S(1)} %collective-permute-done.1.refs_2_), channel_id=1, source_target_pairs={{0,1},{1,0},{2,3},{3,2},{4,5},{5,4},{6,7},{7,6},{8,9},{9,8},{10,11... | collective-permute-start | bytes 786440 | tf_op jit(solution)/shard_map/ppermute | solution.py:194
  14.5 0.0 collective-permute-done.3.outer_ref
  14.5 1.3 %collective-permute-start.8 = (bf16[64,2048]{1,0:T(8,128)(2,1)S(1)}, bf16[64,2048]{1,0:T(8,128)(2,1)S(1)}, u32[]{:S(2)}, u32[]{:S(2)}) collective-permute-start(bf16[64,2048]{1,0:T(8,128)(2,1)S(1)} %collective-permute-done.refs_1_), channel_id=1, source_target_pairs={{0,2},{1,3},{2,4},{3,5},{4,6},{5,7},{6,0},{7,1},{8,10},{9,11},{10,... | collective-permute-start | bytes 786440 | tf_op jit(solution)/shard_map/ppermute | solution.py:199
  15.9 0.0 copy-start.3
  15.9 0.7 copy-done.3
  16.5 0.0 copy-start.1
  16.5 1.2 %copy-done.1 = bf16[256,2048]{1,0:T(8,128)(2,1)S(1)} copy-done((bf16[256,2048]{1,0:T(8,128)(2,1)S(1)}, bf16[256,2048]{1,0:T(8,128)(2,1)}, u32[]{:S(2)}) %copy-start.1) | copy-done | bytes 1048600
  17.8 0.0 copy-start.2
  17.8 0.9 %copy-done.2 = s32[256,128]{1,0:T(8,128)S(1)} copy-done((s32[256,128]{1,0:T(8,128)S(1)}, s32[256,128]{1,0:T(8,128)}, u32[]{:S(2)}) %copy-start.2) | copy-done | bytes 131096
  18.7 1.3 %shard_map.59 = (bf16[256,2048]{1,0:T(8,128)(2,1)S(1)}, s32[256,128]{1,0:T(8,128)S(1)}) custom-call(s32[4]{0:T(128)S(1)} %copy-done.3, s32[1]{0:T(128)} %bitcast.spec_ref, s32[1]{0:T(128)} %bitcast.1.bucket_ref, bf16[256,2048]{1,0:T(8,128)(2,1)S(1)} %copy-done.1, bf16[256,128]{1,0:T(8,128)(2,1)S(1)} %collective-permute-done.2.inner_ref, ...), custom_call_target="tpu_custom_call" | custom-call | flops 536870912 | bytes 2097152 | tf_op jit(solution)/shard_map/pallas_call | solution.py:47
  20.0 0.0 collective-permute-done.4.refs_3_
  20.0 0.5 shard_map.60.early_ref
  20.5 0.0 collective-permute-done.5.refs_0_
  20.5 3.5 %collective-permute-done.6.refs_1_ = bf16[64,2048]{1,0:T(8,128)(2,1)S(1)} collective-permute-done((bf16[64,2048]{1,0:T(8,128)(2,1)S(1)}, bf16[64,2048]{1,0:T(8,128)(2,1)S(1)}, u32[]{:S(2)}, u32[]{:S(2)}) %collective-permute-start.6) | collective-permute-done | bytes 262176 | tf_op jit(solution)/shard_map/ppermute | solution.py:199
  24.0 0.0 collective-permute-done.7.refs_2_
  24.0 0.6 collective-permute-done.8.refs_3_
  24.5 0.6 shard_map.61
  25.1 0.2 collective-permute-start.9
  25.3 1.4 %collective-permute-done.9 = f32[16,8,512]{2,1,0:T(8,128)S(1)} collective-permute-done((f32[16,8,512]{2,1,0:T(8,128)S(1)}, f32[16,8,512]{2,1,0:T(8,128)S(1)}, u32[]{:S(2)}, u32[]{:S(2)}) %collective-permute-start.9) | collective-permute-done | bytes 262176 | tf_op jit(solution)/shard_map/ppermute | solution.py:234
  26.8 17.7 %all_to_all.15.parts_ref = bf16[16,8,512]{2,1,0:T(8,128)(2,1)S(1)} all-to-all(bf16[16,8,512]{2,1,0:T(8,128)(2,1)S(1)} %add_convert_fusion), channel_id=1, replica_groups={{0,16,32,48,64,80,96,112,128,144,160,176,192,208,224,240},{8,24,40,56,7..., dimensions={0} | all-to-all | bytes 262144 | tf_op jit(solution)/shard_map/all_to_all | solution.py:237
  44.4 0.2 shard_map.62
  44.6 12.5 %all_to_all.16.value_ref = bf16[32,8,128]{2,1,0:T(8,128)(2,1)S(1)} all-to-all(bf16[32,8,128]{2,1,0:T(8,128)(2,1)S(1)} %shard_map.62), channel_id=1, replica_groups=mesh['spec'=32,'bucket'=8] {'spec'}, dimensions={0} | all-to-all | bytes 131072 | tf_op jit(solution)/shard_map/all_to_all | solution.py:239
  57.2 0.3 shard_map.63
  57.5 11.8 %all_to_all.17.evidence_ref = f32[8,2,128]{2,1,0:T(2,128)S(1)} all-to-all(f32[8,2,128]{2,1,0:T(2,128)S(1)} %bitcast.5), channel_id=1, replica_groups=mesh['spec'=32,'bucket'=8] {'bucket'}, dimensions={0} | all-to-all | bytes 16384 | tf_op jit(solution)/shard_map/all_to_all | solution.py:244
  69.3 0.7 shard_map.64
  (1 shorter events, 0.0 us)
Async XLA Ops:
  0.6 7.1 %copy-start = (bf16[64,2048]{1,0:T(8,128)(2,1)S(1)}, bf16[64,2048]{1,0:T(8,128)(2,1)}, u32[]{:S(2)}) copy-start(bf16[64,2048]{1,0:T(8,128)(2,1)} %refs_0_.1) | copy-start | bytes 786436
  0.6 9.8 %collective-permute-start = (bf16[64,2048]{1,0:T(8,128)(2,1)}, bf16[64,2048]{1,0:T(8,128)(2,1)S(1)}, u32[]{:S(2)}, u32[]{:S(2)}) collective-permute-start(bf16[64,2048]{1,0:T(8,128)(2,1)} %refs_0_.1), channel_id=1, source_target_pairs={{0,1},{1,0},{2,3},{3,2},{4,5},{5,4},{6,7},{7,6},{8,9},{9,8},{10,11... | collective-permute-start | bytes 786440 | tf_op jit(solution)/shard_map/ppermute | solution.py:194
  3.8 9.6 %collective-permute-start.1 = (bf16[64,2048]{1,0:T(8,128)(2,1)}, bf16[64,2048]{1,0:T(8,128)(2,1)S(1)}, u32[]{:S(2)}, u32[]{:S(2)}) collective-permute-start(bf16[64,2048]{1,0:T(8,128)(2,1)} %refs_0_.1), channel_id=1, source_target_pairs={{0,4},{1,5},{2,6},{3,7},{4,0},{5,1},{6,2},{7,3},{8,12},{9,13},{10,... | collective-permute-start | bytes 786440 | tf_op jit(solution)/shard_map/ppermute | solution.py:199
  6.9 2.2 %collective-permute-start.2 = (bf16[256,128]{1,0:T(8,128)(2,1)S(1)}, bf16[256,128]{1,0:T(8,128)(2,1)S(1)}, u32[]{:S(2)}, u32[]{:S(2)}) collective-permute-start(bf16[256,128]{1,0:T(8,128)(2,1)S(1)} %get-tuple-element.21), channel_id=1, source_target_pairs={{0,8},{8,0},{16,24},{24,16},{32,40},{40,32},{48,56},{56,48},{64,72... | collective-permute-start | bytes 196616 | tf_op jit(solution)/shard_map/ppermute | solution.py:222
  7.0 7.5 %collective-permute-start.3 = (bf16[256,128]{1,0:T(8,128)(2,1)S(1)}, bf16[256,128]{1,0:T(8,128)(2,1)S(1)}, u32[]{:S(2)}, u32[]{:S(2)}) collective-permute-start(bf16[256,128]{1,0:T(8,128)(2,1)S(1)} %get-tuple-element.20), channel_id=1, source_target_pairs={{8,16},{24,32},{40,48},{56,64},{72,80},{88,96},{104,112},{120,128}... | collective-permute-start | bytes 196616 | tf_op jit(solution)/shard_map/ppermute | solution.py:223
  7.7 12.3 %collective-permute-start.4 = (bf16[64,2048]{1,0:T(8,128)(2,1)S(1)}, bf16[64,2048]{1,0:T(8,128)(2,1)S(1)}, u32[]{:S(2)}, u32[]{:S(2)}) collective-permute-start(bf16[64,2048]{1,0:T(8,128)(2,1)S(1)} %copy-done), channel_id=1, source_target_pairs={{0,6},{1,7},{2,0},{3,1},{4,2},{5,3},{6,4},{7,5},{8,14},{9,15},{10,... | collective-permute-start | bytes 786440 | tf_op jit(solution)/shard_map/ppermute | solution.py:199
  9.1 11.3 %collective-permute-start.5 = (bf16[64,2048]{1,0:T(8,128)(2,1)S(1)}, bf16[64,2048]{1,0:T(8,128)(2,1)S(1)}, u32[]{:S(2)}, u32[]{:S(2)}) collective-permute-start(bf16[64,2048]{1,0:T(8,128)(2,1)S(1)} %copy-done), channel_id=1, source_target_pairs={{0,2},{1,3},{2,4},{3,5},{4,6},{5,7},{6,0},{7,1},{8,10},{9,11},{10,... | collective-permute-start | bytes 786440 | tf_op jit(solution)/shard_map/ppermute | solution.py:199
  13.3 10.6 %collective-permute-start.6 = (bf16[64,2048]{1,0:T(8,128)(2,1)S(1)}, bf16[64,2048]{1,0:T(8,128)(2,1)S(1)}, u32[]{:S(2)}, u32[]{:S(2)}) collective-permute-start(bf16[64,2048]{1,0:T(8,128)(2,1)S(1)} %collective-permute-done.refs_1_), channel_id=1, source_target_pairs={{0,6},{1,7},{2,0},{3,1},{4,2},{5,3},{6,4},{7,5},{8,14},{9,15},{10,... | collective-permute-start | bytes 786440 | tf_op jit(solution)/shard_map/ppermute | solution.py:199
  13.7 10.3 %collective-permute-start.7 = (bf16[64,2048]{1,0:T(8,128)(2,1)S(1)}, bf16[64,2048]{1,0:T(8,128)(2,1)S(1)}, u32[]{:S(2)}, u32[]{:S(2)}) collective-permute-start(bf16[64,2048]{1,0:T(8,128)(2,1)S(1)} %collective-permute-done.1.refs_2_), channel_id=1, source_target_pairs={{0,1},{1,0},{2,3},{3,2},{4,5},{5,4},{6,7},{7,6},{8,9},{9,8},{10,11... | collective-permute-start | bytes 786440 | tf_op jit(solution)/shard_map/ppermute | solution.py:194
  14.5 10.0 %collective-permute-start.8 = (bf16[64,2048]{1,0:T(8,128)(2,1)S(1)}, bf16[64,2048]{1,0:T(8,128)(2,1)S(1)}, u32[]{:S(2)}, u32[]{:S(2)}) collective-permute-start(bf16[64,2048]{1,0:T(8,128)(2,1)S(1)} %collective-permute-done.refs_1_), channel_id=1, source_target_pairs={{0,2},{1,3},{2,4},{3,5},{4,6},{5,7},{6,0},{7,1},{8,10},{9,11},{10,... | collective-permute-start | bytes 786440 | tf_op jit(solution)/shard_map/ppermute | solution.py:199
  15.9 0.7 copy-start.3
  16.5 1.2 %copy-start.1 = (bf16[256,2048]{1,0:T(8,128)(2,1)S(1)}, bf16[256,2048]{1,0:T(8,128)(2,1)}, u32[]{:S(2)}) copy-start(bf16[256,2048]{1,0:T(8,128)(2,1)} %spectra_ref.1) | copy-start | bytes 3145732
  17.8 0.9 %copy-start.2 = (s32[256,128]{1,0:T(8,128)S(1)}, s32[256,128]{1,0:T(8,128)}, u32[]{:S(2)}) copy-start(s32[256,128]{1,0:T(8,128)} %cand_ref.1) | copy-start | bytes 393220
  25.1 1.6 %collective-permute-start.9 = (f32[16,8,512]{2,1,0:T(8,128)S(1)}, f32[16,8,512]{2,1,0:T(8,128)S(1)}, u32[]{:S(2)}, u32[]{:S(2)}) collective-permute-start(f32[16,8,512]{2,1,0:T(8,128)S(1)} %get-tuple-element.16), channel_id=1, source_target_pairs={{0,8},{8,0},{16,24},{24,16},{32,40},{40,32},{48,56},{56,48},{64,72... | collective-permute-start | bytes 786440 | tf_op jit(solution)/shard_map/ppermute | solution.py:234

commit v10 on v9

--- a/solution.py
+++ b/solution.py
@@ -90,16 +90,16 @@
     even, odd = halves[:, 0], halves[:, 1]
     first = core_ref[0] == 0
     keep_ref[...] = jnp.where(first, even, odd)
-    send_ref[...] = jnp.where(first, odd, even)
+    send_ref[...] = jnp.where(first, odd, even).astype(send_ref.dtype)
 
 
 def scored(core, early, processed, pieces, own):
     rows, bins = processed.shape
     late = sum(piece.shape[0] for piece in pieces)
-    half_rows = jax.ShapeDtypeStruct((rows // own // 2, own, early.shape[1] + late), jnp.float32)
+    half_rows = (rows // own // 2, own, early.shape[1] + late)
     return pl.pallas_call(
         score_kernel,
-        out_shape=(half_rows, half_rows),
+        out_shape=(jax.ShapeDtypeStruct(half_rows, jnp.float32), jax.ShapeDtypeStruct(half_rows, jnp.bfloat16)),
         in_specs=[SMEM, VMEM, VMEM] + [VMEM] * len(pieces),
         out_specs=(VMEM, VMEM),
         compiler_params=params(),
@@ -232,7 +232,7 @@
     own = row_count // spec_count
     keep, send = scored(core, early, processed, pieces, own)
     got = lax.ppermute(send, "spec", inside)
-    chip = (keep + got).astype(jnp.bfloat16)
+    chip = (keep + got.astype(jnp.float32)).astype(jnp.bfloat16)
     groups = [list(range(c, spec_count, 2)) for c in range(2)]
     parts = lax.all_to_all(chip, "spec", 0, 0, axis_index_groups=groups, tiled=True)
     copies = picked_copies(where, parts, cand, spec_count)

time: 70.3 us -> 70.1 us (level)
  no operation moved by 1% of the time
where the time goes in v10:
time: 70.1 us; the launch traced here: 69.8 us
  blocking collectives  42 us (60%)
  starting transfers between devices  11 us (16%)
  waiting for transfers between devices  8.8 us (13%)
  Pallas kernels  3.51 us (5%)
  local copies, waits for them, and re-layouts  2.79 us (4%)
  other arithmetic  0.91 us (1%)
  between operations  0.73 us (1%)
    all_to_all x1, blocking collectives, on_device(): lax.all_to_all(chip, 'spec', 0, 0, axis_index_groups=groups, tiled=True)  17.7 us
    all_to_all x1, blocking collectives, on_device(): values = lax.all_to_all(copies, 'spec', 0, 0, tiled=True)  12.6 us
    all_to_all x1, blocking collectives, on_device(): lax.all_to_all(evidence.reshape(bucket_count, share // bucket_count, cand...  11.8 us
    ppermute x5, waiting for transfers between devices, shifted_along_y(): lax.ppermute(shard, 'bucket', [(b, (b - 2 * step) % count) for b in range...  6.9 us
    ppermute x5, starting transfers between devices, shifted_along_y(): lax.ppermute(shard, 'bucket', [(b, (b - 2 * step) % count) for b in range...  6.1 us
    ppermute x2, starting transfers between devices, swapped_along_x(): lax.ppermute(shard, 'bucket', [(b, b ^ 1) for b in range(lax.axis_size('b...  3.94 us
    unnamed x8, local copies, waits for them, and re-layouts  2.79 us
  transfers between devices with their start and end apart: 10, of which 5 were waited for; matrix products, arithmetic and copies ran while one was open for 1% of the time, Pallas kernels for 3%

profile of v10, /device:TPU:8, one launch (start us, length us, event | category | flops | bytes accessed | tf_op | source)
XLA Modules:
  0.0 69.8 jit_solution(9445774135546447798)
XLA Ops:
  0.6 0.0 copy-start
  0.6 3.1 %collective-permute-start = (bf16[64,2048]{1,0:T(8,128)(2,1)}, bf16[64,2048]{1,0:T(8,128)(2,1)S(1)}, u32[]{:S(2)}, u32[]{:S(2)}) collective-permute-start(bf16[64,2048]{1,0:T(8,128)(2,1)} %refs_0_.1), channel_id=1, source_target_pairs={{0,1},{1,0},{2,3},{3,2},{4,5},{5,4},{6,7},{7,6},{8,9},{9,8},{10,11... | collective-permute-start | bytes 786440 | tf_op jit(solution)/shard_map/ppermute | solution.py:194
  3.8 2.3 %collective-permute-start.1 = (bf16[64,2048]{1,0:T(8,128)(2,1)}, bf16[64,2048]{1,0:T(8,128)(2,1)S(1)}, u32[]{:S(2)}, u32[]{:S(2)}) collective-permute-start(bf16[64,2048]{1,0:T(8,128)(2,1)} %refs_0_.1), channel_id=1, source_target_pairs={{0,4},{1,5},{2,6},{3,7},{4,0},{5,1},{6,2},{7,3},{8,12},{9,13},{10,... | collective-permute-start | bytes 786440 | tf_op jit(solution)/shard_map/ppermute | solution.py:199
  6.0 0.9 %broadcast_select_fusion = (bf16[256,128]{1,0:T(8,128)(2,1)S(1)}, bf16[256,128]{1,0:T(8,128)(2,1)S(1)}) fusion(pred[]{:T(512)S(6)} %eq.6, bf16[256,2048]{1,0:T(8,128)(2,1)} %spectra_ref.1), kind=kLoop, calls=%fused_computation.1 | loop fusion | flops 65536 | bytes 262145 | tf_op jit(solution)/shard_map/jit(_where)/select_n | solution.py:223
  6.9 0.1 collective-permute-start.2
  7.0 0.7 collective-permute-start.3
  7.7 0.0 copy-done
  7.7 1.4 %collective-permute-start.4 = (bf16[64,2048]{1,0:T(8,128)(2,1)S(1)}, bf16[64,2048]{1,0:T(8,128)(2,1)S(1)}, u32[]{:S(2)}, u32[]{:S(2)}) collective-permute-start(bf16[64,2048]{1,0:T(8,128)(2,1)S(1)} %copy-done), channel_id=1, source_target_pairs={{0,6},{1,7},{2,0},{3,1},{4,2},{5,3},{6,4},{7,5},{8,14},{9,15},{10,... | collective-permute-start | bytes 786440 | tf_op jit(solution)/shard_map/ppermute | solution.py:199
  9.1 0.0 collective-permute-done.2.inner_ref
  9.1 0.7 collective-permute-start.5
  9.8 0.7 collective-permute-done.refs_1_
  10.5 2.8 %collective-permute-done.1.refs_2_ = bf16[64,2048]{1,0:T(8,128)(2,1)S(1)} collective-permute-done((bf16[64,2048]{1,0:T(8,128)(2,1)}, bf16[64,2048]{1,0:T(8,128)(2,1)S(1)}, u32[]{:S(2)}, u32[]{:S(2)}) %collective-permute-start.1) | collective-permute-done | bytes 262176 | tf_op jit(solution)/shard_map/ppermute | solution.py:199
  13.3 0.4 collective-permute-start.6
  13.7 0.8 %collective-permute-start.7 = (bf16[64,2048]{1,0:T(8,128)(2,1)S(1)}, bf16[64,2048]{1,0:T(8,128)(2,1)S(1)}, u32[]{:S(2)}, u32[]{:S(2)}) collective-permute-start(bf16[64,2048]{1,0:T(8,128)(2,1)S(1)} %collective-permute-done.1.refs_2_), channel_id=1, source_target_pairs={{0,1},{1,0},{2,3},{3,2},{4,5},{5,4},{6,7},{7,6},{8,9},{9,8},{10,11... | collective-permute-start | bytes 786440 | tf_op jit(solution)/shard_map/ppermute | solution.py:194
  14.5 0.0 collective-permute-done.3.outer_ref
  14.5 1.3 %collective-permute-start.8 = (bf16[64,2048]{1,0:T(8,128)(2,1)S(1)}, bf16[64,2048]{1,0:T(8,128)(2,1)S(1)}, u32[]{:S(2)}, u32[]{:S(2)}) collective-permute-start(bf16[64,2048]{1,0:T(8,128)(2,1)S(1)} %collective-permute-done.refs_1_), channel_id=1, source_target_pairs={{0,2},{1,3},{2,4},{3,5},{4,6},{5,7},{6,0},{7,1},{8,10},{9,11},{10,... | collective-permute-start | bytes 786440 | tf_op jit(solution)/shard_map/ppermute | solution.py:199
  15.9 0.0 copy-start.3
  15.9 0.7 copy-done.3
  16.5 0.0 copy-start.1
  16.5 1.2 %copy-done.1 = bf16[256,2048]{1,0:T(8,128)(2,1)S(1)} copy-done((bf16[256,2048]{1,0:T(8,128)(2,1)S(1)}, bf16[256,2048]{1,0:T(8,128)(2,1)}, u32[]{:S(2)}) %copy-start.1) | copy-done | bytes 1048600
  17.8 0.0 copy-start.2
  17.8 0.9 %copy-done.2 = s32[256,128]{1,0:T(8,128)S(1)} copy-done((s32[256,128]{1,0:T(8,128)S(1)}, s32[256,128]{1,0:T(8,128)}, u32[]{:S(2)}) %copy-start.2) | copy-done | bytes 131096
  18.7 1.3 %shard_map.59 = (bf16[256,2048]{1,0:T(8,128)(2,1)S(1)}, s32[256,128]{1,0:T(8,128)S(1)}) custom-call(s32[4]{0:T(128)S(1)} %copy-done.3, s32[1]{0:T(128)} %bitcast.spec_ref, s32[1]{0:T(128)} %bitcast.1.bucket_ref, bf16[256,2048]{1,0:T(8,128)(2,1)S(1)} %copy-done.1, bf16[256,128]{1,0:T(8,128)(2,1)S(1)} %collective-permute-done.2.inner_ref, ...), custom_call_target="tpu_custom_call" | custom-call | flops 536870912 | bytes 2097152 | tf_op jit(solution)/shard_map/pallas_call | solution.py:47
  20.0 0.0 collective-permute-done.4.refs_3_
  20.0 0.5 shard_map.60.early_ref
  20.5 0.0 collective-permute-done.5.refs_0_
  20.5 3.5 %collective-permute-done.6.refs_1_ = bf16[64,2048]{1,0:T(8,128)(2,1)S(1)} collective-permute-done((bf16[64,2048]{1,0:T(8,128)(2,1)S(1)}, bf16[64,2048]{1,0:T(8,128)(2,1)S(1)}, u32[]{:S(2)}, u32[]{:S(2)}) %collective-permute-start.6) | collective-permute-done | bytes 262176 | tf_op jit(solution)/shard_map/ppermute | solution.py:199
  24.0 0.0 collective-permute-done.7.refs_2_
  24.0 0.6 collective-permute-done.8.refs_3_
  24.5 0.6 shard_map.61
  25.1 0.2 collective-permute-start.9
  25.3 1.2 %collective-permute-done.9 = bf16[16,8,512]{2,1,0:T(8,128)(2,1)S(1)} collective-permute-done((bf16[16,8,512]{2,1,0:T(8,128)(2,1)S(1)}, bf16[16,8,512]{2,1,0:T(8,128)(2,1)S(1)}, u32[]{:S(2)}, u32[]{:S(2)}) %collective-permute-start.9) | collective-permute-done | bytes 131104 | tf_op jit(solution)/shard_map/ppermute | solution.py:234
  26.6 17.7 %all_to_all.15.parts_ref = bf16[16,8,512]{2,1,0:T(8,128)(2,1)S(1)} all-to-all(bf16[16,8,512]{2,1,0:T(8,128)(2,1)S(1)} %add_convert_fusion), channel_id=1, replica_groups={{0,16,32,48,64,80,96,112,128,144,160,176,192,208,224,240},{8,24,40,56,7..., dimensions={0} | all-to-all | bytes 262144 | tf_op jit(solution)/shard_map/all_to_all | solution.py:237
  44.2 0.2 shard_map.62
  44.4 12.6 %all_to_all.16.value_ref = bf16[32,8,128]{2,1,0:T(8,128)(2,1)S(1)} all-to-all(bf16[32,8,128]{2,1,0:T(8,128)(2,1)S(1)} %shard_map.62), channel_id=1, replica_groups=mesh['spec'=32,'bucket'=8] {'spec'}, dimensions={0} | all-to-all | bytes 131072 | tf_op jit(solution)/shard_map/all_to_all | solution.py:239
  57.0 0.3 shard_map.63
  57.3 11.8 %all_to_all.17.evidence_ref = f32[8,2,128]{2,1,0:T(2,128)S(1)} all-to-all(f32[8,2,128]{2,1,0:T(2,128)S(1)} %bitcast.5), channel_id=1, replica_groups=mesh['spec'=32,'bucket'=8] {'bucket'}, dimensions={0} | all-to-all | bytes 16384 | tf_op jit(solution)/shard_map/all_to_all | solution.py:244
  69.1 0.7 shard_map.64
  (1 shorter events, 0.0 us)
Async XLA Ops:
  0.6 7.1 %copy-start = (bf16[64,2048]{1,0:T(8,128)(2,1)S(1)}, bf16[64,2048]{1,0:T(8,128)(2,1)}, u32[]{:S(2)}) copy-start(bf16[64,2048]{1,0:T(8,128)(2,1)} %refs_0_.1) | copy-start | bytes 786436
  0.6 9.8 %collective-permute-start = (bf16[64,2048]{1,0:T(8,128)(2,1)}, bf16[64,2048]{1,0:T(8,128)(2,1)S(1)}, u32[]{:S(2)}, u32[]{:S(2)}) collective-permute-start(bf16[64,2048]{1,0:T(8,128)(2,1)} %refs_0_.1), channel_id=1, source_target_pairs={{0,1},{1,0},{2,3},{3,2},{4,5},{5,4},{6,7},{7,6},{8,9},{9,8},{10,11... | collective-permute-start | bytes 786440 | tf_op jit(solution)/shard_map/ppermute | solution.py:194
  3.8 9.6 %collective-permute-start.1 = (bf16[64,2048]{1,0:T(8,128)(2,1)}, bf16[64,2048]{1,0:T(8,128)(2,1)S(1)}, u32[]{:S(2)}, u32[]{:S(2)}) collective-permute-start(bf16[64,2048]{1,0:T(8,128)(2,1)} %refs_0_.1), channel_id=1, source_target_pairs={{0,4},{1,5},{2,6},{3,7},{4,0},{5,1},{6,2},{7,3},{8,12},{9,13},{10,... | collective-permute-start | bytes 786440 | tf_op jit(solution)/shard_map/ppermute | solution.py:199
  6.9 2.2 %collective-permute-start.2 = (bf16[256,128]{1,0:T(8,128)(2,1)S(1)}, bf16[256,128]{1,0:T(8,128)(2,1)S(1)}, u32[]{:S(2)}, u32[]{:S(2)}) collective-permute-start(bf16[256,128]{1,0:T(8,128)(2,1)S(1)} %get-tuple-element.21), channel_id=1, source_target_pairs={{0,8},{8,0},{16,24},{24,16},{32,40},{40,32},{48,56},{56,48},{64,72... | collective-permute-start | bytes 196616 | tf_op jit(solution)/shard_map/ppermute | solution.py:222
  7.0 7.5 %collective-permute-start.3 = (bf16[256,128]{1,0:T(8,128)(2,1)S(1)}, bf16[256,128]{1,0:T(8,128)(2,1)S(1)}, u32[]{:S(2)}, u32[]{:S(2)}) collective-permute-start(bf16[256,128]{1,0:T(8,128)(2,1)S(1)} %get-tuple-element.20), channel_id=1, source_target_pairs={{8,16},{24,32},{40,48},{56,64},{72,80},{88,96},{104,112},{120,128}... | collective-permute-start | bytes 196616 | tf_op jit(solution)/shard_map/ppermute | solution.py:223
  7.7 12.3 %collective-permute-start.4 = (bf16[64,2048]{1,0:T(8,128)(2,1)S(1)}, bf16[64,2048]{1,0:T(8,128)(2,1)S(1)}, u32[]{:S(2)}, u32[]{:S(2)}) collective-permute-start(bf16[64,2048]{1,0:T(8,128)(2,1)S(1)} %copy-done), channel_id=1, source_target_pairs={{0,6},{1,7},{2,0},{3,1},{4,2},{5,3},{6,4},{7,5},{8,14},{9,15},{10,... | collective-permute-start | bytes 786440 | tf_op jit(solution)/shard_map/ppermute | solution.py:199
  9.1 11.3 %collective-permute-start.5 = (bf16[64,2048]{1,0:T(8,128)(2,1)S(1)}, bf16[64,2048]{1,0:T(8,128)(2,1)S(1)}, u32[]{:S(2)}, u32[]{:S(2)}) collective-permute-start(bf16[64,2048]{1,0:T(8,128)(2,1)S(1)} %copy-done), channel_id=1, source_target_pairs={{0,2},{1,3},{2,4},{3,5},{4,6},{5,7},{6,0},{7,1},{8,10},{9,11},{10,... | collective-permute-start | bytes 786440 | tf_op jit(solution)/shard_map/ppermute | solution.py:199
  13.3 10.6 %collective-permute-start.6 = (bf16[64,2048]{1,0:T(8,128)(2,1)S(1)}, bf16[64,2048]{1,0:T(8,128)(2,1)S(1)}, u32[]{:S(2)}, u32[]{:S(2)}) collective-permute-start(bf16[64,2048]{1,0:T(8,128)(2,1)S(1)} %collective-permute-done.refs_1_), channel_id=1, source_target_pairs={{0,6},{1,7},{2,0},{3,1},{4,2},{5,3},{6,4},{7,5},{8,14},{9,15},{10,... | collective-permute-start | bytes 786440 | tf_op jit(solution)/shard_map/ppermute | solution.py:199
  13.7 10.3 %collective-permute-start.7 = (bf16[64,2048]{1,0:T(8,128)(2,1)S(1)}, bf16[64,2048]{1,0:T(8,128)(2,1)S(1)}, u32[]{:S(2)}, u32[]{:S(2)}) collective-permute-start(bf16[64,2048]{1,0:T(8,128)(2,1)S(1)} %collective-permute-done.1.refs_2_), channel_id=1, source_target_pairs={{0,1},{1,0},{2,3},{3,2},{4,5},{5,4},{6,7},{7,6},{8,9},{9,8},{10,11... | collective-permute-start | bytes 786440 | tf_op jit(solution)/shard_map/ppermute | solution.py:194
  14.5 10.0 %collective-permute-start.8 = (bf16[64,2048]{1,0:T(8,128)(2,1)S(1)}, bf16[64,2048]{1,0:T(8,128)(2,1)S(1)}, u32[]{:S(2)}, u32[]{:S(2)}) collective-permute-start(bf16[64,2048]{1,0:T(8,128)(2,1)S(1)} %collective-permute-done.refs_1_), channel_id=1, source_target_pairs={{0,2},{1,3},{2,4},{3,5},{4,6},{5,7},{6,0},{7,1},{8,10},{9,11},{10,... | collective-permute-start | bytes 786440 | tf_op jit(solution)/shard_map/ppermute | solution.py:199
  15.9 0.7 copy-start.3
  16.5 1.2 %copy-start.1 = (bf16[256,2048]{1,0:T(8,128)(2,1)S(1)}, bf16[256,2048]{1,0:T(8,128)(2,1)}, u32[]{:S(2)}) copy-start(bf16[256,2048]{1,0:T(8,128)(2,1)} %spectra_ref.1) | copy-start | bytes 3145732
  17.8 0.9 %copy-start.2 = (s32[256,128]{1,0:T(8,128)S(1)}, s32[256,128]{1,0:T(8,128)}, u32[]{:S(2)}) copy-start(s32[256,128]{1,0:T(8,128)} %cand_ref.1) | copy-start | bytes 393220
  25.1 1.4 %collective-permute-start.9 = (bf16[16,8,512]{2,1,0:T(8,128)(2,1)S(1)}, bf16[16,8,512]{2,1,0:T(8,128)(2,1)S(1)}, u32[]{:S(2)}, u32[]{:S(2)}) collective-permute-start(bf16[16,8,512]{2,1,0:T(8,128)(2,1)S(1)} %get-tuple-element.16), channel_id=1, source_target_pairs={{0,8},{8,0},{16,24},{24,16},{32,40},{40,32},{48,56},{56,48},{64,72... | collective-permute-start | bytes 393224 | tf_op jit(solution)/shard_map/ppermute | solution.py:234
